TPU v7x, 128 devices: a whole 4x4x4 slice. The times are simulated.
128 devices in a mesh: rep: 32 (over x, z_hi, y), shard: 4 (over z_lo, core).
Axes of the slice: x: 4, y: 4, z: 4 (z_hi: 2, z_lo: 2; z = z_hi * 2 + z_lo), core: 2. Of those that a mesh axis runs over, the one named last changes fastest.
Arguments:
- inputs: bfloat16 [16384, 1024], P(('rep', 'shard')), may hold values from -10 to 10
- lengths: int32 [32], P('rep'), may hold values from 385 to 512, as said below
- gains: bfloat16 [2, 1024], P(None, 'shard'), may hold values from 0.5 to 1.5
- shifts: bfloat16 [2, 1024], P(None, 'shard'), may hold values from -4 to 4
- triple: bfloat16 [2, 1024, 3072], P(None, 'shard'), may hold values from -0.1875 to 0.1875
- triple_bias: bfloat16 [2, 3072], P(None, 'shard'), may hold values from -4 to 4
- merger: bfloat16 [2, 1024, 1024], P(None, 'shard'), may hold values from -1.5 to 1.5
- merger_bias: bfloat16 [2, 1024], P(None, 'shard'), may hold values from -4 to 4
- expander: bfloat16 [2, 1024, 4096], P(None, 'shard'), may hold values from -0.1875 to 0.1875
- expander_bias: bfloat16 [2, 4096], P(None, 'shard'), may hold values from -4 to 4
- shrinker: bfloat16 [2, 4096, 1024], P(None, 'shard'), may hold values from -0.09375 to 0.09375
- shrinker_bias: bfloat16 [2, 1024], P(None, 'shard'), may hold values from -4 to 4
- cotangent: bfloat16 [16384, 1024], P(('rep', 'shard')), may hold values from -6 to 6
Outputs:
- hidden_out: bfloat16 [16384, 1024], P(('rep', 'shard'))
- input_grad: float32 [16384, 1024], P(('rep', 'shard'))
- gains_gradient: float32 [2, 1024], P(None, 'shard')
- shifts_gradient: float32 [2, 1024], P(None, 'shard')
- triple_gradient: float32 [2, 1024, 3072], P(None, 'shard')
- triple_bias_gradient: float32 [2, 3072], P(None, 'shard')
- merger_gradient: float32 [2, 1024, 1024], P(None, 'shard')
- merger_bias_gradient: float32 [2, 1024], P(None, 'shard')
- expander_gradient: float32 [2, 1024, 4096], P(None, 'shard')
- expander_bias_gradient: float32 [2, 4096], P(None, 'shard')
- shrinker_gradient: float32 [2, 4096, 1024], P(None, 'shard')
- shrinker_bias_gradient: float32 [2, 1024], P(None, 'shard')
- rms_stats: float32 [32, 6], P('rep')
Inputs may be any that keep to these rules, and one draw needn't show every extreme that they name: `lengths`: one sequence of every draw has all 512 slots valid.
All inputs are finite; a program needn't handle non-finite values.
Results may differ from a plain program's by a relative error of at most 0.025.
Values may be sent and summed in bfloat16 or wider, within the bound.
No kernel may reach another device: no remote copies, remote signals or barrier semaphores. Data moves between devices by JAX's collectives and lax.ppermute only.
A program may use at most 256 MiB of HBM per device.

v0:
```python
import functools
import math

import jax
import jax.numpy as jnp
from jax import lax
from jax.experimental import pallas as pl
from jax.experimental.pallas import tpu as pltpu
from jax.sharding import PartitionSpec as P

HD = 64
ROT = 32
LAYERS = 2
EPS_NORM = 1e-05
AXES = ("rep", "shard")
BF = jnp.bfloat16
F32 = jnp.float32
MINE = 4
W = 1024
WIDE = 1792
PART = 768
PAIR = 1536
ORDERS = ((0, 2, 1, 3), (2, 0, 1, 3), (1, 3, 2, 0), (3, 1, 2, 0))

VM = pl.BlockSpec(memory_space=pltpu.VMEM)
ANY = pl.BlockSpec(memory_space=pl.ANY)
HBM = pl.BlockSpec(memory_space=pltpu.HBM)
SM = pl.BlockSpec(memory_space=pltpu.SMEM)


def place_of(index):
    rep, shard = divmod(index, 4)
    x, rest = divmod(rep, 8)
    z_hi, y = divmod(rest, 4)
    z_lo, core = divmod(shard, 2)
    return x, y, z_hi * 2 + z_lo, core


def index_of(x, y, z, core):
    return ((x * 2 + z // 2) * 4 + y) * 4 + (z % 2) * 2 + core


def move(value, flip_x=0, flip_y=0, flip_z=0, flip_core=0):
    pairs = []
    for index in range(128):
        x, y, z, core = place_of(index)
        pairs.append((index, index_of(x ^ flip_x, y ^ flip_y, z ^ flip_z, core ^ flip_core)))
    return lax.ppermute(value, AXES, pairs)


def hop(value, link):
    by = 3 if link & 1 else 1
    return move(value, flip_y=by) if link > 1 else move(value, flip_x=by)


def link_bit(place, link):
    return place[4 + link]


def after(value, *others):
    return lax.optimization_barrier((value,) + others)[0]


def pick(value, index, axis=0):
    return lax.dynamic_index_in_dim(value, index, axis, keepdims=False)


def shape(*dims, dtype=BF):
    return jax.ShapeDtypeStruct(dims, dtype)


def call(body, args, specs, outs, out_specs=None, scratch=(), flops=0, aliases=None, room=4):
    held = sum(math.prod(o.shape) * o.dtype.itemsize for o in outs)
    held += sum(math.prod(a.shape) * a.dtype.itemsize for a, s in zip(args, specs) if s is VM)
    held += sum(math.prod(s.shape) * s.dtype.itemsize for s in scratch if jnp.issubdtype(s.dtype, jnp.floating))
    room = held + (room << 20)
    return pl.pallas_call(
        body,
        out_shape=outs,
        in_specs=specs,
        out_specs=out_specs or [VM] * len(outs),
        scratch_shapes=scratch,
        input_output_aliases=aliases or {},
        compiler_params=pltpu.CompilerParams(vmem_limit_bytes=room),
        cost_estimate=pl.CostEstimate(flops=1, bytes_accessed=1, transcendentals=0),
    )(*args)


def dot(left, right):
    return jnp.dot(left, right, preferred_element_type=F32)


def dot_t(left, right):
    return lax.dot_general(left, right, (((1,), (1,)), ((), ())), preferred_element_type=F32)


def t_dot(left, right):
    return lax.dot_general(left, right, (((0,), (0,)), ((), ())), preferred_element_type=F32)


def copies(pairs, sems):
    started = []
    for at, (source, target) in enumerate(pairs):
        copy = pltpu.make_async_copy(source, target, sems.at[at])
        copy.start()
        started.append(copy)
    return started


def finish(started):
    for copy in started:
        copy.wait()


def lanes(start, size):
    return pl.ds(pl.multiple_of(start, 128), size)


def rows_at(start, size):
    return pl.ds(pl.multiple_of(start, 16), size)


def cut_triple(
    place, gains, shifts, merger_bias, shrinker_bias, triple_bias, triple,
    small, out1, out2, out3, slab, sems,
):
    shard = place[2]
    started = copies([(triple.at[0], slab)], sems)
    narrow = [v[...].astype(F32) for v in (gains, shifts, merger_bias, shrinker_bias)]
    narrow = jnp.concatenate(narrow + [jnp.zeros((8, 256), F32)], axis=0)
    tall = jnp.concatenate(
        [jnp.zeros((8, 768), F32), triple_bias[...].astype(F32), jnp.zeros((6, 768), F32)], axis=0
    )
    both = jnp.concatenate([narrow, jnp.zeros((16, 512), F32)], axis=1) + tall
    small[...] = both.astype(BF)
    for ref in (out1, out2, out3):
        ref[pl.ds(256, 16), :] = both.astype(BF)
    finish(started)
    for k, ref in ((2, out2), (3, out3), (1, out1)):
        for p in range(3):
            ref[pl.ds(0, 256), pl.ds(p * 256, 256)] = slab[:, lanes(p * W + (shard ^ k) * 256, 256)]


def cut_rest(
    place, cotangent, triple, expander, e1, e2, e3, w1, wz, slab, first, second, sems
):
    shard = place[2]
    pairs = [(expander.at[0], first), (expander.at[1], second), (triple.at[1], slab)]
    started = copies(pairs, sems)
    e2[pl.ds(256, 128), :] = cotangent[...]
    started[0].wait()
    for k, ref in ((2, e2), (3, e3), (1, e1)):
        ref[pl.ds(0, 256), :] = first[:, lanes((shard ^ k) * W, W)]
    finish(started[1:])
    for k, ref in ((2, wz.at[pl.ds(0, 256)]), (3, wz.at[pl.ds(256, 256)]), (1, w1)):
        block = shard ^ k
        ref[:, pl.ds(0, W)] = second[:, lanes(block * W, W)]
        for p in range(3):
            ref[:, pl.ds(W + p * 256, 256)] = slab[:, lanes(p * W + block * 256, 256)]


def own_triple(shard, layer, triple, wide):
    return [
        (
            triple.at[layer, :, lanes(p * W + shard * 256, 256)],
            wide.at[rows_at(shard * 256, 256), pl.ds(W + p * 256, 256)],
        )
        for p in range(3)
    ]


def own_expander(shard, layer, expander, wide):
    return [
        (expander.at[layer, :, lanes(shard * W, W)], wide.at[rows_at(shard * 256, 256), pl.ds(0, W)])
    ]


def piece_rows(shard, k, wide):
    return wide.at[rows_at((shard ^ k) * 256, 256)]


def first_triple(shard, pieces, wide):
    return [
        (ref.at[pl.ds(0, 256)], piece_rows(shard, k, wide).at[:, pl.ds(W, 768)])
        for k, ref in zip((1, 2, 3), pieces)
    ]


def first_expander(shard, pieces, wide):
    return [
        (ref.at[pl.ds(0, 256)], piece_rows(shard, k, wide).at[:, pl.ds(0, W)])
        for k, ref in zip((1, 2, 3), pieces)
    ]


def second_wide(shard, pieces, wide):
    one, two, three = pieces
    return [
        (one, piece_rows(shard, 1, wide)),
        (two.at[pl.ds(0, 256)], piece_rows(shard, 2, wide)),
        (three, piece_rows(shard, 3, wide)),
    ]


def spots(shard):
    row = lax.broadcasted_iota(jnp.int32, (512, 1), 0)
    col = lax.broadcasted_iota(jnp.int32, (1, 512), 1)

    def at(i):
        return (((i >> 7) ^ shard) << 7) | (i & 127)

    return at(row), at(col)


def rotate(values, turn, back=False):
    ahead = pltpu.roll(values, 256 - 16, 1) * turn[1]
    behind = pltpu.roll(values, 16, 1) * turn[2]
    if back:
        return values * turn[0] - ahead - behind
    return values * turn[0] + ahead + behind


def normalize(state):
    mean = jnp.mean(state, axis=-1, keepdims=True)
    centred = state - mean
    spread = jnp.mean(centred * centred, axis=-1, keepdims=True)
    factor = lax.rsqrt(spread + EPS_NORM)
    return centred * factor, factor


ROOT = math.sqrt(2.0 / math.pi)


def gelu_both(v):
    square = v * v
    t = jnp.tanh(ROOT * v * (1.0 + 0.044715 * square))
    half = 0.5 * (1.0 + t)
    slope = half + 0.5 * v * (1.0 - t * t) * (ROOT + (3.0 * 0.044715 * ROOT) * square)
    return v * half, slope


def heads_out(normed, wide, bias, turn, qkv):
    scale = HD ** (-0.5)
    for p in range(3):
        part = dot(normed[...], wide[:, pl.ds(W + p * 256, 256)]) + bias[:, pl.ds(p * 256, 256)]
        if p < 2:
            part = rotate(part, turn)
        if p == 0:
            part = part * scale
        qkv[:, pl.ds(p * 256, 256)] = part.astype(BF)


def probabilities(qkv, h, allowed):
    q = qkv[:, pl.ds(h * HD, HD)]
    k = qkv[:, pl.ds(256 + h * HD, HD)]
    scores = jnp.where(allowed, dot_t(q, k), -1000000000.0)
    powered = jnp.exp(scores - jnp.max(scores, axis=-1, keepdims=True))
    return powered * (1.0 / jnp.sum(powered, axis=-1, keepdims=True))


def attend(qkv, allowed, mixed):
    for h in range(MINE):
        low = probabilities(qkv, h, allowed).astype(BF)
        mixed[:, pl.ds(h * HD, HD)] = dot(low, qkv[:, pl.ds(512 + h * HD, HD)]).astype(BF)


def attend_back(qkv, allowed, mixed, slope_mixed, slopes, forward):
    for h in range(MINE):
        probs = probabilities(qkv, h, allowed)
        low = probs.astype(BF)
        q = qkv[:, pl.ds(h * HD, HD)]
        k = qkv[:, pl.ds(256 + h * HD, HD)]
        v = qkv[:, pl.ds(512 + h * HD, HD)]
        if forward:
            mixed[:, pl.ds(h * HD, HD)] = dot(low, v).astype(BF)
        out = slope_mixed[:, pl.ds(h * HD, HD)]
        slope_probs = dot_t(out, v)
        centre = jnp.sum(probs * slope_probs, axis=-1, keepdims=True)
        slope_scores = (probs * (slope_probs - centre)).astype(BF)
        slopes[:, pl.ds(h * HD, HD)] = dot(slope_scores, k)
        slopes[:, pl.ds(256 + h * HD, HD)] = t_dot(slope_scores, q)
        slopes[:, pl.ds(512 + h * HD, HD)] = t_dot(low, out)


def hand_out(left, right, send, keep):
    for n in range(4):
        cols = pl.ds(n * 256, 256)
        part = dot(left[...], right[:, cols])
        spread_out(part, cols, send, keep)


def spread_out(part, cols, send, keep):
    keep[pl.ds(0, 128), cols] = part[0:128]
    send[pl.ds(0, 128), cols] = part[128:256].astype(BF)
    keep[pl.ds(128, 128), cols] = part[256:384]
    send[pl.ds(128, 128), cols] = part[384:512].astype(BF)


def first_attention(
    place, x0, x1, x2, x3, small, bias, turn, triple, merger, t1, t2, t3,
    normed, qkv, mixed, send, keep, vec, wide, merge, smalls, sems,
):
    shard, length = place[2], place[3]
    pairs = [(small, smalls.at[shard])]
    pairs += [(t1.at[pl.ds(256, 16)], smalls.at[shard ^ 1])]
    pairs += [(t2.at[pl.ds(256, 16)], smalls.at[shard ^ 2])]
    pairs += [(t3.at[pl.ds(256, 16)], smalls.at[shard ^ 3])]
    pairs += own_triple(shard, 0, triple, wide) + [(merger.at[0], merge)]
    started = copies(pairs + first_triple(shard, (t1, t2, t3), wide), sems)
    for copy in started[:4]:
        copy.wait()
    vec[...] = jnp.zeros_like(vec)
    for j in range(4):
        vec[pl.ds(0, 8), pl.ds(j * 256, 256)] = smalls[j].astype(F32)[0:8, 0:256]
    for p in range(3):
        block = p * 4 + shard
        j = (block * 11) >> 5
        vec[pl.ds(8, 2), pl.ds(p * 256, 256)] = smalls[j, :, lanes((block - 3 * j) * 256, 256)].astype(
            F32
        )[8:10]
    vec[pl.ds(10, 2), :] = bias[...].astype(F32)
    gain, shift = vec[pl.ds(0, 1), :], vec[pl.ds(2, 1), :]
    for k, ref in enumerate((x0, x1, x2, x3)):
        hat, _ = normalize(ref[...].astype(F32))
        normed[pl.ds(k * 128, 128), :] = (hat * gain + shift).astype(BF)
    finish(started[4:])
    row, col = spots(shard)
    allowed = (col <= row) & (col < length)
    heads_out(normed, wide, vec[pl.ds(8, 1), pl.ds(0, 768)], turn, qkv)
    attend(qkv, allowed, mixed)
    hand_out(mixed, merge, send, keep)


def first_forward(
    place, normed, vec, expander, shrinker, e1, e2, e3,
    before, send, keep, wide, shrink, act, sems,
):
    shard = place[2]
    pairs = own_expander(shard, 0, expander, wide) + first_expander(shard, (e1, e2, e3), wide)
    started = copies(pairs + [(shrinker.at[0], shrink)], sems)
    finish(started)
    for n in range(4):
        cols = pl.ds(n * 256, 256)
        part = dot(normed[...], wide[:, cols]) + vec[pl.ds(10, 1), cols]
        before[:, cols] = part
        act[:, cols] = gelu_both(part)[0].astype(BF)
    hand_out(act, shrink, send, keep)


def slopes_out(ss, bias, wide, send, keep):
    bias[...] = jnp.broadcast_to(jnp.sum(ss[...].astype(F32), axis=0, keepdims=True), bias.shape)
    for n in range(4):
        part = dot_t(ss[...], wide[pl.ds(n * 256, 256), :])
        spread_out(part, pl.ds(n * 256, 256), send, keep)


def triple_slopes(slopes, turn, ss):
    scale = HD ** (-0.5)
    ss[:, pl.ds(W, 256)] = (rotate(slopes[:, pl.ds(0, 256)], turn, True) * scale).astype(BF)
    ss[:, pl.ds(W + 256, 256)] = rotate(slopes[:, pl.ds(256, 256)], turn, True).astype(BF)
    ss[:, pl.ds(W + 512, 256)] = slopes[:, pl.ds(512, 256)].astype(BF)


def last_layer(
    place, n0, n1, n2, n3, u0, u1, u2, u3, vec, turn, triple, merger, expander, shrinker, w1, w2, w3,
    normed, up, act, ss, mixed, bsend, bkeep, send, keep, bias,
    wide, merge, shrink, qkv, slopes, out, before, sems,
):
    shard, length = place[2], place[3]
    pairs = own_triple(shard, 1, triple, wide) + own_expander(shard, 1, expander, wide)
    pairs += second_wide(shard, (w1, w2, w3), wide) + [(merger.at[1], merge), (shrinker.at[1], shrink)]
    started = copies(pairs, sems)
    row, col = spots(shard)
    for k, (n, u) in enumerate(((n0, u0), (n1, u1), (n2, u2), (n3, u3))):
        rows = pl.ds(k * 128, 128)
        normed[rows, :] = n[...]
        up[rows, :] = jnp.where(row[k * 128 : k * 128 + 128] < length, u[...].astype(F32), 0.0).astype(BF)
    finish(started)
    for n in range(4):
        cols = pl.ds(n * 256, 256)
        part = dot(normed[...], wide[:, cols]) + vec[pl.ds(11, 1), cols]
        value, slope = gelu_both(part)
        act[:, cols] = value.astype(BF)
        ss[:, cols] = (dot_t(up[...], shrink[cols, :]) * slope).astype(BF)
    hand_out(act, shrink, bsend.at[pl.ds(256, 256)], bkeep.at[pl.ds(256, 256)])
    allowed = (col <= row) & (col < length)
    heads_out(normed, wide, vec[pl.ds(9, 1), pl.ds(0, 768)], turn, qkv)
    out[...] = dot_t(up[...], merge[...]).astype(BF)
    attend_back(qkv, allowed, mixed, out, slopes, True)
    hand_out(mixed, merge, bsend.at[pl.ds(0, 256)], bkeep.at[pl.ds(0, 256)])
    triple_slopes(slopes, turn, ss)
    slopes_out(ss, bias, wide, send, keep)


def first_back(
    place, u0, u1, u2, u3, before, qkv, turn, triple, merger, expander, shrinker,
    t1, t2, t3, e1, e2, e3,
    up, act, ss, send, keep, bias, wide, merge, shrink, slopes, out, sems,
):
    shard, length = place[2], place[3]
    pairs = own_triple(shard, 0, triple, wide) + own_expander(shard, 0, expander, wide)
    pairs += first_triple(shard, (t1, t2, t3), wide)
    pairs += first_expander(shard, (e1, e2, e3), wide)
    started = copies(pairs + [(merger.at[0], merge), (shrinker.at[0], shrink)], sems)
    for k, u in enumerate((u0, u1, u2, u3)):
        up[pl.ds(k * 128, 128), :] = u[...]
    finish(started)
    for n in range(4):
        cols = pl.ds(n * 256, 256)
        value, slope = gelu_both(before[:, cols])
        act[:, cols] = value.astype(BF)
        ss[:, cols] = (dot_t(up[...], shrink[cols, :]) * slope).astype(BF)
    row, col = spots(shard)
    allowed = (col <= row) & (col < length)
    out[...] = dot_t(up[...], merge[...]).astype(BF)
    attend_back(qkv, allowed, None, out, slopes, False)
    triple_slopes(slopes, turn, ss)
    slopes_out(ss, bias, wide, send, keep)


def halve(term, cols, o, bit, send, keep, at):
    for ref, half in ((keep, bit), (send, 1 - bit)):
        value = term[pl.ds(pl.multiple_of(half * 128, 128), 128), cols].astype(BF)
        for k in range(8):
            ref[pl.ds(k * 64 + o * 16, 16), at] = value[k * 16 : k * 16 + 16]


def terms_one(place, act, up, normed, ss, s0, k0, s2, k2, term):
    whole = pl.ds(0, PART)
    for o in range(4):
        cols = pl.ds(o * 256, 256)
        term[...] = t_dot(act[:, cols], up[:, pl.ds(0, PART)])
        halve(term, whole, o, link_bit(place, ORDERS[0][0]), s0, k0, whole)
        term[...] = t_dot(normed[:, cols], ss[:, pl.ds(0, PART)])
        halve(term, whole, o, link_bit(place, ORDERS[2][0]), s2, k2, whole)


def terms_two(place, act, up, normed, ss, mixed, s1, k1, s3, k3, term, last):
    one, three = link_bit(place, ORDERS[1][0]), link_bit(place, ORDERS[3][0])
    whole = pl.ds(0, PART)
    last[...] = t_dot(mixed[...], up[...])
    for o in range(4):
        cols = pl.ds(o * 256, 256)
        term[:, pl.ds(0, 256)] = t_dot(act[:, cols], up[:, pl.ds(PART, 256)])
        term[:, pl.ds(256, 256)] = last[:, cols]
        both = t_dot(normed[:, cols], ss[:, pl.ds(PART, W)])
        term[:, pl.ds(512, 256)] = both[:, 256:512]
        halve(term, whole, o, one, s1, k1, whole)
        term[:, pl.ds(0, 256)] = both[:, 0:256]
        term[:, pl.ds(256, 512)] = both[:, 512:W]
        halve(term, whole, o, three, s3, k3, whole)


def weight_one(place, act, up, normed, ss):
    return call(
        terms_one, [place, act, up, normed, ss], [SM] + [VM] * 4, [shape(512, PART)] * 4,
        scratch=[pltpu.VMEM((256, PART), F32)], flops=2 * 10**9,
    )


def weight_two(place, act, up, normed, ss, mixed):
    return call(
        terms_two, [place, act, up, normed, ss, mixed], [SM] + [VM] * 5, [shape(512, PART)] * 4,
        scratch=[pltpu.VMEM((256, PART), F32), pltpu.VMEM((256, W), F32)], flops=2 * 10**9,
    )


def join(place, state, *refs, layer):
    shard, length = place[2], place[3]
    spot = shard * 128 + lax.broadcasted_iota(jnp.int32, (128, 1), 0)
    valid = (spot < length).astype(F32)
    if layer == 0:
        ak, ag, az, fk, fg, fz, vec, new, out, squares = refs
        attended = ak[pl.ds(0, 128), :] + ag[pl.ds(0, 128), :].astype(F32) + az[...].astype(F32)
        branch = fk[pl.ds(0, 128), :] + fg[pl.ds(0, 128), :].astype(F32) + fz[...].astype(F32)
    else:
        kept, got, far, vec, out, squares = refs
        attended, branch = [
            kept[pl.ds(at * 256, 128), :]
            + got[pl.ds(at * 256, 128), :].astype(F32)
            + far[pl.ds(at * 128, 128), :].astype(F32)
            for at in (0, 1)
        ]
    attended = attended + vec[pl.ds(4 + layer, 1), :]
    branch = branch + vec[pl.ds(6 + layer, 1), :]
    old = state[...].astype(F32)
    for at, item in enumerate((old, attended, branch)):
        total = jnp.sum(jnp.sum(item * item, axis=1, keepdims=True) * valid)
        squares[pl.ds(at, 1), :] = jnp.full((1, 128), total, F32)
    state_new = old + attended + branch
    if layer == 0:
        new[...] = state_new
        hat, _ = normalize(state_new)
        out[...] = (hat * vec[pl.ds(1, 1), :] + vec[pl.ds(3, 1), :]).astype(BF)
    else:
        out[...] = (state_new * valid).astype(BF)


def norm_back(place, state, slope, up, sk, sg, sz, vec, new, low, rows, *, layer):
    shard, length = place[2], place[3]
    spot = shard * 128 + lax.broadcasted_iota(jnp.int32, (128, 1), 0)
    given = slope[...].astype(F32)
    upstream = up[...].astype(F32)
    if layer == LAYERS - 1:
        given = jnp.where(spot < length, given, 0.0)
        upstream = given
    sn = sk[pl.ds(0, 128), :] + sg[pl.ds(0, 128), :].astype(F32) + sz[...].astype(F32)
    hat, factor = normalize(state[...].astype(F32))
    rows[...] = jnp.zeros_like(rows)
    rows[pl.ds(0, 1), :] = jnp.sum(sn * hat, axis=0, keepdims=True)
    rows[pl.ds(1, 1), :] = jnp.sum(sn, axis=0, keepdims=True)
    rows[pl.ds(2, 1), :] = jnp.sum(upstream, axis=0, keepdims=True)
    d = sn * vec[pl.ds(layer, 1), :]
    mean = jnp.mean(d, axis=-1, keepdims=True)
    along = jnp.mean(d * hat, axis=-1, keepdims=True)
    result = given + factor * (d - mean - hat * along)
    new[...] = result
    low[...] = result.astype(BF)


def vectors_out(place, rows0, bias0, rows1, bias1, out, full):
    shard = place[2]
    full[...] = jnp.zeros_like(full)
    for at, (rows, bias) in enumerate(((rows0, bias0), (rows1, bias1))):
        base = at * 7
        full[pl.ds(base, 3), :] = rows[pl.ds(0, 3), :]
        for p in range(3):
            full[pl.ds(base + 3 + p, 1), lanes(shard * 256, 256)] = bias[
                pl.ds(0, 1), pl.ds(W + p * 256, 256)
            ]
        full[pl.ds(base + 6, 1), :] = bias[pl.ds(0, 1), pl.ds(0, W)]
    out[pl.ds(0, 16), :] = full[:, pl.ds(0, 512)]
    out[pl.ds(16, 16), :] = full[:, pl.ds(512, 512)]


def add_half(kept, got, bit, refs, at):
    size = kept.shape[0] // 2
    for ref, half in zip(refs, (1 - bit, bit)):
        rows = rows_at(half * size, size)
        total = kept[rows, :].astype(F32) + got[rows, :].astype(F32)
        ref[:, at] = total.astype(BF)


def fold_one(place, ka, ga, kb, gb, sa, ha, sb, hb, *, parts):
    for part, (k, g, s, h) in zip(parts, ((ka, ga, sa, ha), (kb, gb, sb, hb))):
        add_half(k, g, link_bit(place, ORDERS[part][1]), (s, h), slice(None))


def fold_two(place, k0, g0, k1, g1, k2, g2, k3, g3, sa, ha, sb, hb):
    for part, (k, g) in enumerate(((k0, g0), (k1, g1), (k2, g2), (k3, g3))):
        refs = (sb, hb) if part > 1 else (sa, ha)
        at = pl.ds((part & 1) * PART, PART)
        add_half(k, g, link_bit(place, ORDERS[part][2]), refs, at)


def fold_three(place, ka, ga, kb, gb, sa, ha, sb, hb):
    for part, (k, g, s, h) in zip((0, 2), ((ka, ga, sa, ha), (kb, gb, sb, hb))):
        add_half(k, g, link_bit(place, ORDERS[part][3]), (s, h), slice(None))


def first_folds(place, kept, got, parts):
    args = [kept[0], got[0], kept[1], got[1]]
    return call(
        functools.partial(fold_one, parts=parts), [place] + args, [SM] + [VM] * 4, [shape(256, PART)] * 4
    )


def z_send(place, *refs):
    ka, ga, kb, gb, *refs = refs
    shard = place[2]
    z_lo = shard >> 1
    if len(refs) == 6:
        vector, *refs = refs
    else:
        vector = None
    side, across, cross, plain, wide = refs
    a = ka[...].astype(F32) + ga[...].astype(F32)
    b = kb[...].astype(F32) + gb[...].astype(F32)
    wide[:, pl.ds(0, W)] = b[:, 0:W]
    wide[:, pl.ds(W, 256)] = a[:, 1280:PAIR]
    wide[:, pl.ds(1280, 512)] = b[:, W:PAIR]
    plain[...] = a[:, 0:1280]
    cross[...] = wide[rows_at(z_lo * 32, 32), :]
    side[:, pl.ds(0, WIDE)] = wide[rows_at((1 - z_lo) * 32, 32), :].astype(BF)
    across[:, pl.ds(0, WIDE)] = cross[...].astype(BF)
    across[:, pl.ds(WIDE, 1280)] = plain[pl.ds(0, 32), :].astype(BF)
    across[:, pl.ds(WIDE + 1280, 1280)] = plain[pl.ds(32, 32), :].astype(BF)
    if vector is not None:
        side[:, pl.ds(WIDE, 512)] = vector[...].astype(BF)
        across[:, pl.ds(WIDE + 2560, 512)] = vector[...].astype(BF)


def local_rows():
    row = lax.broadcasted_iota(jnp.int32, (32, 1), 0) & 15
    return (row == 6) | (row == 13)


def z_sum(place, *refs):
    cross, plain, za, zb, z2, *refs = refs
    vector = None
    if len(refs) == 6:
        vector, *refs = refs
        near, kept, whole, vec, both = refs
    else:
        near, kept, whole, both = refs
    core = place[2] & 1
    both[pl.ds(0, 32), :] = cross[...] + z2[:, pl.ds(0, WIDE)].astype(F32)
    both[pl.ds(32, 32), :] = za[:, pl.ds(0, WIDE)].astype(F32) + zb[:, pl.ds(0, WIDE)].astype(F32)
    for at in range(2):
        own = both[rows_at(at * 32 + core * 16, 16), :]
        other = both[rows_at(at * 32 + (1 - core) * 16, 16), :]
        kept[pl.ds(at * 16, 16), :] = own.astype(BF)
        near[pl.ds(at * 16, 16), pl.ds(0, WIDE)] = other.astype(BF)
    for at in range(2):
        rows = pl.ds(at * 32, 32)
        got = z2[:, pl.ds(WIDE + at * 1280, 1280)].astype(F32)
        whole[rows, :] = (plain[rows, :] + got).astype(BF)
    if vector is not None:
        sides = za[:, pl.ds(WIDE, 512)].astype(F32) + zb[:, pl.ds(WIDE, 512)].astype(F32)
        total = vector[...] + z2[:, pl.ds(WIDE + 2560, 512)].astype(F32)
        total = total + jnp.where(local_rows(), 0.0, sides)
        vec[...] = total
        near[:, pl.ds(WIDE, 512)] = total.astype(BF)


def payload_parts(place, kept, near, whole, a, b):
    shard = place[2]
    for k in range(4):
        rows = rows_at((shard ^ k) * 16, 16)
        ref, at = (near, k >> 1) if k & 1 else (kept, k >> 1)
        source = ref[pl.ds(at * 16, 16), pl.ds(0, WIDE)]
        b[rows, pl.ds(0, W)] = source[:, 0:W]
        a[rows, pl.ds(1280, 256)] = source[:, W:1280]
        b[rows, pl.ds(W, 512)] = source[:, 1280:WIDE]
    a[pl.ds(0, 64), pl.ds(0, 1280)] = whole[...]


def payload_both(place, kept, near, whole, out):
    payload_parts(place, kept, near, whole, out.at[pl.ds(0, 64)], out.at[pl.ds(64, 64)])


def payload(place, kept, near, whole, *refs):
    *vec, a, b = refs
    payload_parts(place, kept, near, whole, a, b)
    if not vec:
        return
    vec = vec[0]
    total = vec[...] + jnp.where(local_rows(), 0.0, near[:, pl.ds(WIDE, 512)].astype(F32))
    low = total.astype(BF)
    a[pl.ds(64, 16), :] = jnp.zeros((16, PAIR), BF)
    a[pl.ds(64, 16), pl.ds(0, 512)] = low[0:16]
    a[pl.ds(64, 16), pl.ds(512, 512)] = low[16:32]


def line_up(own, got, bit, size, outs, cols):
    for ref, at in zip(outs, cols):
        ref[rows_at(bit * size, size), :] = own[pl.ds(0, size), at]
        ref[rows_at((1 - bit) * size, size), :] = got[pl.ds(0, size), at]


def vector_rows(own, got, at, size):
    rows = pl.ds(at, size)
    return (own[rows, :].astype(F32) + got[rows, :].astype(F32)).astype(BF)


def gather_four(place, oa, ga, ob, gb, a, b):
    line_up(oa, ga, link_bit(place, ORDERS[0][3]), 64, [a], [slice(None)])
    line_up(ob, gb, link_bit(place, ORDERS[2][3]), 64, [b], [slice(None)])
    if a.shape[0] > 128:
        a[pl.ds(128, 16), :] = vector_rows(oa, ga, 64, 16)


def gather_three(place, oa, ga, ob, gb, p0, p1, p2, p3):
    cols = [pl.ds(0, PART), pl.ds(PART, PART)]
    line_up(oa, ga, link_bit(place, ORDERS[0][2]), 128, [p0, p1], cols)
    line_up(ob, gb, link_bit(place, ORDERS[2][2]), 128, [p2, p3], cols)
    if p0.shape[0] == 256:
        return
    low = vector_rows(oa, ga, 128, 16)
    p0[pl.ds(256, 32), :] = jnp.zeros((32, PART), BF)
    p0[pl.ds(256, 16), pl.ds(0, 512)] = low[:, 0:512]
    p0[pl.ds(272, 16), pl.ds(0, 512)] = low[:, 512:W]


def gather_two(place, o0, g0, o1, g1, o2, g2, o3, g3, p0, p1, p2, p3):
    outs = (p0, p1, p2, p3)
    for part, (o, g) in enumerate(((o0, g0), (o1, g1), (o2, g2), (o3, g3))):
        line_up(o, g, link_bit(place, ORDERS[part][1]), 256, [outs[part]], [slice(None)])
    p0[pl.ds(512, 32), :] = vector_rows(o0, g0, 256, 32)


def each(count, step):
    lax.fori_loop(0, count, lambda at, none: step(at) or none, 0)


def put(part, value, o, base, t, m, e, s):
    rows = rows_at(base, 16)
    if part == 0:
        s[rows_at(o * 256 + base, 16), pl.ds(0, PART)] = value
    elif part == 1:
        s[rows_at(o * 256 + base, 16), pl.ds(PART, 256)] = value[:, 0:256]
        m[rows, pl.ds(o * 256, 256)] = value[:, 256:512]
        t[rows, pl.ds(o * 256, 256)] = value[:, 512:PART]
    elif part == 2:
        e[rows, pl.ds(o * W, PART)] = value
    else:
        e[rows, pl.ds(o * W + PART, 256)] = value[:, 0:256]
        t[rows, pl.ds(W + o * 256, 256)] = value[:, 256:512]
        t[rows, pl.ds(2 * W + o * 256, 256)] = value[:, 512:PART]


def assemble_last(every, t_out, m_out, e_out, s_out, t, m, e, s, sems):
    def device(at):
        x, y = at >> 2, at & 3
        bits = ((x & 1) ^ (x >> 1), x >> 1, (y & 1) ^ (y >> 1), y >> 1)
        for part in range(4):
            unit = sum(bits[link] << (3 - n) for n, link in enumerate(ORDERS[part]))
            for o in range(4):
                rows = rows_at(at * 128 + (part >> 1) * 64 + o * 16, 16)
                value = every[rows, pl.ds((part & 1) * PART, PART)].astype(F32)
                put(part, value, o, unit * 16, t, m, e, s)

    each(16, device)
    pairs = [(t, t_out.at[1]), (m, m_out.at[1]), (e, e_out.at[1]), (s, s_out.at[1])]
    finish(copies(pairs, sems))


def put_half(place, p0, p1, p2, p3, *refs, mine):
    if not mine:
        old, *refs = refs
        t_out, m_out, e_out, s_out, *sums, s0, s1, m1, t1, e2, e3, t3, both, vec, sems = refs[4:]
    else:
        t_out, m_out, e_out, s_out, s0, s1, m1, t1, e2, e3, t3, sems = refs[4:]
    pairs = []
    for part, ref in enumerate((p0, p1, p2, p3)):
        half = link_bit(place, ORDERS[part][0])
        base = (half if mine else 1 - half) * 128
        rows = rows_at(base, 128)
        for o in range(4):
            for k in range(8):
                value = ref[pl.ds(k * 64 + o * 16, 16), :].astype(F32)
                at = pl.ds(k * 16, 16)
                if part == 0:
                    s0[o, at, :] = value
                elif part == 1:
                    s1[o, at, :] = value[:, 0:256]
                    m1[at, pl.ds(o * 256, 256)] = value[:, 256:512]
                    t1[at, pl.ds(o * 256, 256)] = value[:, 512:PART]
                elif part == 2:
                    e2[o, at, :] = value
                else:
                    e3[o, at, :] = value[:, 0:256]
                    t3[at, pl.ds(o * 256, 256)] = value[:, 256:512]
                    t3[at, pl.ds(W + o * 256, 256)] = value[:, 512:PART]
            if part < 2:
                target = s_out.at[0, rows_at(o * 256 + base, 128)]
                pairs.append((s0.at[o], target.at[:, pl.ds(0, PART)]) if part == 0 else (s1.at[o], target.at[:, pl.ds(PART, 256)]))
            else:
                target = e_out.at[0, rows]
                pairs.append((e2.at[o], target.at[:, pl.ds(o * W, PART)]) if part == 2 else (e3.at[o], target.at[:, pl.ds(o * W + PART, 256)]))
        if part == 1:
            pairs.append((m1, m_out.at[0, rows]))
            pairs.append((t1, t_out.at[0, rows, pl.ds(0, W)]))
        if part == 3:
            pairs.append((t3, t_out.at[0, rows, pl.ds(W, 2 * W)]))
    started = copies(pairs, sems)
    if not mine:
        fetch = copies([(old.at[pl.ds(512, 32)], both)], sems.at[pl.ds(len(pairs), 1)])
        finish(fetch)
        low = both[...].astype(F32) + p0[pl.ds(512, 32), :].astype(F32)
        vec[:, pl.ds(0, 512)] = low[0:16, 0:512]
        vec[:, pl.ds(512, 512)] = low[16:32, 0:512]
        for at in range(LAYERS):
            own_sums(vec, at, place[2], *sums)
    finish(started)


def own_sums(vec, layer, shard, g_sum, s_sum, b_sum, b_copy, t_sum, e_sum):
    base = layer * 7
    row = pl.ds(layer, 1)
    for at, ref in ((0, g_sum), (1, s_sum), (2, b_sum), (2, b_copy)):
        ref[row, :] = vec[pl.ds(base + at, 1), lanes(shard * 256, 256)]
    for r in range(3):
        block = shard * 3 + r
        t_sum[row, pl.ds(r * 256, 256)] = vec[
            pl.ds(base + 3 + (block >> 2), 1), lanes((block & 3) * 256, 256)
        ]
    e_sum[row, :] = vec[pl.ds(base + 6, 1), :]


def hops(values, parts, phase):
    return [hop(value, ORDERS[part][phase]) for value, part in zip(values, parts)]


def fold_middle(place, one, two):
    kept = [one[0], two[0], one[1], two[1]]
    got = [one[2], two[2], one[3], two[3]]
    args = [v for pair in zip(kept, got) for v in pair]
    sa, ka, sb, kb = call(fold_two, [place] + args, [SM] + [VM] * 8, [shape(128, PAIR)] * 4)
    ga, gb = hops([sa, sb], (0, 2), 2)
    return [ka, ga, kb, gb]


def fold_last(place, units):
    sa, ka, sb, kb = call(fold_three, [place] + units, [SM] + [VM] * 4, [shape(64, PAIR)] * 4)
    ga, gb = hops([sa, sb], (0, 2), 3)
    return [ka, ga, kb, gb]


def send_z(place, units, vector):
    more = 512 * len(vector)
    side, across, cross, plain = call(
        z_send, [place] + units + vector, [SM] + [VM] * (4 + len(vector)),
        [
            shape(32, WIDE + more), shape(32, WIDE + 2560 + more),
            shape(32, WIDE, dtype=F32), shape(64, 1280, dtype=F32),
        ],
        scratch=[pltpu.VMEM((64, WIDE), F32)],
    )
    z2 = move(across, flip_z=2)
    za = move(side, flip_z=1)
    zb = move(side, flip_z=3)
    return [cross, plain, za, zb, z2] + vector


def sum_z(place, terms):
    vectors = len(terms) - 5
    near, kept, whole, *vec = call(
        z_sum, [place] + terms, [SM] + [VM] * len(terms),
        [shape(32, WIDE + 512 * vectors), shape(32, WIDE), shape(64, 1280)]
        + [shape(32, 512, dtype=F32)] * vectors,
        scratch=[pltpu.VMEM((64, WIDE), F32)],
    )
    return [kept, move(near, flip_core=1), whole] + vec


OUTS = [
    shape(LAYERS, 256, 3072, dtype=F32),
    shape(LAYERS, 256, 1024, dtype=F32),
    shape(LAYERS, 256, 4096, dtype=F32),
    shape(LAYERS, 1024, 1024, dtype=F32),
]


def line_unit(place, pieces):
    rows = 80 if len(pieces) == 4 else 64
    a, b = call(
        payload, [place] + pieces, [SM] + [VM] * len(pieces), [shape(rows, PAIR), shape(64, PAIR)]
    )
    ga, gb = hops([a, b], (0, 2), 3)
    return [a, ga, b, gb]


def line_four(place, args):
    rows = args[0].shape[0] + 64
    a, b = call(gather_four, [place] + args, [SM] + [VM] * 4, [shape(rows, PAIR), shape(128, PAIR)])
    ga, gb = hops([a, b], (0, 2), 2)
    return [a, ga, b, gb]


def line_three(place, args):
    rows = 288 if args[0].shape[0] > 128 else 256
    own = call(
        gather_three, [place] + args, [SM] + [VM] * 4, [shape(rows, PART)] + [shape(256, PART)] * 3
    )
    got = hops(own, range(4), 1)
    return [v for pair in zip(own, got) for v in pair]


def line_two(place, args):
    own = call(
        gather_two, [place] + args, [SM] + [VM] * 8, [shape(544, PART)] + [shape(512, PART)] * 3
    )
    return list(own), hops(own, range(4), 0)


def collect_last(place, pieces):
    (both,) = call(payload_both, [place] + pieces, [SM] + [VM] * 3, [shape(128, PAIR)])
    planes = [[(x * 2 + z) * 4 + y for x in range(4) for y in range(4)] for z in range(2)]
    return lax.all_gather(both, "rep", axis_index_groups=planes, axis=0, tiled=True)


def put_last(every):
    return call(
        assemble_last, [every], [VM], OUTS, out_specs=[ANY] * 4,
        scratch=[pltpu.VMEM(out.shape[1:], F32) for out in OUTS] + [pltpu.SemaphoreType.DMA((4,))],
    )


def put_sums(place, parts, earlier, old):
    outs, specs = list(OUTS), [ANY] * 4
    scratch = [
        pltpu.VMEM((4, 128, PART), F32), pltpu.VMEM((4, 128, 256), F32), pltpu.VMEM((128, W), F32),
        pltpu.VMEM((128, W), F32), pltpu.VMEM((4, 128, PART), F32), pltpu.VMEM((4, 128, 256), F32),
        pltpu.VMEM((128, 2 * W), F32),
    ]
    if old:
        outs += [shape(LAYERS, n, dtype=F32) for n in (256, 256, 256, 256, 768, 1024)]
        specs += [VM] * 6
        scratch += [pltpu.VMEM((32, PART), BF), pltpu.VMEM((16, W), F32)]
    return call(
        functools.partial(put_half, mine=not old), [place] + parts + old + list(earlier),
        [SM] + [VM] * 4 + [ANY] * (4 + len(old)), outs, out_specs=specs,
        scratch=scratch + [pltpu.SemaphoreType.DMA((20,))],
        aliases={5 + len(old) + i: i for i in range(4)},
    )


def gather_tokens(own):
    far = move(own, flip_z=1)
    near = move(own, flip_core=1)
    return [own, near, far, move(far, flip_core=1)]


def gather_late(own):
    far = move(own, flip_z=1)
    return [own, move(after(own, far), flip_core=1), far, move(far, flip_core=1)]


def body(
    inputs,
    lengths,
    gains,
    shifts,
    triple,
    triple_bias,
    merger,
    merger_bias,
    expander,
    expander_bias,
    shrinker,
    shrinker_bias,
    cotangent,
):
    rep = lax.axis_index("rep")
    shard = lax.axis_index("shard")
    length = lengths[0]
    x, y = rep // 8, rep % 4
    place = [x, y, shard, length, (x & 1) ^ (x >> 1), x >> 1, (y & 1) ^ (y >> 1), y >> 1]
    place = jnp.stack(place).astype(jnp.int32)

    small, *pieces = call(
        cut_triple,
        [place, gains, shifts, merger_bias, shrinker_bias, triple_bias, triple],
        [SM] + [VM] * 5 + [HBM],
        [shape(16, 768)] + [shape(272, 768)] * 3,
        scratch=[pltpu.VMEM((256, 3072), BF), pltpu.SemaphoreType.DMA((1,))],
    )

    def recut(one, two, three):
        return [
            move(one, flip_core=1),
            move(two, flip_z=1),
            move(three, flip_z=3, flip_core=1),
        ]

    t_pieces = recut(*pieces)
    x_blocks = gather_tokens(after(inputs, small))
    cut = call(
        cut_rest, [after(place, pieces[0], x_blocks[1]), cotangent, triple, expander],
        [SM, VM, HBM, HBM],
        [shape(256, W), shape(384, W), shape(256, W)]
        + [shape(256, WIDE), shape(512, WIDE)],
        scratch=[
            pltpu.VMEM((256, 3072), BF), pltpu.VMEM((256, 4096), BF), pltpu.VMEM((256, 4096), BF),
            pltpu.SemaphoreType.DMA((3,)),
        ],
    )
    e_pieces = recut(*after(tuple(cut[:2]), x_blocks[2]), after(cut[2], t_pieces[2]))

    spot = after(jnp.arange(512, dtype=jnp.int32), x_blocks[1])
    spot = (((spot >> 7) ^ shard) << 7) | (spot & 127)
    index = jnp.arange(ROT // 2, dtype=F32)
    freq = jnp.exp(index * (-2.0 * math.log(10000.0) / ROT))
    lane = jnp.arange(256, dtype=jnp.int32) % HD
    phase = spot.astype(F32)[:, None] * jnp.tile(freq, 16)[None, :]
    cosine, sine = jnp.cos(phase), jnp.sin(phase)
    turn = jnp.stack(
        [
            jnp.where(lane < ROT, cosine, 1.0),
            jnp.where(lane < ROT // 2, -sine, 0.0),
            jnp.where((lane >= ROT // 2) & (lane < ROT), sine, 0.0),
        ]
    )

    full = shape(512, W)
    send, keep = shape(256, W), shape(256, W, dtype=F32)
    wide = pltpu.VMEM((W, WIDE), BF)
    merge, shrink = pltpu.VMEM((256, W), BF), pltpu.VMEM((W, W), BF)

    normed0, qkv0, mixed0, a_send, a_keep, vec = call(
        first_attention,
        [place] + x_blocks + [small, expander_bias, turn, triple, merger] + t_pieces,
        [SM] + [VM] * 4 + [ANY, VM, VM, HBM, HBM] + [ANY] * 3,
        [full, shape(512, 768), shape(512, 256), send, keep, shape(16, W, dtype=F32)],
        scratch=[wide, merge, pltpu.VMEM((4, 16, 768), BF), pltpu.SemaphoreType.DMA((11,))],
        room=14,
        flops=2 * 10**9,
    )
    a_got = move(after(a_send, e_pieces[1]), flip_core=1)
    w_near, w_far = after(tuple(cut[3:]), e_pieces[2])
    w_far = move(w_far, flip_z=3)
    before0, f_send, f_keep = call(
        first_forward,
        [place, normed0, vec, expander, shrinker] + e_pieces,
        [SM, VM, VM, HBM, HBM] + [ANY] * 3,
        [shape(512, W, dtype=F32), send, keep],
        scratch=[wide, shrink, pltpu.VMEM((512, W), BF), pltpu.SemaphoreType.DMA((5,))],
        room=14,
        flops=2 * 10**9,
    )
    f_got = move(f_send, flip_core=1)

    def other(kept, got):
        return move((kept[128:] + got[128:].astype(F32)).astype(BF), flip_z=1)

    a_far = other(a_keep, a_got)
    sums = [a_keep, a_got, a_far, f_keep, f_got, other(f_keep, f_got)]
    block = [shape(128, W, dtype=F32), shape(128, W), shape(8, 128, dtype=F32)]
    state1, normed1, squares0 = call(
        functools.partial(join, layer=0), [place, inputs] + sums + [vec], [SM] + [VM] * 8, block
    )
    n_blocks = gather_tokens(normed1)
    w_far = after(w_far, n_blocks[2])
    u_far = after(e_pieces[1][256:], f_got)
    up_blocks = [
        cotangent, move(after(cotangent, f_got), flip_core=1), u_far, move(u_far, flip_core=1)
    ]
    w_pieces = [move(w_near, flip_core=1), w_far, move(w_far[256:], flip_core=1)]

    normed1, up1, act1, ss1, mixed1, b_send, b_keep, send1, keep1, bias1 = call(
        last_layer,
        [place] + n_blocks + up_blocks + [vec, turn, triple, merger, expander, shrinker] + w_pieces,
        [SM] + [VM] * 10 + [HBM] * 4 + [ANY] * 3,
        [full, full, full, shape(512, WIDE), shape(512, 256), full, shape(512, W, dtype=F32)]
        + [send, keep, shape(8, WIDE, dtype=F32)],
        scratch=[
            wide, merge, shrink, pltpu.VMEM((512, 768), BF), pltpu.VMEM((512, 768), F32),
            pltpu.VMEM((512, 256), BF), pltpu.VMEM((512, W), F32), pltpu.SemaphoreType.DMA((9,)),
        ],
        room=14,
        flops=8 * 10**9,
    )
    got1 = move(send1, flip_core=1)
    s0, k0, s2, k2 = weight_one(place, act1, up1, normed1, ss1)
    low1 = (keep1[128:] + after(got1, s0)[128:].astype(F32)).astype(BF)
    far1 = move(low1, flip_z=1)
    s1, k1, s3, k3 = weight_two(after(place, low1), act1, up1, normed1, ss1, mixed1)
    g0, g2 = hops(after((s0, s2), low1), (0, 2), 0)
    slope1, low1, rows1 = call(
        functools.partial(norm_back, layer=1),
        [after(place, s1), state1, cotangent, cotangent, keep1, got1, far1, vec],
        [SM] + [VM] * 7,
        [shape(128, W, dtype=F32), shape(128, W), shape(8, W, dtype=F32)],
    )
    u_blocks = gather_late(low1)
    g1, g3 = hops(after((s1, s3), low1), (1, 3), 0)
    s0, k0, s2, k2 = first_folds(after(place, low1), (k0, k2), (g0, g2), (0, 2))
    one1 = [k0, k2] + hops([s0, s2], (0, 2), 1)

    up0, act0, ss0, send0, keep0, bias0 = call(
        first_back,
        [place] + u_blocks + [before0, qkv0, turn, triple, merger, expander, shrinker]
        + t_pieces + e_pieces,
        [SM] + [VM] * 7 + [HBM] * 4 + [ANY] * 6,
        [full, full, shape(512, WIDE), send, keep, shape(8, WIDE, dtype=F32)],
        scratch=[
            wide, merge, shrink, pltpu.VMEM((512, 768), F32), pltpu.VMEM((512, 256), BF),
            pltpu.SemaphoreType.DMA((12,)),
        ],
        room=14,
        flops=5 * 10**9,
    )
    got0 = move(send0, flip_core=1)
    s0, k0, s2, k2 = weight_one(place, act0, up0, normed0, ss0)
    f1, h1, f3, h3 = first_folds(after(place, s0), (k1, k3), (g1, g3), (1, 3))
    g0, g2 = hops((s0, s2), (0, 2), 0)
    s1, k1, s3, k3 = weight_two(after(place, f1), act0, up0, normed0, ss0, mixed0)
    two1 = [h1, h3] + hops([f1, f3], (1, 3), 1)
    g1, g3 = hops((s1, s3), (1, 3), 0)
    far0 = other(keep0, got0)
    s0, k0, s2, k2 = first_folds(place, (k0, k2), (g0, g2), (0, 2))
    one0 = [k0, k2] + hops([s0, s2], (0, 2), 1)
    units1 = fold_middle(after(place, s0), one1, two1)
    s1, k1, s3, k3 = first_folds(place, (k1, k3), (g1, g3), (1, 3))
    two0 = [k1, k3] + hops([s1, s3], (1, 3), 1)
    units1 = fold_last(after(place, s1), units1)
    input_grad, _, rows0 = call(
        functools.partial(norm_back, layer=0),
        [place, inputs, slope1, low1, keep0, got0, far0, vec],
        [SM] + [VM] * 7,
        [shape(128, W, dtype=F32), shape(128, W), shape(8, W, dtype=F32)],
    )
    (vector,) = call(
        vectors_out, [place, rows0, bias0, rows1, bias1], [SM] + [VM] * 4,
        [shape(32, 512, dtype=F32)], scratch=[pltpu.VMEM((16, W), F32)],
    )
    units0 = fold_middle(after(place, vector), one0, two0)
    terms1 = send_z(after(place, units0[0]), units1, [])
    units0 = fold_last(place, units0)
    pieces1 = sum_z(after(place, units0[0]), terms1)
    every1 = collect_last(after(place, units0[0]), pieces1)
    terms0 = send_z(place, units0, [vector])
    pieces0 = sum_z(place, terms0)
    line0 = line_unit(place, pieces0)
    b_got = move(after(b_send, pieces1[0]), flip_core=1)
    b_low = (
        b_keep.reshape(2, 256, W)[:, 128:] + b_got.reshape(2, 256, W)[:, 128:].astype(F32)
    ).astype(BF)
    b_far = move(b_low.reshape(256, W), flip_z=1)
    hidden_out, squares1 = call(
        functools.partial(join, layer=1),
        [place, state1, b_keep, b_got, b_far, vec],
        [SM] + [VM] * 5,
        [shape(128, W), shape(8, 128, dtype=F32)],
    )

    line0 = line_four(after(place, hidden_out), line0)
    totals = jnp.concatenate([squares0[:3, :1], squares1[:3, :1]]).reshape(1, 6)
    totals = totals + move(totals, flip_core=1)
    totals = totals + move(totals, flip_z=1)
    rms_stats = jnp.sqrt(totals / (length.astype(F32) * W) + 1e-06)
    line0 = line_three(after(place, rms_stats), line0)
    own0, got0 = line_two(place, line0)
    sums1 = put_last(after(every1, own0[0]))
    sums0 = put_sums(place, own0, sums1, [])
    *sums0, g_sum, s_sum, b_sum, b_copy, t_sum, e_sum = put_sums(place, got0, sums0, [own0[0]])
    return (
        hidden_out,
        input_grad,
        g_sum,
        s_sum,
        sums0[0],
        t_sum,
        sums0[1],
        b_sum,
        sums0[2],
        e_sum,
        sums0[3],
        b_copy,
        rms_stats,
    )


def solution(mesh):
    return jax.shard_map(
        body,
        mesh=mesh,
        in_specs=(
            P(("rep", "shard"), None),
            P("rep"),
            P(None, "shard"),
            P(None, "shard"),
            P(None, "shard", None),
            P(None, "shard"),
            P(None, "shard", None),
            P(None, "shard"),
            P(None, "shard", None),
            P(None, "shard"),
            P(None, "shard", None),
            P(None, "shard"),
            P(("rep", "shard"), None),
        ),
        out_specs=(
            P(("rep", "shard"), None),
            P(("rep", "shard"), None),
            P(None, "shard"),
            P(None, "shard"),
            P(None, "shard", None),
            P(None, "shard"),
            P(None, "shard", None),
            P(None, "shard"),
            P(None, "shard", None),
            P(None, "shard"),
            P(None, "shard", None),
            P(None, "shard"),
            P("rep", None),
        ),
        check_vma=False,
    )
```

profile of v0, /device:TPU:0, one launch (start us, length us, event | category | flops | bytes accessed | tf_op | source)
XLA Modules:
  0.0 340.3 jit_solution(11378536876705184192)
XLA Ops:
  8.0 1.9 copy-done
  13.3 1.7 shard_map.228
  15.0 3.6 %collective-permute-start.5 = (bf16[272,768]{1,0:T(8,128)(2,1)S(1)}, bf16[272,768]{1,0:T(8,128)(2,1)S(1)}, u32[]{:S(2)}, u32[]{:S(2)}) collective-permute-start(bf16[272,768]{1,0:T(8,128)(2,1)S(1)} %get-tuple-element.187), channel_id=1, source_target_pairs={{0,19},{1,18},{2,17},{3,16},{4,23},{5,22},{6,21},{7,20},{8,27},{9,... | collective-permute-start | bytes 1253384 | tf_op jit(solution)/shard_map/ppermute | solution.py:48
  19.3 2.0 collective-permute-start.4
  21.4 2.2 copy-done.3
  24.5 2.4 shard_map.230
  30.6 2.2 collective-permute-start.10
  33.5 12.5 %collective-permute-done.10.e3 = bf16[256,1024]{1,0:T(8,128)(2,1)} collective-permute-done((bf16[256,1024]{1,0:T(8,128)(2,1)}, bf16[256,1024]{1,0:T(8,128)(2,1)}, u32[]{:S(2)}, u32[]{:S(2)}) %collective-permute-start.10) | collective-permute-done | bytes 524320 | tf_op jit(solution)/shard_map/ppermute | solution.py:48
  46.2 2.7 collective-permute-start.19
  48.9 2.0 fusion.4
  51.1 7.7 %shard_map.229 = (bf16[512,1024]{1,0:T(8,128)(2,1)S(1)}, bf16[512,768]{1,0:T(8,128)(2,1)S(1)}, bf16[512,256]{1,0:T(8,128)(2,1)S(1)}, bf16[256,1024]{1,0:T(8,128)...) custom-call(s32[8]{0:T(128)S(1)} %stack.37.place, bf16[128,1024]{1,0:T(8,128)(2,1)S(1)} %copy-done.16, ...), custom_call_target="tpu_custom_call" | custom-call | flops 1 | bytes 1 | tf_op jit(solution)/shard_map/pallas_call | solution.py:77
  58.9 4.6 %shard_map.231 = (f32[512,1024]{1,0:T(8,128)S(1)}, bf16[256,1024]{1,0:T(8,128)(2,1)S(1)}, f32[256,1024]{1,0:T(8,128)S(1)}) custom-call(s32[8]{0:T(128)S(1)} %stack.37.place, bf16[512,1024]{1,0:T(8,128)(2,1)S(1)} %get-tuple-element.195.normed, f32[16,1024]{1,0:T(8,128)S(1)} %get-tuple-element.196.vec.refs_6_.refs_3_, bf16[2,256,4096]{2,1,0:T(8,128)(2,1)S(1)} %copy-done.4, ...), custom_call_target="tpu_custom_call" | custom-call | flops 1 | bytes 1 | tf_op jit(solution)/shard_map/pallas_call | solution.py:77
  67.9 7.0 %collective-permute-done.12.refs_5_ = bf16[128,1024]{1,0:T(8,128)(2,1)S(1)} collective-permute-done((bf16[128,1024]{1,0:T(8,128)(2,1)S(1)}, bf16[128,1024]{1,0:T(8,128)(2,1)S(1)}, u32[]{:S(2)}, u32[]{:S(2)}) %collective-permute-start.12) | collective-permute-done | bytes 262176 | tf_op jit(solution)/shard_map/ppermute | solution.py:48
  74.8 4.8 %collective-permute-done.8.refs_2_ = bf16[128,1024]{1,0:T(8,128)(2,1)S(1)} collective-permute-done((bf16[128,1024]{1,0:T(8,128)(2,1)S(1)}, bf16[128,1024]{1,0:T(8,128)(2,1)S(1)}, u32[]{:S(2)}, u32[]{:S(2)}) %collective-permute-start.8) | collective-permute-done | bytes 262176 | tf_op jit(solution)/shard_map/ppermute | solution.py:48
  81.1 7.2 %collective-permute-done.14.n2 = bf16[128,1024]{1,0:T(8,128)(2,1)S(1)} collective-permute-done((bf16[128,1024]{1,0:T(8,128)(2,1)S(1)}, bf16[128,1024]{1,0:T(8,128)(2,1)S(1)}, u32[]{:S(2)}, u32[]{:S(2)}) %collective-permute-start.14) | collective-permute-done | bytes 262176 | tf_op jit(solution)/shard_map/ppermute | solution.py:48
  88.4 1.7 collective-permute-done.19.w2
  96.1 15.9 %shard_map.233 = (bf16[512,1024]{1,0:T(8,128)(2,1)S(1)}, bf16[512,1024]{1,0:T(8,128)(2,1)S(1)}, bf16[512,1024]{1,0:T(8,128)(2,1)S(1)}, bf16[512,1792]{1,0:T(8,12...) custom-call(s32[8]{0:T(128)S(1)} %stack.37.place, ...), custom_call_target="tpu_custom_call" | custom-call | flops 1 | bytes 1 | tf_op jit(solution)/shard_map/pallas_call | solution.py:77
  112.3 3.6 %shard_map.234 = (bf16[512,768]{1,0:T(8,128)(2,1)}, bf16[512,768]{1,0:T(8,128)(2,1)S(1)}, bf16[512,768]{1,0:T(8,128)(2,1)}, bf16[512,768]{1,0:T(8,128)(2,1)S(1)}) custom-call(s32[8]{0:T(128)S(1)} %stack.37.place, bf16[512,1024]{1,0:T(8,128)(2,1)S(1)} %get-tuple-element.215.act, bf16[512,1024]{1,0:T(8,128)(2,1)S(1)} %get-tuple-element.216.up, ...), custom_call_target="tpu_custom_call" | custom-call | flops 1 | bytes 1 | tf_op jit(solution)/shard_map/pallas_call | solution.py:77
  116.1 2.8 shard_map.235
  118.9 5.6 %collective-permute-done.22.sz = bf16[128,1024]{1,0:T(8,128)(2,1)S(1)} collective-permute-done((bf16[128,1024]{1,0:T(8,128)(2,1)S(1)}, bf16[128,1024]{1,0:T(8,128)(2,1)S(1)}, u32[]{:S(2)}, u32[]{:S(2)}) %collective-permute-start.22) | collective-permute-done | bytes 262176 | tf_op jit(solution)/shard_map/ppermute | solution.py:48
  127.5 2.1 collective-permute-start.41
  131.2 2.2 collective-permute-done.23.u2
  134.9 3.1 collective-permute-start.32
  138.2 12.0 %shard_map.237 = (bf16[512,1024]{1,0:T(8,128)(2,1)S(1)}, bf16[512,1024]{1,0:T(8,128)(2,1)S(1)}, bf16[512,1792]{1,0:T(8,128)(2,1)S(1)}, bf16[256,1024]{1,0:T(8,12...) custom-call(s32[8]{0:T(128)S(1)} %stack.37.place, bf16[128,1024]{1,0:T(8,128)(2,1)S(1)} %get-tuple-element.227.u0.up, ...), custom_call_target="tpu_custom_call" | custom-call | flops 1 | bytes 1 | tf_op jit(solution)/shard_map/pallas_call | solution.py:77
  150.2 2.5 shard_map.240
  152.7 1.6 collective-permute-start.28
  154.3 2.1 collective-permute-start.29
  160.4 2.7 shard_map.243
  163.1 4.6 %collective-permute-done.42.g0 = bf16[256,768]{1,0:T(8,128)(2,1)S(1)} collective-permute-done((bf16[256,768]{1,0:T(8,128)(2,1)S(1)}, bf16[256,768]{1,0:T(8,128)(2,1)S(1)}, u32[]{:S(2)}, u32[]{:S(2)}) %collective-permute-start.42) | collective-permute-done | bytes 393248 | tf_op jit(solution)/shard_map/ppermute | solution.py:48
  170.1 3.1 collective-permute-done.28.ga
  173.2 2.8 collective-permute-start.45
  176.9 3.6 %collective-permute-done.43.g1 = bf16[256,768]{1,0:T(8,128)(2,1)S(1)} collective-permute-done((bf16[256,768]{1,0:T(8,128)(2,1)S(1)}, bf16[256,768]{1,0:T(8,128)(2,1)S(1)}, u32[]{:S(2)}, u32[]{:S(2)}) %collective-permute-start.43) | collective-permute-done | bytes 393248 | tf_op jit(solution)/shard_map/ppermute | solution.py:48
  180.5 2.8 collective-permute-done.45.g3
  184.2 2.9 collective-permute-start.46
  187.3 1.9 collective-permute-start.30
  191.0 2.6 collective-permute-done.46.ga
  193.6 2.8 collective-permute-start.37
  196.5 2.6 collective-permute-done.47.gb
  200.4 5.0 %collective-permute-done.27.sz = bf16[128,1024]{1,0:T(8,128)(2,1)S(1)} collective-permute-done((bf16[128,1024]{1,0:T(8,128)(2,1)S(1)}, bf16[128,1024]{1,0:T(8,128)(2,1)S(1)}, u32[]{:S(2)}, u32[]{:S(2)}) %collective-permute-start.27) | collective-permute-done | bytes 262176 | tf_op jit(solution)/shard_map/ppermute | solution.py:48
  206.4 2.0 shard_map.238
  210.4 1.9 collective-permute-done.48.refs_1_
  213.0 2.6 collective-permute-start.52
  217.2 1.8 collective-permute-done.38.ga
  219.7 2.5 collective-permute-done.50.refs_2_
  226.1 2.0 collective-permute-start.57
  228.2 6.5 %collective-permute-done.57.refs_1_ = bf16[64,1536]{1,0:T(8,128)(2,1)S(1)} collective-permute-done((bf16[64,1536]{1,0:T(8,128)(2,1)}, bf16[64,1536]{1,0:T(8,128)(2,1)S(1)}, u32[]{:S(2)}, u32[]{:S(2)}) %collective-permute-start.57) | collective-permute-done | bytes 196640 | tf_op jit(solution)/shard_map/ppermute | solution.py:48
  238.1 2.0 collective-permute-start.60
  243.3 6.8 %collective-permute-done.60.refs_3_ = bf16[32,2304]{1,0:T(8,128)(2,1)S(1)} collective-permute-done((bf16[32,2304]{1,0:T(8,128)(2,1)S(1)}, bf16[32,2304]{1,0:T(8,128)(2,1)S(1)}, u32[]{:S(2)}, u32[]{:S(2)}) %collective-permute-start.60) | collective-permute-done | bytes 147488 | tf_op jit(solution)/shard_map/ppermute | solution.py:48
  250.1 2.1 collective-permute-done.61.refs_4_
  257.3 3.1 collective-permute-done.54.refs_2_
  261.4 2.1 shard_map.252
  263.5 4.8 %collective-permute-done.64.gb = bf16[64,1536]{1,0:T(8,128)(2,1)} collective-permute-done((bf16[64,1536]{1,0:T(8,128)(2,1)}, bf16[64,1536]{1,0:T(8,128)(2,1)}, u32[]{:S(2)}, u32[]{:S(2)}) %collective-permute-start.64) | collective-permute-done | bytes 196640 | tf_op jit(solution)/shard_map/ppermute | solution.py:48
  271.9 3.5 %collective-permute-done.56 = f32[1,6]{1,0:T(1,128)S(1)} collective-permute-done((f32[1,6]{1,0:T(1,128)S(1)}, f32[1,6]{1,0:T(1,128)S(1)}, u32[]{:S(2)}, u32[]{:S(2)}) %collective-permute-start.56) | collective-permute-done | bytes 56 | tf_op jit(solution)/shard_map/ppermute | solution.py:48
  276.0 13.9 %collective-permute-done.66.gb = bf16[128,1536]{1,0:T(8,128)(2,1)S(1)} collective-permute-done((bf16[128,1536]{1,0:T(8,128)(2,1)S(1)}, bf16[128,1536]{1,0:T(8,128)(2,1)S(1)}, u32[]{:S(2)}, u32[]{:S(2)}) %collective-permute-start.66) | collective-permute-done | bytes 393248 | tf_op jit(solution)/shard_map/ppermute | solution.py:48
  289.8 3.1 collective-permute-done.65.ga
  293.8 2.8 collective-permute-start.69
  296.7 5.4 %collective-permute-done.68.g1 = bf16[256,768]{1,0:T(8,128)(2,1)S(1)} collective-permute-done((bf16[256,768]{1,0:T(8,128)(2,1)S(1)}, bf16[256,768]{1,0:T(8,128)(2,1)S(1)}, u32[]{:S(2)}, u32[]{:S(2)}) %collective-permute-start.68) | collective-permute-done | bytes 393248 | tf_op jit(solution)/shard_map/ppermute | solution.py:48
  303.4 2.3 collective-permute-done.70.g3
  305.7 1.7 shard_map.258
  309.9 2.1 collective-permute-start.74
  312.1 2.8 copy-done.10
  314.8 5.6 %shard_map.260 = (f32[2,256,3072]{2,1,0:T(8,128)}, f32[2,256,1024]{2,1,0:T(8,128)}, f32[2,256,4096]{2,1,0:T(8,128)}, f32[2,1024,1024]{2,1,0:T(8,128)}) custom-call(bf16[2048,1536]{1,0:T(8,128)(2,1)S(1)} %copy-done.10), custom_call_target="tpu_custom_call" | custom-call | flops 1 | bytes 1 | tf_op jit(solution)/shard_map/pallas_call | solution.py:77
  320.5 4.1 %shard_map.261 = (f32[2,256,3072]{2,1,0:T(8,128)}, f32[2,256,1024]{2,1,0:T(8,128)}, f32[2,256,4096]{2,1,0:T(8,128)}, f32[2,1024,1024]{2,1,0:T(8,128)}) custom-call(s32[8]{0:T(128)S(1)} %stack.37.place, bf16[544,768]{1,0:T(8,128)(2,1)S(1)} %get-tuple-element.326.p0.refs_0_, ...), custom_call_target="tpu_custom_call", output_to_operand_aliasing={{0}: (5, {}), {1}: (6, {}), {2}: (7, {}), {3}: (8, {})} | custom-call | flops 1 | bytes 1 | tf_op jit(solution)/shard_map/pallas_call | solution.py:77
  328.0 5.2 %shard_map.262 = (f32[2,256,3072]{2,1,0:T(8,128)}, f32[2,256,1024]{2,1,0:T(8,128)}, f32[2,256,4096]{2,1,0:T(8,128)}, f32[2,1024,1024]{2,1,0:T(8,128)}, f32[2,256...) custom-call(s32[8]{0:T(128)S(1)} %stack.37.place, ...), custom_call_target="tpu_custom_call", output_to_operand_aliasing={{0}: (6, {}), {1}: (7, {}), {2}: (8, {}), {3}: (9, {})} | custom-call | flops 1 | bytes 1 | tf_op jit(solution)/shard_map/pallas_call | solution.py:77
  (240 shorter events, 74.4 us)
Async XLA Ops:
  7.2 304.9 %all-gather.2.cloned.1.call-start = ((), (), s32[]{:S(2)}) async-start(), calls=%async_computation | async-start | bytes 6684672 | tf_op jit(solution)/shard_map/all_gather | solution.py:880
  15.0 14.8 %collective-permute-start.5 = (bf16[272,768]{1,0:T(8,128)(2,1)S(1)}, bf16[272,768]{1,0:T(8,128)(2,1)S(1)}, u32[]{:S(2)}, u32[]{:S(2)}) collective-permute-start(bf16[272,768]{1,0:T(8,128)(2,1)S(1)} %get-tuple-element.187), channel_id=1, source_target_pairs={{0,19},{1,18},{2,17},{3,16},{4,23},{5,22},{6,21},{7,20},{8,27},{9,... | collective-permute-start | bytes 1253384 | tf_op jit(solution)/shard_map/ppermute | solution.py:48
  19.3 13.5 %collective-permute-start.1 = (bf16[128,1024]{1,0:T(8,128)(2,1)}, bf16[128,1024]{1,0:T(8,128)(2,1)}, u32[]{:S(2)}, u32[]{:S(2)}) collective-permute-start(bf16[128,1024]{1,0:T(8,128)(2,1)} %state.3), channel_id=1, source_target_pairs={{0,2},{1,3},{2,0},{3,1},{4,6},{5,7},{6,4},{7,5},{8,10},{9,11},{10,... | collective-permute-start | bytes 786440 | tf_op jit(solution)/shard_map/ppermute | solution.py:48
  19.3 26.9 %collective-permute-start.3 = (bf16[272,768]{1,0:T(8,128)(2,1)}, bf16[272,768]{1,0:T(8,128)(2,1)}, u32[]{:S(2)}, u32[]{:S(2)}) collective-permute-start(bf16[272,768]{1,0:T(8,128)(2,1)} %get-tuple-element.185), channel_id=1, source_target_pairs={{0,1},{1,0},{2,3},{3,2},{4,5},{5,4},{6,7},{7,6},{8,9},{9,8},{10,11... | collective-permute-start | bytes 1253384 | tf_op jit(solution)/shard_map/ppermute | solution.py:48
  19.3 31.7 %collective-permute-start.4 = (bf16[272,768]{1,0:T(8,128)(2,1)}, bf16[272,768]{1,0:T(8,128)(2,1)}, u32[]{:S(2)}, u32[]{:S(2)}) collective-permute-start(bf16[272,768]{1,0:T(8,128)(2,1)} %get-tuple-element.186), channel_id=1, source_target_pairs={{0,2},{1,3},{2,0},{3,1},{4,6},{5,7},{6,4},{7,5},{8,10},{9,11},{10,... | collective-permute-start | bytes 1253384 | tf_op jit(solution)/shard_map/ppermute | solution.py:48
  30.6 15.4 %collective-permute-start.10 = (bf16[256,1024]{1,0:T(8,128)(2,1)}, bf16[256,1024]{1,0:T(8,128)(2,1)}, u32[]{:S(2)}, u32[]{:S(2)}) collective-permute-start(bf16[256,1024]{1,0:T(8,128)(2,1)} %get-tuple-element.199), channel_id=1, source_target_pairs={{0,19},{1,18},{2,17},{3,16},{4,23},{5,22},{6,21},{7,20},{8,27},{9,... | collective-permute-start | bytes 1572872 | tf_op jit(solution)/shard_map/ppermute | solution.py:48
  32.8 26.0 %collective-permute-start.6 = (bf16[384,1024]{1,0:T(8,128)(2,1)}, bf16[384,1024]{1,0:T(8,128)(2,1)}, u32[]{:S(2)}, u32[]{:S(2)}) collective-permute-start(bf16[384,1024]{1,0:T(8,128)(2,1)} %get-tuple-element.193), channel_id=1, source_target_pairs={{0,2},{1,3},{2,0},{3,1},{4,6},{5,7},{6,4},{7,5},{8,10},{9,11},{10,... | collective-permute-start | bytes 2359304 | tf_op jit(solution)/shard_map/ppermute | solution.py:48
  33.0 25.8 %collective-permute-start.9 = (bf16[256,1024]{1,0:T(8,128)(2,1)}, bf16[256,1024]{1,0:T(8,128)(2,1)S(1)}, u32[]{:S(2)}, u32[]{:S(2)}) collective-permute-start(bf16[256,1024]{1,0:T(8,128)(2,1)} %copy-done.42), channel_id=1, source_target_pairs={{0,1},{1,0},{2,3},{3,2},{4,5},{5,4},{6,7},{7,6},{8,9},{9,8},{10,11... | collective-permute-start | bytes 1572872 | tf_op jit(solution)/shard_map/ppermute | solution.py:48
  46.0 5.0 %collective-permute-start.2 = (bf16[128,1024]{1,0:T(8,128)(2,1)}, bf16[128,1024]{1,0:T(8,128)(2,1)S(1)}, u32[]{:S(2)}, u32[]{:S(2)}) collective-permute-start(bf16[128,1024]{1,0:T(8,128)(2,1)} %collective-permute-done.1.x2), channel_id=1, source_target_pairs={{0,1},{1,0},{2,3},{3,2},{4,5},{5,4},{6,7},{7,6},{8,9},{9,8},{10,11... | collective-permute-start | bytes 786440 | tf_op jit(solution)/shard_map/ppermute | solution.py:48
  46.2 43.8 %collective-permute-start.19 = (bf16[512,1792]{1,0:T(8,128)(2,1)}, bf16[512,1792]{1,0:T(8,128)(2,1)S(1)}, u32[]{:S(2)}, u32[]{:S(2)}) collective-permute-start(bf16[512,1792]{1,0:T(8,128)(2,1)} %copy-done.38), channel_id=1, source_target_pairs={{0,18},{1,19},{2,16},{3,17},{4,22},{5,23},{6,20},{7,21},{8,26},{9,... | collective-permute-start | bytes 5505032 | tf_op jit(solution)/shard_map/ppermute | solution.py:48
  65.6 9.2 %collective-permute-start.12 = (bf16[128,1024]{1,0:T(8,128)(2,1)S(1)}, bf16[128,1024]{1,0:T(8,128)(2,1)S(1)}, u32[]{:S(2)}, u32[]{:S(2)}) collective-permute-start(bf16[128,1024]{1,0:T(8,128)(2,1)S(1)} %add_convert_fusion.2), channel_id=1, source_target_pairs={{0,2},{1,3},{2,0},{3,1},{4,6},{5,7},{6,4},{7,5},{8,10},{9,11},{10,... | collective-permute-start | bytes 786440 | tf_op jit(solution)/shard_map/ppermute | solution.py:48
  66.4 13.3 %collective-permute-start.8 = (bf16[128,1024]{1,0:T(8,128)(2,1)S(1)}, bf16[128,1024]{1,0:T(8,128)(2,1)S(1)}, u32[]{:S(2)}, u32[]{:S(2)}) collective-permute-start(bf16[128,1024]{1,0:T(8,128)(2,1)S(1)} %add_convert_fusion.3), channel_id=1, source_target_pairs={{0,2},{1,3},{2,0},{3,1},{4,6},{5,7},{6,4},{7,5},{8,10},{9,11},{10,... | collective-permute-start | bytes 786440 | tf_op jit(solution)/shard_map/ppermute | solution.py:48
  80.8 7.6 %collective-permute-start.14 = (bf16[128,1024]{1,0:T(8,128)(2,1)S(1)}, bf16[128,1024]{1,0:T(8,128)(2,1)S(1)}, u32[]{:S(2)}, u32[]{:S(2)}) collective-permute-start(bf16[128,1024]{1,0:T(8,128)(2,1)S(1)} %get-tuple-element.203.n0), channel_id=1, source_target_pairs={{0,2},{1,3},{2,0},{3,1},{4,6},{5,7},{6,4},{7,5},{8,10},{9,11},{10,... | collective-permute-start | bytes 786440 | tf_op jit(solution)/shard_map/ppermute | solution.py:48
  81.1 12.5 %collective-permute-start.18 = (bf16[256,1792]{1,0:T(8,128)(2,1)S(1)}, bf16[256,1792]{1,0:T(8,128)(2,1)S(1)}, u32[]{:S(2)}, u32[]{:S(2)}) collective-permute-start(bf16[256,1792]{1,0:T(8,128)(2,1)S(1)} %copy-done.41), channel_id=1, source_target_pairs={{0,1},{1,0},{2,3},{3,2},{4,5},{5,4},{6,7},{7,6},{8,9},{9,8},{10,11... | collective-permute-start | bytes 2752520 | tf_op jit(solution)/shard_map/ppermute | solution.py:48
  90.1 4.5 %collective-permute-start.20 = (bf16[256,1792]{1,0:T(8,128)(2,1)S(1)}, bf16[256,1792]{1,0:T(8,128)(2,1)S(1)}, u32[]{:S(2)}, u32[]{:S(2)}) collective-permute-start(bf16[256,1792]{1,0:T(8,128)(2,1)S(1)} %slice.47), channel_id=1, source_target_pairs={{0,1},{1,0},{2,3},{3,2},{4,5},{5,4},{6,7},{7,6},{8,9},{9,8},{10,11... | collective-permute-start | bytes 2752520 | tf_op jit(solution)/shard_map/ppermute | solution.py:48
  116.0 8.5 %collective-permute-start.22 = (bf16[128,1024]{1,0:T(8,128)(2,1)S(1)}, bf16[128,1024]{1,0:T(8,128)(2,1)S(1)}, u32[]{:S(2)}, u32[]{:S(2)}) collective-permute-start(bf16[128,1024]{1,0:T(8,128)(2,1)S(1)} %add_convert_fusion.1), channel_id=1, source_target_pairs={{0,2},{1,3},{2,0},{3,1},{4,6},{5,7},{6,4},{7,5},{8,10},{9,11},{10,... | collective-permute-start | bytes 786440 | tf_op jit(solution)/shard_map/ppermute | solution.py:48
  125.7 7.7 %collective-permute-start.23 = (bf16[128,1024]{1,0:T(8,128)(2,1)S(1)}, bf16[128,1024]{1,0:T(8,128)(2,1)S(1)}, u32[]{:S(2)}, u32[]{:S(2)}) collective-permute-start(bf16[128,1024]{1,0:T(8,128)(2,1)S(1)} %get-tuple-element.227.u0.up), channel_id=1, source_target_pairs={{0,2},{1,3},{2,0},{3,1},{4,6},{5,7},{6,4},{7,5},{8,10},{9,11},{10,... | collective-permute-start | bytes 786440 | tf_op jit(solution)/shard_map/ppermute | solution.py:48
  126.0 28.3 %collective-permute-start.40 = (bf16[512,768]{1,0:T(8,128)(2,1)}, bf16[512,768]{1,0:T(8,128)(2,1)S(1)}, u32[]{:S(2)}, u32[]{:S(2)}) collective-permute-start(bf16[512,768]{1,0:T(8,128)(2,1)} %get-tuple-element.277), channel_id=1, source_target_pairs={{0,32},{1,33},{2,34},{3,35},{4,36},{5,37},{6,38},{7,39},{8,40},{9,... | collective-permute-start | bytes 2359304 | tf_op jit(solution)/shard_map/ppermute | solution.py:48
  127.5 28.9 %collective-permute-start.41 = (bf16[512,768]{1,0:T(8,128)(2,1)}, bf16[512,768]{1,0:T(8,128)(2,1)S(1)}, u32[]{:S(2)}, u32[]{:S(2)}) collective-permute-start(bf16[512,768]{1,0:T(8,128)(2,1)} %get-tuple-element.279), channel_id=1, source_target_pairs={{0,96},{1,97},{2,98},{3,99},{4,100},{5,101},{6,102},{7,103},{8,104... | collective-permute-start | bytes 2359304 | tf_op jit(solution)/shard_map/ppermute | solution.py:48
  129.6 27.9 %collective-permute-start.31 = (bf16[512,768]{1,0:T(8,128)(2,1)S(1)}, bf16[512,768]{1,0:T(8,128)(2,1)S(1)}, u32[]{:S(2)}, u32[]{:S(2)}) collective-permute-start(bf16[512,768]{1,0:T(8,128)(2,1)S(1)} %get-tuple-element.249), channel_id=1, source_target_pairs={{0,4},{1,5},{2,6},{3,7},{4,0},{5,1},{6,2},{7,3},{8,12},{9,13},{10,... | collective-permute-start | bytes 2359304 | tf_op jit(solution)/shard_map/ppermute | solution.py:48
  133.4 4.7 %collective-permute-start.25 = (bf16[128,1024]{1,0:T(8,128)(2,1)S(1)}, bf16[128,1024]{1,0:T(8,128)(2,1)S(1)}, u32[]{:S(2)}, u32[]{:S(2)}) collective-permute-start(bf16[128,1024]{1,0:T(8,128)(2,1)S(1)} %collective-permute-done.23.u2), channel_id=1, source_target_pairs={{0,1},{1,0},{2,3},{3,2},{4,5},{5,4},{6,7},{7,6},{8,9},{9,8},{10,11... | collective-permute-start | bytes 786440 | tf_op jit(solution)/shard_map/ppermute | solution.py:48
  134.9 23.9 %collective-permute-start.32 = (bf16[512,768]{1,0:T(8,128)(2,1)S(1)}, bf16[512,768]{1,0:T(8,128)(2,1)S(1)}, u32[]{:S(2)}, u32[]{:S(2)}) collective-permute-start(bf16[512,768]{1,0:T(8,128)(2,1)S(1)} %get-tuple-element.251), channel_id=1, source_target_pairs={{0,12},{1,13},{2,14},{3,15},{4,8},{5,9},{6,10},{7,11},{8,4},{9,5},... | collective-permute-start | bytes 2359304 | tf_op jit(solution)/shard_map/ppermute | solution.py:48
  152.7 20.5 %collective-permute-start.28 = (bf16[512,768]{1,0:T(8,128)(2,1)S(1)}, bf16[512,768]{1,0:T(8,128)(2,1)S(1)}, u32[]{:S(2)}, u32[]{:S(2)}) collective-permute-start(bf16[512,768]{1,0:T(8,128)(2,1)S(1)} %get-tuple-element.241), channel_id=1, source_target_pairs={{0,32},{1,33},{2,34},{3,35},{4,36},{5,37},{6,38},{7,39},{8,40},{9,... | collective-permute-start | bytes 2359304 | tf_op jit(solution)/shard_map/ppermute | solution.py:48
  154.3 21.7 %collective-permute-start.29 = (bf16[512,768]{1,0:T(8,128)(2,1)S(1)}, bf16[512,768]{1,0:T(8,128)(2,1)S(1)}, u32[]{:S(2)}, u32[]{:S(2)}) collective-permute-start(bf16[512,768]{1,0:T(8,128)(2,1)S(1)} %get-tuple-element.243), channel_id=1, source_target_pairs={{0,96},{1,97},{2,98},{3,99},{4,100},{5,101},{6,102},{7,103},{8,104... | collective-permute-start | bytes 2359304 | tf_op jit(solution)/shard_map/ppermute | solution.py:48
  157.3 10.4 %collective-permute-start.42 = (bf16[256,768]{1,0:T(8,128)(2,1)S(1)}, bf16[256,768]{1,0:T(8,128)(2,1)S(1)}, u32[]{:S(2)}, u32[]{:S(2)}) collective-permute-start(bf16[256,768]{1,0:T(8,128)(2,1)S(1)} %get-tuple-element.281), channel_id=1, source_target_pairs={{0,4},{1,5},{2,6},{3,7},{4,0},{5,1},{6,2},{7,3},{8,12},{9,13},{10,... | collective-permute-start | bytes 1179656 | tf_op jit(solution)/shard_map/ppermute | solution.py:48
  157.6 11.7 %collective-permute-start.44 = (bf16[256,768]{1,0:T(8,128)(2,1)S(1)}, bf16[256,768]{1,0:T(8,128)(2,1)S(1)}, u32[]{:S(2)}, u32[]{:S(2)}) collective-permute-start(bf16[256,768]{1,0:T(8,128)(2,1)S(1)} %get-tuple-element.284), channel_id=1, source_target_pairs={{0,12},{1,13},{2,14},{3,15},{4,8},{5,9},{6,10},{7,11},{8,4},{9,5},... | collective-permute-start | bytes 1179656 | tf_op jit(solution)/shard_map/ppermute | solution.py:48
  159.7 20.8 %collective-permute-start.43 = (bf16[256,768]{1,0:T(8,128)(2,1)S(1)}, bf16[256,768]{1,0:T(8,128)(2,1)S(1)}, u32[]{:S(2)}, u32[]{:S(2)}) collective-permute-start(bf16[256,768]{1,0:T(8,128)(2,1)S(1)} %get-tuple-element.252), channel_id=1, source_target_pairs={{0,32},{1,33},{2,34},{3,35},{4,36},{5,37},{6,38},{7,39},{8,40},{9,... | collective-permute-start | bytes 1179656 | tf_op jit(solution)/shard_map/ppermute | solution.py:48
  167.7 19.6 %collective-permute-start.33 = (bf16[512,768]{1,0:T(8,128)(2,1)S(1)}, bf16[512,768]{1,0:T(8,128)(2,1)S(1)}, u32[]{:S(2)}, u32[]{:S(2)}) collective-permute-start(bf16[512,768]{1,0:T(8,128)(2,1)S(1)} %get-tuple-element.256), channel_id=1, source_target_pairs={{0,4},{1,5},{2,6},{3,7},{4,0},{5,1},{6,2},{7,3},{8,12},{9,13},{10,... | collective-permute-start | bytes 2359304 | tf_op jit(solution)/shard_map/ppermute | solution.py:48
  169.3 19.9 %collective-permute-start.34 = (bf16[512,768]{1,0:T(8,128)(2,1)S(1)}, bf16[512,768]{1,0:T(8,128)(2,1)S(1)}, u32[]{:S(2)}, u32[]{:S(2)}) collective-permute-start(bf16[512,768]{1,0:T(8,128)(2,1)S(1)} %get-tuple-element.258), channel_id=1, source_target_pairs={{0,12},{1,13},{2,14},{3,15},{4,8},{5,9},{6,10},{7,11},{8,4},{9,5},... | collective-permute-start | bytes 2359304 | tf_op jit(solution)/shard_map/ppermute | solution.py:48
  173.2 10.1 %collective-permute-start.45 = (bf16[256,768]{1,0:T(8,128)(2,1)S(1)}, bf16[256,768]{1,0:T(8,128)(2,1)S(1)}, u32[]{:S(2)}, u32[]{:S(2)}) collective-permute-start(bf16[256,768]{1,0:T(8,128)(2,1)S(1)} %get-tuple-element.286), channel_id=1, source_target_pairs={{0,96},{1,97},{2,98},{3,99},{4,100},{5,101},{6,102},{7,103},{8,104... | collective-permute-start | bytes 1179656 | tf_op jit(solution)/shard_map/ppermute | solution.py:48
  176.0 14.9 %collective-permute-start.26 = (bf16[256,1024]{1,0:T(8,128)(2,1)S(1)}, bf16[256,1024]{1,0:T(8,128)(2,1)S(1)}, u32[]{:S(2)}, u32[]{:S(2)}) collective-permute-start(bf16[256,1024]{1,0:T(8,128)(2,1)S(1)} %get-tuple-element.231), channel_id=1, source_target_pairs={{0,1},{1,0},{2,3},{3,2},{4,5},{5,4},{6,7},{7,6},{8,9},{9,8},{10,11... | collective-permute-start | bytes 1572872 | tf_op jit(solution)/shard_map/ppermute | solution.py:48
  184.2 9.4 %collective-permute-start.46 = (bf16[128,1536]{1,0:T(8,128)(2,1)S(1)}, bf16[128,1536]{1,0:T(8,128)(2,1)S(1)}, u32[]{:S(2)}, u32[]{:S(2)}) collective-permute-start(bf16[128,1536]{1,0:T(8,128)(2,1)S(1)} %get-tuple-element.288), channel_id=1, source_target_pairs={{0,96},{1,97},{2,98},{3,99},{4,100},{5,101},{6,102},{7,103},{8,104... | collective-permute-start | bytes 1179656 | tf_op jit(solution)/shard_map/ppermute | solution.py:48
  187.1 11.9 %collective-permute-start.47 = (bf16[128,1536]{1,0:T(8,128)(2,1)S(1)}, bf16[128,1536]{1,0:T(8,128)(2,1)S(1)}, u32[]{:S(2)}, u32[]{:S(2)}) collective-permute-start(bf16[128,1536]{1,0:T(8,128)(2,1)S(1)} %get-tuple-element.290), channel_id=1, source_target_pairs={{0,4},{1,5},{2,6},{3,7},{4,0},{5,1},{6,2},{7,3},{8,12},{9,13},{10,... | collective-permute-start | bytes 1179656 | tf_op jit(solution)/shard_map/ppermute | solution.py:48
  187.3 19.1 %collective-permute-start.30 = (bf16[256,768]{1,0:T(8,128)(2,1)S(1)}, bf16[256,768]{1,0:T(8,128)(2,1)S(1)}, u32[]{:S(2)}, u32[]{:S(2)}) collective-permute-start(bf16[256,768]{1,0:T(8,128)(2,1)S(1)} %get-tuple-element.245), channel_id=1, source_target_pairs={{0,4},{1,5},{2,6},{3,7},{4,0},{5,1},{6,2},{7,3},{8,12},{9,13},{10,... | collective-permute-start | bytes 1179656 | tf_op jit(solution)/shard_map/ppermute | solution.py:48
  189.2 19.8 %collective-permute-start.36 = (bf16[256,768]{1,0:T(8,128)(2,1)S(1)}, bf16[256,768]{1,0:T(8,128)(2,1)S(1)}, u32[]{:S(2)}, u32[]{:S(2)}) collective-permute-start(bf16[256,768]{1,0:T(8,128)(2,1)S(1)} %get-tuple-element.262), channel_id=1, source_target_pairs={{0,12},{1,13},{2,14},{3,15},{4,8},{5,9},{6,10},{7,11},{8,4},{9,5},... | collective-permute-start | bytes 1179656 | tf_op jit(solution)/shard_map/ppermute | solution.py:48
  190.9 18.0 %collective-permute-start.35 = (bf16[256,768]{1,0:T(8,128)(2,1)S(1)}, bf16[256,768]{1,0:T(8,128)(2,1)S(1)}, u32[]{:S(2)}, u32[]{:S(2)}) collective-permute-start(bf16[256,768]{1,0:T(8,128)(2,1)S(1)} %get-tuple-element.260), channel_id=1, source_target_pairs={{0,32},{1,33},{2,34},{3,35},{4,36},{5,37},{6,38},{7,39},{8,40},{9,... | collective-permute-start | bytes 1179656 | tf_op jit(solution)/shard_map/ppermute | solution.py:48
  193.6 15.4 %collective-permute-start.37 = (bf16[256,768]{1,0:T(8,128)(2,1)S(1)}, bf16[256,768]{1,0:T(8,128)(2,1)S(1)}, u32[]{:S(2)}, u32[]{:S(2)}) collective-permute-start(bf16[256,768]{1,0:T(8,128)(2,1)S(1)} %get-tuple-element.264), channel_id=1, source_target_pairs={{0,96},{1,97},{2,98},{3,99},{4,100},{5,101},{6,102},{7,103},{8,104... | collective-permute-start | bytes 1179656 | tf_op jit(solution)/shard_map/ppermute | solution.py:48
  199.0 6.4 %collective-permute-start.27 = (bf16[128,1024]{1,0:T(8,128)(2,1)S(1)}, bf16[128,1024]{1,0:T(8,128)(2,1)S(1)}, u32[]{:S(2)}, u32[]{:S(2)}) collective-permute-start(bf16[128,1024]{1,0:T(8,128)(2,1)S(1)} %add_convert_fusion), channel_id=1, source_target_pairs={{0,2},{1,3},{2,0},{3,1},{4,6},{5,7},{6,4},{7,5},{8,10},{9,11},{10,... | collective-permute-start | bytes 786440 | tf_op jit(solution)/shard_map/ppermute | solution.py:48
  205.4 6.9 %collective-permute-start.48 = (bf16[64,1536]{1,0:T(8,128)(2,1)S(1)}, bf16[64,1536]{1,0:T(8,128)(2,1)S(1)}, u32[]{:S(2)}, u32[]{:S(2)}) collective-permute-start(bf16[64,1536]{1,0:T(8,128)(2,1)S(1)} %get-tuple-element.292), channel_id=1, source_target_pairs={{0,12},{1,13},{2,14},{3,15},{4,8},{5,9},{6,10},{7,11},{8,4},{9,5},... | collective-permute-start | bytes 589832 | tf_op jit(solution)/shard_map/ppermute | solution.py:48
  206.4 5.9 %collective-permute-start.49 = (bf16[64,1536]{1,0:T(8,128)(2,1)S(1)}, bf16[64,1536]{1,0:T(8,128)(2,1)S(1)}, u32[]{:S(2)}, u32[]{:S(2)}) collective-permute-start(bf16[64,1536]{1,0:T(8,128)(2,1)S(1)} %get-tuple-element.294), channel_id=1, source_target_pairs={{0,32},{1,33},{2,34},{3,35},{4,36},{5,37},{6,38},{7,39},{8,40},{9,... | collective-permute-start | bytes 589832 | tf_op jit(solution)/shard_map/ppermute | solution.py:48
  209.9 9.1 %collective-permute-start.38 = (bf16[128,1536]{1,0:T(8,128)(2,1)S(1)}, bf16[128,1536]{1,0:T(8,128)(2,1)S(1)}, u32[]{:S(2)}, u32[]{:S(2)}) collective-permute-start(bf16[128,1536]{1,0:T(8,128)(2,1)S(1)} %get-tuple-element.266), channel_id=1, source_target_pairs={{0,96},{1,97},{2,98},{3,99},{4,100},{5,101},{6,102},{7,103},{8,104... | collective-permute-start | bytes 1179656 | tf_op jit(solution)/shard_map/ppermute | solution.py:48
  210.3 8.6 %collective-permute-start.39 = (bf16[128,1536]{1,0:T(8,128)(2,1)S(1)}, bf16[128,1536]{1,0:T(8,128)(2,1)S(1)}, u32[]{:S(2)}, u32[]{:S(2)}) collective-permute-start(bf16[128,1536]{1,0:T(8,128)(2,1)S(1)} %get-tuple-element.268), channel_id=1, source_target_pairs={{0,4},{1,5},{2,6},{3,7},{4,0},{5,1},{6,2},{7,3},{8,12},{9,13},{10,... | collective-permute-start | bytes 1179656 | tf_op jit(solution)/shard_map/ppermute | solution.py:48
  213.0 9.5 %collective-permute-start.52 = (bf16[32,4352]{1,0:T(8,128)(2,1)S(1)}, bf16[32,4352]{1,0:T(8,128)(2,1)S(1)}, u32[]{:S(2)}, u32[]{:S(2)}) collective-permute-start(bf16[32,4352]{1,0:T(8,128)(2,1)S(1)} %get-tuple-element.298), channel_id=1, source_target_pairs={{0,16},{1,17},{2,18},{3,19},{4,20},{5,21},{6,22},{7,23},{8,24},{9,... | collective-permute-start | bytes 835592 | tf_op jit(solution)/shard_map/ppermute | solution.py:48
  215.6 6.7 %collective-permute-start.50 = (bf16[32,1792]{1,0:T(8,128)(2,1)S(1)}, bf16[32,1792]{1,0:T(8,128)(2,1)S(1)}, u32[]{:S(2)}, u32[]{:S(2)}) collective-permute-start(bf16[32,1792]{1,0:T(8,128)(2,1)S(1)} %get-tuple-element.297), channel_id=1, source_target_pairs={{0,2},{1,3},{2,0},{3,1},{4,6},{5,7},{6,4},{7,5},{8,10},{9,11},{10,... | collective-permute-start | bytes 344072 | tf_op jit(solution)/shard_map/ppermute | solution.py:48
  216.5 6.0 %collective-permute-start.51 = (bf16[32,1792]{1,0:T(8,128)(2,1)S(1)}, bf16[32,1792]{1,0:T(8,128)(2,1)S(1)}, u32[]{:S(2)}, u32[]{:S(2)}) collective-permute-start(bf16[32,1792]{1,0:T(8,128)(2,1)S(1)} %get-tuple-element.297), channel_id=1, source_target_pairs={{0,18},{1,19},{2,16},{3,17},{4,22},{5,23},{6,20},{7,21},{8,26},{9,... | collective-permute-start | bytes 344072 | tf_op jit(solution)/shard_map/ppermute | solution.py:48
  225.9 15.4 %collective-permute-start.53 = (bf16[512,1024]{1,0:T(8,128)(2,1)}, bf16[512,1024]{1,0:T(8,128)(2,1)S(1)}, u32[]{:S(2)}, u32[]{:S(2)}) collective-permute-start(bf16[512,1024]{1,0:T(8,128)(2,1)} %copy-done.39), channel_id=1, source_target_pairs={{0,1},{1,0},{2,3},{3,2},{4,5},{5,4},{6,7},{7,6},{8,9},{9,8},{10,11... | collective-permute-start | bytes 3145736 | tf_op jit(solution)/shard_map/ppermute | solution.py:48
  226.1 8.6 %collective-permute-start.57 = (bf16[64,1536]{1,0:T(8,128)(2,1)}, bf16[64,1536]{1,0:T(8,128)(2,1)S(1)}, u32[]{:S(2)}, u32[]{:S(2)}) collective-permute-start(bf16[64,1536]{1,0:T(8,128)(2,1)} %copy-done.44), channel_id=1, source_target_pairs={{0,12},{1,13},{2,14},{3,15},{4,8},{5,9},{6,10},{7,11},{8,4},{9,5},... | collective-permute-start | bytes 589832 | tf_op jit(solution)/shard_map/ppermute | solution.py:48
  228.2 7.1 %collective-permute-start.58 = (bf16[64,1536]{1,0:T(8,128)(2,1)}, bf16[64,1536]{1,0:T(8,128)(2,1)S(1)}, u32[]{:S(2)}, u32[]{:S(2)}) collective-permute-start(bf16[64,1536]{1,0:T(8,128)(2,1)} %copy-done.43), channel_id=1, source_target_pairs={{0,32},{1,33},{2,34},{3,35},{4,36},{5,37},{6,38},{7,39},{8,40},{9,... | collective-permute-start | bytes 589832 | tf_op jit(solution)/shard_map/ppermute | solution.py:48
  236.9 6.4 %collective-permute-start.59 = (bf16[32,2304]{1,0:T(8,128)(2,1)S(1)}, bf16[32,2304]{1,0:T(8,128)(2,1)S(1)}, u32[]{:S(2)}, u32[]{:S(2)}) collective-permute-start(bf16[32,2304]{1,0:T(8,128)(2,1)S(1)} %get-tuple-element.312), channel_id=1, source_target_pairs={{0,2},{1,3},{2,0},{3,1},{4,6},{5,7},{6,4},{7,5},{8,10},{9,11},{10,... | collective-permute-start | bytes 442376 | tf_op jit(solution)/shard_map/ppermute | solution.py:48
  238.1 12.0 %collective-permute-start.60 = (bf16[32,2304]{1,0:T(8,128)(2,1)S(1)}, bf16[32,2304]{1,0:T(8,128)(2,1)S(1)}, u32[]{:S(2)}, u32[]{:S(2)}) collective-permute-start(bf16[32,2304]{1,0:T(8,128)(2,1)S(1)} %get-tuple-element.312), channel_id=1, source_target_pairs={{0,18},{1,19},{2,16},{3,17},{4,22},{5,23},{6,20},{7,21},{8,26},{9,... | collective-permute-start | bytes 442376 | tf_op jit(solution)/shard_map/ppermute | solution.py:48
  240.2 12.1 %collective-permute-start.61 = (bf16[32,4864]{1,0:T(8,128)(2,1)S(1)}, bf16[32,4864]{1,0:T(8,128)(2,1)S(1)}, u32[]{:S(2)}, u32[]{:S(2)}) collective-permute-start(bf16[32,4864]{1,0:T(8,128)(2,1)S(1)} %get-tuple-element.313), channel_id=1, source_target_pairs={{0,16},{1,17},{2,18},{3,19},{4,20},{5,21},{6,22},{7,23},{8,24},{9,... | collective-permute-start | bytes 933896 | tf_op jit(solution)/shard_map/ppermute | solution.py:48
  242.3 18.1 %collective-permute-start.54 = (bf16[256,1024]{1,0:T(8,128)(2,1)}, bf16[256,1024]{1,0:T(8,128)(2,1)}, u32[]{:S(2)}, u32[]{:S(2)}) collective-permute-start(bf16[256,1024]{1,0:T(8,128)(2,1)} %bitcast.9), channel_id=1, source_target_pairs={{0,2},{1,3},{2,0},{3,1},{4,6},{5,7},{6,4},{7,5},{8,10},{9,11},{10,... | collective-permute-start | bytes 1572872 | tf_op jit(solution)/shard_map/ppermute | solution.py:48
  255.6 13.3 %collective-permute-start.63 = (bf16[80,1536]{1,0:T(8,128)(2,1)S(1)}, bf16[80,1536]{1,0:T(8,128)(2,1)}, u32[]{:S(2)}, u32[]{:S(2)}) collective-permute-start(bf16[80,1536]{1,0:T(8,128)(2,1)S(1)} %get-tuple-element.318.oa), channel_id=1, source_target_pairs={{0,12},{1,13},{2,14},{3,15},{4,8},{5,9},{6,10},{7,11},{8,4},{9,5},... | collective-permute-start | bytes 737288 | tf_op jit(solution)/shard_map/ppermute | solution.py:48
  257.1 11.3 %collective-permute-start.64 = (bf16[64,1536]{1,0:T(8,128)(2,1)}, bf16[64,1536]{1,0:T(8,128)(2,1)}, u32[]{:S(2)}, u32[]{:S(2)}) collective-permute-start(bf16[64,1536]{1,0:T(8,128)(2,1)} %get-tuple-element.319.ob), channel_id=1, source_target_pairs={{0,32},{1,33},{2,34},{3,35},{4,36},{5,37},{6,38},{7,39},{8,40},{9,... | collective-permute-start | bytes 589832 | tf_op jit(solution)/shard_map/ppermute | solution.py:48
  270.2 22.8 %collective-permute-start.65 = (bf16[144,1536]{1,0:T(8,128)(2,1)S(1)}, bf16[144,1536]{1,0:T(8,128)(2,1)S(1)}, u32[]{:S(2)}, u32[]{:S(2)}) collective-permute-start(bf16[144,1536]{1,0:T(8,128)(2,1)S(1)} %get-tuple-element.320.oa), channel_id=1, source_target_pairs={{0,96},{1,97},{2,98},{3,99},{4,100},{5,101},{6,102},{7,103},{8,104... | collective-permute-start | bytes 1327112 | tf_op jit(solution)/shard_map/ppermute | solution.py:48
  270.5 19.3 %collective-permute-start.66 = (bf16[128,1536]{1,0:T(8,128)(2,1)S(1)}, bf16[128,1536]{1,0:T(8,128)(2,1)S(1)}, u32[]{:S(2)}, u32[]{:S(2)}) collective-permute-start(bf16[128,1536]{1,0:T(8,128)(2,1)S(1)} %get-tuple-element.321.ob), channel_id=1, source_target_pairs={{0,4},{1,5},{2,6},{3,7},{4,0},{5,1},{6,2},{7,3},{8,12},{9,13},{10,... | collective-permute-start | bytes 1179656 | tf_op jit(solution)/shard_map/ppermute | solution.py:48
  293.6 12.1 %collective-permute-start.67 = (bf16[288,768]{1,0:T(8,128)(2,1)S(1)}, bf16[288,768]{1,0:T(8,128)(2,1)S(1)}, u32[]{:S(2)}, u32[]{:S(2)}) collective-permute-start(bf16[288,768]{1,0:T(8,128)(2,1)S(1)} %get-tuple-element.322.o0), channel_id=1, source_target_pairs={{0,4},{1,5},{2,6},{3,7},{4,0},{5,1},{6,2},{7,3},{8,12},{9,13},{10,... | collective-permute-start | bytes 1327112 | tf_op jit(solution)/shard_map/ppermute | solution.py:48
  293.7 8.4 %collective-permute-start.68 = (bf16[256,768]{1,0:T(8,128)(2,1)S(1)}, bf16[256,768]{1,0:T(8,128)(2,1)S(1)}, u32[]{:S(2)}, u32[]{:S(2)}) collective-permute-start(bf16[256,768]{1,0:T(8,128)(2,1)S(1)} %get-tuple-element.323.o1), channel_id=1, source_target_pairs={{0,32},{1,33},{2,34},{3,35},{4,36},{5,37},{6,38},{7,39},{8,40},{9,... | collective-permute-start | bytes 1179656 | tf_op jit(solution)/shard_map/ppermute | solution.py:48
  293.8 9.6 %collective-permute-start.69 = (bf16[256,768]{1,0:T(8,128)(2,1)S(1)}, bf16[256,768]{1,0:T(8,128)(2,1)S(1)}, u32[]{:S(2)}, u32[]{:S(2)}) collective-permute-start(bf16[256,768]{1,0:T(8,128)(2,1)S(1)} %get-tuple-element.324.o2), channel_id=1, source_target_pairs={{0,12},{1,13},{2,14},{3,15},{4,8},{5,9},{6,10},{7,11},{8,4},{9,5},... | collective-permute-start | bytes 1179656 | tf_op jit(solution)/shard_map/ppermute | solution.py:48
  296.6 9.2 %collective-permute-start.70 = (bf16[256,768]{1,0:T(8,128)(2,1)S(1)}, bf16[256,768]{1,0:T(8,128)(2,1)S(1)}, u32[]{:S(2)}, u32[]{:S(2)}) collective-permute-start(bf16[256,768]{1,0:T(8,128)(2,1)S(1)} %get-tuple-element.325.o3), channel_id=1, source_target_pairs={{0,96},{1,97},{2,98},{3,99},{4,100},{5,101},{6,102},{7,103},{8,104... | collective-permute-start | bytes 1179656 | tf_op jit(solution)/shard_map/ppermute | solution.py:48
  307.5 20.5 %collective-permute-start.71 = (bf16[544,768]{1,0:T(8,128)(2,1)S(1)}, bf16[544,768]{1,0:T(8,128)(2,1)S(1)}, u32[]{:S(2)}, u32[]{:S(2)}) collective-permute-start(bf16[544,768]{1,0:T(8,128)(2,1)S(1)} %get-tuple-element.326.p0.refs_0_), channel_id=1, source_target_pairs={{0,32},{1,33},{2,34},{3,35},{4,36},{5,37},{6,38},{7,39},{8,40},{9,... | collective-permute-start | bytes 2506760 | tf_op jit(solution)/shard_map/ppermute | solution.py:48
  308.0 17.2 %collective-permute-start.72 = (bf16[512,768]{1,0:T(8,128)(2,1)}, bf16[512,768]{1,0:T(8,128)(2,1)}, u32[]{:S(2)}, u32[]{:S(2)}) collective-permute-start(bf16[512,768]{1,0:T(8,128)(2,1)} %get-tuple-element.327.p1), channel_id=1, source_target_pairs={{0,4},{1,5},{2,6},{3,7},{4,0},{5,1},{6,2},{7,3},{8,12},{9,13},{10,... | collective-permute-start | bytes 2359304 | tf_op jit(solution)/shard_map/ppermute | solution.py:48
  309.3 17.2 %collective-permute-start.73 = (bf16[512,768]{1,0:T(8,128)(2,1)S(1)}, bf16[512,768]{1,0:T(8,128)(2,1)}, u32[]{:S(2)}, u32[]{:S(2)}) collective-permute-start(bf16[512,768]{1,0:T(8,128)(2,1)S(1)} %get-tuple-element.328.p2), channel_id=1, source_target_pairs={{0,96},{1,97},{2,98},{3,99},{4,100},{5,101},{6,102},{7,103},{8,104... | collective-permute-start | bytes 2359304 | tf_op jit(solution)/shard_map/ppermute | solution.py:48
  309.9 18.0 %collective-permute-start.74 = (bf16[512,768]{1,0:T(8,128)(2,1)S(1)}, bf16[512,768]{1,0:T(8,128)(2,1)}, u32[]{:S(2)}, u32[]{:S(2)}) collective-permute-start(bf16[512,768]{1,0:T(8,128)(2,1)S(1)} %get-tuple-element.329.p3), channel_id=1, source_target_pairs={{0,12},{1,13},{2,14},{3,15},{4,8},{5,9},{6,10},{7,11},{8,4},{9,5},... | collective-permute-start | bytes 2359304 | tf_op jit(solution)/shard_map/ppermute | solution.py:48
  (58 other events, 337.7 us)
Sparse Core Ops, SparseCore 0:
  226.0 70.6 all-gather.1
where the time goes:
time: 344 us; the launch traced here: 340 us
  waiting for transfers between devices  139 us (40%)
  Pallas kernels  93.5 us (27%)
  starting transfers between devices  67.7 us (20%)
  local copies, waits for them, and re-layouts  20.2 us (6%)
  between operations  15.8 us (5%)
  other arithmetic  3.98 us (1%)
    ppermute x76, waiting for transfers between devices, move(): return lax.ppermute(value, AXES, pairs)  139 us
    pallas_call x35, Pallas kernels, call(): pl.pallas_call(body, out_shape=outs, in_specs=specs, out_specs=out_specs...  93.5 us
    ppermute x76, starting transfers between devices, move(): return lax.ppermute(value, AXES, pairs)  67.6 us
    unnamed x90, local copies, waits for them, and re-layouts  18.6 us
  transfers between devices with their start and end apart: 77, of which 46 were waited for; matrix products, arithmetic and copies ran while one was open for 2% of the time, Pallas kernels for 20%

commit v1 on v0

--- a/solution.py
+++ b/solution.py
@@ -69,7 +69,7 @@
     return jax.ShapeDtypeStruct(dims, dtype)
 
 
-def call(body, args, specs, outs, out_specs=None, scratch=(), flops=0, aliases=None, room=4):
+def call(body, args, specs, outs, out_specs=None, scratch=(), flops=0, aliases=None, room=3):
     held = sum(math.prod(o.shape) * o.dtype.itemsize for o in outs)
     held += sum(math.prod(a.shape) * a.dtype.itemsize for a, s in zip(args, specs) if s is VM)
     held += sum(math.prod(s.shape) * s.dtype.itemsize for s in scratch if jnp.issubdtype(s.dtype, jnp.floating))
@@ -283,8 +283,8 @@
 
 
 def hand_out(left, right, send, keep):
-    for n in range(4):
-        cols = pl.ds(n * 256, 256)
+    for n in range(2):
+        cols = pl.ds(n * 512, 512)
         part = dot(left[...], right[:, cols])
         spread_out(part, cols, send, keep)
 
@@ -339,8 +339,8 @@
     pairs = own_expander(shard, 0, expander, wide) + first_expander(shard, (e1, e2, e3), wide)
     started = copies(pairs + [(shrinker.at[0], shrink)], sems)
     finish(started)
-    for n in range(4):
-        cols = pl.ds(n * 256, 256)
+    for n in range(2):
+        cols = pl.ds(n * 512, 512)
         part = dot(normed[...], wide[:, cols]) + vec[pl.ds(10, 1), cols]
         before[:, cols] = part
         act[:, cols] = gelu_both(part)[0].astype(BF)
@@ -349,9 +349,9 @@
 
 def slopes_out(ss, bias, wide, send, keep):
     bias[...] = jnp.broadcast_to(jnp.sum(ss[...].astype(F32), axis=0, keepdims=True), bias.shape)
-    for n in range(4):
-        part = dot_t(ss[...], wide[pl.ds(n * 256, 256), :])
-        spread_out(part, pl.ds(n * 256, 256), send, keep)
+    for n in range(2):
+        part = dot_t(ss[...], wide[pl.ds(n * 512, 512), :])
+        spread_out(part, pl.ds(n * 512, 512), send, keep)
 
 
 def triple_slopes(slopes, turn, ss):
@@ -364,7 +364,7 @@
 def last_layer(
     place, n0, n1, n2, n3, u0, u1, u2, u3, vec, turn, triple, merger, expander, shrinker, w1, w2, w3,
     normed, up, act, ss, mixed, bsend, bkeep, send, keep, bias,
-    wide, merge, shrink, qkv, slopes, out, before, sems,
+    wide, merge, shrink, qkv, slopes, out, sems,
 ):
     shard, length = place[2], place[3]
     pairs = own_triple(shard, 1, triple, wide) + own_expander(shard, 1, expander, wide)
@@ -376,8 +376,8 @@
         normed[rows, :] = n[...]
         up[rows, :] = jnp.where(row[k * 128 : k * 128 + 128] < length, u[...].astype(F32), 0.0).astype(BF)
     finish(started)
-    for n in range(4):
-        cols = pl.ds(n * 256, 256)
+    for n in range(2):
+        cols = pl.ds(n * 512, 512)
         part = dot(normed[...], wide[:, cols]) + vec[pl.ds(11, 1), cols]
         value, slope = gelu_both(part)
         act[:, cols] = value.astype(BF)
@@ -405,8 +405,8 @@
     for k, u in enumerate((u0, u1, u2, u3)):
         up[pl.ds(k * 128, 128), :] = u[...]
     finish(started)
-    for n in range(4):
-        cols = pl.ds(n * 256, 256)
+    for n in range(2):
+        cols = pl.ds(n * 512, 512)
         value, slope = gelu_both(before[:, cols])
         act[:, cols] = value.astype(BF)
         ss[:, cols] = (dot_t(up[...], shrink[cols, :]) * slope).astype(BF)
@@ -994,11 +994,11 @@
         [SM] + [VM] * 4 + [ANY, VM, VM, HBM, HBM] + [ANY] * 3,
         [full, shape(512, 768), shape(512, 256), send, keep, shape(16, W, dtype=F32)],
         scratch=[wide, merge, pltpu.VMEM((4, 16, 768), BF), pltpu.SemaphoreType.DMA((11,))],
-        room=14,
+        room=9,
         flops=2 * 10**9,
     )
     a_got = move(after(a_send, e_pieces[1]), flip_core=1)
-    w_near, w_far = after(tuple(cut[3:]), e_pieces[2])
+    w_near, w_far = after(tuple(cut[3:]), e_pieces[2], turn)
     w_far = move(w_far, flip_z=3)
     before0, f_send, f_keep = call(
         first_forward,
@@ -1006,7 +1006,7 @@
         [SM, VM, VM, HBM, HBM] + [ANY] * 3,
         [shape(512, W, dtype=F32), send, keep],
         scratch=[wide, shrink, pltpu.VMEM((512, W), BF), pltpu.SemaphoreType.DMA((5,))],
-        room=14,
+        room=9,
         flops=2 * 10**9,
     )
     f_got = move(f_send, flip_core=1)
@@ -1036,9 +1036,9 @@
         + [send, keep, shape(8, WIDE, dtype=F32)],
         scratch=[
             wide, merge, shrink, pltpu.VMEM((512, 768), BF), pltpu.VMEM((512, 768), F32),
-            pltpu.VMEM((512, 256), BF), pltpu.VMEM((512, W), F32), pltpu.SemaphoreType.DMA((9,)),
+            pltpu.VMEM((512, 256), BF), pltpu.SemaphoreType.DMA((9,)),
         ],
-        room=14,
+        room=9,
         flops=8 * 10**9,
     )
     got1 = move(send1, flip_core=1)
@@ -1068,7 +1068,7 @@
             wide, merge, shrink, pltpu.VMEM((512, 768), F32), pltpu.VMEM((512, 256), BF),
             pltpu.SemaphoreType.DMA((12,)),
         ],
-        room=14,
+        room=9,
         flops=5 * 10**9,
     )
     got0 = move(send0, flip_core=1)

time: 344 us -> 343 us (level)
  local copies, waits for them, and re-layouts: 20.2 us -> 14.7 us
    unnamed x90 -> x82, local copies, waits for them, and re-layouts: 18.6 us -> 14.3 us
  transfers between devices with their start and end apart: 77 -> 77, of which waited for: 46 -> 47; matrix products, arithmetic and copies ran while one was open for 2% -> 1% of each run, Pallas kernels for 20% -> 19%
where the time goes in v1:
time: 343 us; the launch traced here: 338 us
  waiting for transfers between devices  142 us (41%)
  Pallas kernels  90.3 us (26%)
  starting transfers between devices  70.5 us (21%)
  between operations  15.7 us (5%)
  local copies, waits for them, and re-layouts  14.7 us (4%)
  other arithmetic  3.99 us (1%)
    ppermute x76, waiting for transfers between devices, move(): return lax.ppermute(value, AXES, pairs)  142 us
    pallas_call x35, Pallas kernels, call(): pl.pallas_call(body, out_shape=outs, in_specs=specs, out_specs=out_specs...  90.3 us
    ppermute x76, starting transfers between devices, move(): return lax.ppermute(value, AXES, pairs)  70.4 us
    unnamed x82, local copies, waits for them, and re-layouts  14.3 us
  transfers between devices with their start and end apart: 77, of which 47 were waited for; matrix products, arithmetic and copies ran while one was open for 1% of the time, Pallas kernels for 19%

profile of v1, /device:TPU:0, one launch (start us, length us, event | category | flops | bytes accessed | tf_op | source)
XLA Modules:
  0.0 337.5 jit_solution(7706617300834511110)
XLA Ops:
  8.0 1.9 copy-done
  13.3 1.9 shard_map.228
  15.1 3.6 %collective-permute-start.5 = (bf16[272,768]{1,0:T(8,128)(2,1)}, bf16[272,768]{1,0:T(8,128)(2,1)}, u32[]{:S(2)}, u32[]{:S(2)}) collective-permute-start(bf16[272,768]{1,0:T(8,128)(2,1)} %get-tuple-element.187), channel_id=1, source_target_pairs={{0,19},{1,18},{2,17},{3,16},{4,23},{5,22},{6,21},{7,20},{8,27},{9,... | collective-permute-start | bytes 1253384 | tf_op jit(solution)/shard_map/ppermute | solution.py:48
  19.5 2.0 collective-permute-start.4
  21.6 2.2 copy-done.2
  26.1 2.8 collective-permute-done.1.x2
  29.1 3.4 %collective-permute-start.10 = (bf16[256,1024]{1,0:T(8,128)(2,1)S(1)}, bf16[256,1024]{1,0:T(8,128)(2,1)S(1)}, u32[]{:S(2)}, u32[]{:S(2)}) collective-permute-start(bf16[256,1024]{1,0:T(8,128)(2,1)S(1)} %get-tuple-element.199), channel_id=1, source_target_pairs={{0,19},{1,18},{2,17},{3,16},{4,23},{5,22},{6,21},{7,20},{8,27},{9,... | collective-permute-start | bytes 1572872 | tf_op jit(solution)/shard_map/ppermute | solution.py:48
  32.9 2.0 fusion.4
  35.1 9.5 %collective-permute-done.10.e3 = bf16[256,1024]{1,0:T(8,128)(2,1)S(1)} collective-permute-done((bf16[256,1024]{1,0:T(8,128)(2,1)S(1)}, bf16[256,1024]{1,0:T(8,128)(2,1)S(1)}, u32[]{:S(2)}, u32[]{:S(2)}) %collective-permute-start.10) | collective-permute-done | bytes 524320 | tf_op jit(solution)/shard_map/ppermute | solution.py:48
  44.5 3.4 %collective-permute-start.19 = (bf16[512,1792]{1,0:T(8,128)(2,1)S(1)}, bf16[512,1792]{1,0:T(8,128)(2,1)S(1)}, u32[]{:S(2)}, u32[]{:S(2)}) collective-permute-start(bf16[512,1792]{1,0:T(8,128)(2,1)S(1)} %get-tuple-element.209), channel_id=1, source_target_pairs={{0,18},{1,19},{2,16},{3,17},{4,22},{5,23},{6,20},{7,21},{8,26},{9,... | collective-permute-start | bytes 5505032 | tf_op jit(solution)/shard_map/ppermute | solution.py:48
  48.2 1.7 collective-permute-done.2.x3
  50.0 6.9 %shard_map.229 = (bf16[512,1024]{1,0:T(8,128)(2,1)S(1)}, bf16[512,768]{1,0:T(8,128)(2,1)S(1)}, bf16[512,256]{1,0:T(8,128)(2,1)S(1)}, bf16[256,1024]{1,0:T(8,128)...) custom-call(s32[8]{0:T(128)S(1)} %stack.37.place, bf16[128,1024]{1,0:T(8,128)(2,1)S(1)} %copy-done.15, ...), custom_call_target="tpu_custom_call" | custom-call | flops 1 | bytes 1 | tf_op jit(solution)/shard_map/pallas_call | solution.py:77
  57.0 3.4 %shard_map.231 = (f32[512,1024]{1,0:T(8,128)S(1)}, bf16[256,1024]{1,0:T(8,128)(2,1)S(1)}, f32[256,1024]{1,0:T(8,128)S(1)}) custom-call(s32[8]{0:T(128)S(1)} %stack.37.place, bf16[512,1024]{1,0:T(8,128)(2,1)S(1)} %get-tuple-element.195.normed, f32[16,1024]{1,0:T(8,128)S(1)} %get-tuple-element.196.vec.refs_6_.refs_3_, bf16[2,256,4096]{2,1,0:T(8,128)(2,1)S(1)} %copy-done.3, ...), custom_call_target="tpu_custom_call" | custom-call | flops 1 | bytes 1 | tf_op jit(solution)/shard_map/pallas_call | solution.py:77
  64.8 7.0 %collective-permute-done.12.refs_5_ = bf16[128,1024]{1,0:T(8,128)(2,1)S(1)} collective-permute-done((bf16[128,1024]{1,0:T(8,128)(2,1)S(1)}, bf16[128,1024]{1,0:T(8,128)(2,1)S(1)}, u32[]{:S(2)}, u32[]{:S(2)}) %collective-permute-start.12) | collective-permute-done | bytes 262176 | tf_op jit(solution)/shard_map/ppermute | solution.py:48
  71.8 4.8 %collective-permute-done.8.refs_2_ = bf16[128,1024]{1,0:T(8,128)(2,1)S(1)} collective-permute-done((bf16[128,1024]{1,0:T(8,128)(2,1)S(1)}, bf16[128,1024]{1,0:T(8,128)(2,1)S(1)}, u32[]{:S(2)}, u32[]{:S(2)}) %collective-permute-start.8) | collective-permute-done | bytes 262176 | tf_op jit(solution)/shard_map/ppermute | solution.py:48
  78.1 7.2 %collective-permute-done.14.n2 = bf16[128,1024]{1,0:T(8,128)(2,1)S(1)} collective-permute-done((bf16[128,1024]{1,0:T(8,128)(2,1)S(1)}, bf16[128,1024]{1,0:T(8,128)(2,1)S(1)}, u32[]{:S(2)}, u32[]{:S(2)}) %collective-permute-start.14) | collective-permute-done | bytes 262176 | tf_op jit(solution)/shard_map/ppermute | solution.py:48
  85.3 2.9 collective-permute-done.19.w2
  89.5 1.7 collective-permute-done.17.u3
  93.3 15.5 %shard_map.233 = (bf16[512,1024]{1,0:T(8,128)(2,1)S(1)}, bf16[512,1024]{1,0:T(8,128)(2,1)S(1)}, bf16[512,1024]{1,0:T(8,128)(2,1)S(1)}, bf16[512,1792]{1,0:T(8,12...) custom-call(s32[8]{0:T(128)S(1)} %stack.37.place, ...), custom_call_target="tpu_custom_call" | custom-call | flops 1 | bytes 1 | tf_op jit(solution)/shard_map/pallas_call | solution.py:77
  110.1 3.6 %shard_map.234 = (bf16[512,768]{1,0:T(8,128)(2,1)}, bf16[512,768]{1,0:T(8,128)(2,1)S(1)}, bf16[512,768]{1,0:T(8,128)(2,1)}, bf16[512,768]{1,0:T(8,128)(2,1)S(1)}) custom-call(s32[8]{0:T(128)S(1)} %stack.37.place, bf16[512,1024]{1,0:T(8,128)(2,1)S(1)} %get-tuple-element.215.act, bf16[512,1024]{1,0:T(8,128)(2,1)S(1)} %get-tuple-element.216.up, ...), custom_call_target="tpu_custom_call" | custom-call | flops 1 | bytes 1 | tf_op jit(solution)/shard_map/pallas_call | solution.py:77
  113.8 3.8 %shard_map.235 = (bf16[512,768]{1,0:T(8,128)(2,1)}, bf16[512,768]{1,0:T(8,128)(2,1)S(1)}, bf16[512,768]{1,0:T(8,128)(2,1)}, bf16[512,768]{1,0:T(8,128)(2,1)S(1)}) custom-call(s32[8]{0:T(128)S(1)} %stack.37.place, bf16[512,1024]{1,0:T(8,128)(2,1)S(1)} %get-tuple-element.215.act, bf16[512,1024]{1,0:T(8,128)(2,1)S(1)} %get-tuple-element.216.up, ...), custom_call_target="tpu_custom_call" | custom-call | flops 1 | bytes 1 | tf_op jit(solution)/shard_map/pallas_call | solution.py:77
  117.6 4.8 %collective-permute-done.22.sz = bf16[128,1024]{1,0:T(8,128)(2,1)S(1)} collective-permute-done((bf16[128,1024]{1,0:T(8,128)(2,1)S(1)}, bf16[128,1024]{1,0:T(8,128)(2,1)S(1)}, u32[]{:S(2)}, u32[]{:S(2)}) %collective-permute-start.22) | collective-permute-done | bytes 262176 | tf_op jit(solution)/shard_map/ppermute | solution.py:48
  125.4 2.1 collective-permute-start.41
  129.0 2.3 collective-permute-done.23.u2
  132.9 3.0 collective-permute-start.32
  136.0 11.0 %shard_map.237 = (bf16[512,1024]{1,0:T(8,128)(2,1)S(1)}, bf16[512,1024]{1,0:T(8,128)(2,1)S(1)}, bf16[512,1792]{1,0:T(8,128)(2,1)S(1)}, bf16[256,1024]{1,0:T(8,12...) custom-call(s32[8]{0:T(128)S(1)} %stack.37.place, bf16[128,1024]{1,0:T(8,128)(2,1)S(1)} %get-tuple-element.227.u0.up, ...), custom_call_target="tpu_custom_call" | custom-call | flops 1 | bytes 1 | tf_op jit(solution)/shard_map/pallas_call | solution.py:77
  147.0 2.5 shard_map.240
  151.1 2.1 collective-permute-start.29
  157.4 2.8 shard_map.243
  160.2 4.3 %collective-permute-done.42.g0 = bf16[256,768]{1,0:T(8,128)(2,1)S(1)} collective-permute-done((bf16[256,768]{1,0:T(8,128)(2,1)S(1)}, bf16[256,768]{1,0:T(8,128)(2,1)S(1)}, u32[]{:S(2)}, u32[]{:S(2)}) %collective-permute-start.42) | collective-permute-done | bytes 393248 | tf_op jit(solution)/shard_map/ppermute | solution.py:48
  167.2 2.8 collective-permute-done.28.ga
  170.1 2.7 collective-permute-start.45
  173.8 3.6 %collective-permute-done.43.g1 = bf16[256,768]{1,0:T(8,128)(2,1)S(1)} collective-permute-done((bf16[256,768]{1,0:T(8,128)(2,1)S(1)}, bf16[256,768]{1,0:T(8,128)(2,1)S(1)}, u32[]{:S(2)}, u32[]{:S(2)}) %collective-permute-start.43) | collective-permute-done | bytes 393248 | tf_op jit(solution)/shard_map/ppermute | solution.py:48
  177.4 2.8 collective-permute-done.45.g3
  181.1 2.8 collective-permute-start.46
  184.1 1.9 collective-permute-start.30
  188.0 2.5 collective-permute-done.46.ga
  190.5 2.8 collective-permute-start.37
  193.3 2.6 collective-permute-done.47.gb
  197.1 5.2 %collective-permute-done.27.sz = bf16[128,1024]{1,0:T(8,128)(2,1)S(1)} collective-permute-done((bf16[128,1024]{1,0:T(8,128)(2,1)S(1)}, bf16[128,1024]{1,0:T(8,128)(2,1)S(1)}, u32[]{:S(2)}, u32[]{:S(2)}) %collective-permute-start.27) | collective-permute-done | bytes 262176 | tf_op jit(solution)/shard_map/ppermute | solution.py:48
  203.4 2.0 shard_map.238
  209.8 3.0 collective-permute-start.52
  214.0 2.0 collective-permute-done.38.ga
  216.8 2.8 collective-permute-done.50.refs_2_
  223.4 2.0 collective-permute-start.57
  225.6 6.4 %collective-permute-done.57.refs_1_ = bf16[64,1536]{1,0:T(8,128)(2,1)S(1)} collective-permute-done((bf16[64,1536]{1,0:T(8,128)(2,1)}, bf16[64,1536]{1,0:T(8,128)(2,1)S(1)}, u32[]{:S(2)}, u32[]{:S(2)}) %collective-permute-start.57) | collective-permute-done | bytes 196640 | tf_op jit(solution)/shard_map/ppermute | solution.py:48
  235.3 2.0 collective-permute-start.60
  240.6 6.7 %collective-permute-done.60.refs_3_ = bf16[32,2304]{1,0:T(8,128)(2,1)S(1)} collective-permute-done((bf16[32,2304]{1,0:T(8,128)(2,1)S(1)}, bf16[32,2304]{1,0:T(8,128)(2,1)S(1)}, u32[]{:S(2)}, u32[]{:S(2)}) %collective-permute-start.60) | collective-permute-done | bytes 147488 | tf_op jit(solution)/shard_map/ppermute | solution.py:48
  247.2 2.2 collective-permute-done.61.refs_4_
  254.5 3.1 collective-permute-done.54.refs_2_
  258.6 2.1 shard_map.252
  260.8 4.8 %collective-permute-done.64.gb = bf16[64,1536]{1,0:T(8,128)(2,1)} collective-permute-done((bf16[64,1536]{1,0:T(8,128)(2,1)}, bf16[64,1536]{1,0:T(8,128)(2,1)}, u32[]{:S(2)}, u32[]{:S(2)}) %collective-permute-start.64) | collective-permute-done | bytes 196640 | tf_op jit(solution)/shard_map/ppermute | solution.py:48
  269.1 3.5 %collective-permute-done.56 = f32[1,6]{1,0:T(1,128)S(1)} collective-permute-done((f32[1,6]{1,0:T(1,128)S(1)}, f32[1,6]{1,0:T(1,128)S(1)}, u32[]{:S(2)}, u32[]{:S(2)}) %collective-permute-start.56) | collective-permute-done | bytes 56 | tf_op jit(solution)/shard_map/ppermute | solution.py:48
  273.2 13.8 %collective-permute-done.66.gb = bf16[128,1536]{1,0:T(8,128)(2,1)S(1)} collective-permute-done((bf16[128,1536]{1,0:T(8,128)(2,1)S(1)}, bf16[128,1536]{1,0:T(8,128)(2,1)S(1)}, u32[]{:S(2)}, u32[]{:S(2)}) %collective-permute-start.66) | collective-permute-done | bytes 393248 | tf_op jit(solution)/shard_map/ppermute | solution.py:48
  287.0 3.1 collective-permute-done.65.ga
  290.9 2.8 collective-permute-start.69
  293.9 5.2 %collective-permute-done.68.g1 = bf16[256,768]{1,0:T(8,128)(2,1)S(1)} collective-permute-done((bf16[256,768]{1,0:T(8,128)(2,1)S(1)}, bf16[256,768]{1,0:T(8,128)(2,1)S(1)}, u32[]{:S(2)}, u32[]{:S(2)}) %collective-permute-start.68) | collective-permute-done | bytes 393248 | tf_op jit(solution)/shard_map/ppermute | solution.py:48
  300.4 2.3 collective-permute-done.70.g3
  302.7 1.7 shard_map.258
  307.1 2.2 collective-permute-start.74
  309.3 2.8 copy-done.8
  312.1 5.6 %shard_map.260 = (f32[2,256,3072]{2,1,0:T(8,128)}, f32[2,256,1024]{2,1,0:T(8,128)}, f32[2,256,4096]{2,1,0:T(8,128)}, f32[2,1024,1024]{2,1,0:T(8,128)}) custom-call(bf16[2048,1536]{1,0:T(8,128)(2,1)S(1)} %copy-done.8), custom_call_target="tpu_custom_call" | custom-call | flops 1 | bytes 1 | tf_op jit(solution)/shard_map/pallas_call | solution.py:77
  317.8 4.1 %shard_map.261 = (f32[2,256,3072]{2,1,0:T(8,128)}, f32[2,256,1024]{2,1,0:T(8,128)}, f32[2,256,4096]{2,1,0:T(8,128)}, f32[2,1024,1024]{2,1,0:T(8,128)}) custom-call(s32[8]{0:T(128)S(1)} %stack.37.place, bf16[544,768]{1,0:T(8,128)(2,1)S(1)} %get-tuple-element.326.p0.refs_0_, ...), custom_call_target="tpu_custom_call", output_to_operand_aliasing={{0}: (5, {}), {1}: (6, {}), {2}: (7, {}), {3}: (8, {})} | custom-call | flops 1 | bytes 1 | tf_op jit(solution)/shard_map/pallas_call | solution.py:77
  325.3 5.2 %shard_map.262 = (f32[2,256,3072]{2,1,0:T(8,128)}, f32[2,256,1024]{2,1,0:T(8,128)}, f32[2,256,4096]{2,1,0:T(8,128)}, f32[2,1024,1024]{2,1,0:T(8,128)}, f32[2,256...) custom-call(s32[8]{0:T(128)S(1)} %stack.37.place, ...), custom_call_target="tpu_custom_call", output_to_operand_aliasing={{0}: (6, {}), {1}: (7, {}), {2}: (8, {}), {3}: (9, {})} | custom-call | flops 1 | bytes 1 | tf_op jit(solution)/shard_map/pallas_call | solution.py:77
  (232 shorter events, 74.4 us)
Async XLA Ops:
  7.2 302.2 %all-gather.2.cloned.1.call-start = ((), (), s32[]{:S(2)}) async-start(), calls=%async_computation | async-start | bytes 6684672 | tf_op jit(solution)/shard_map/all_gather | solution.py:880
  15.1 14.0 %collective-permute-start.5 = (bf16[272,768]{1,0:T(8,128)(2,1)}, bf16[272,768]{1,0:T(8,128)(2,1)}, u32[]{:S(2)}, u32[]{:S(2)}) collective-permute-start(bf16[272,768]{1,0:T(8,128)(2,1)} %get-tuple-element.187), channel_id=1, source_target_pairs={{0,19},{1,18},{2,17},{3,16},{4,23},{5,22},{6,21},{7,20},{8,27},{9,... | collective-permute-start | bytes 1253384 | tf_op jit(solution)/shard_map/ppermute | solution.py:48
  19.5 9.5 %collective-permute-start.1 = (bf16[128,1024]{1,0:T(8,128)(2,1)}, bf16[128,1024]{1,0:T(8,128)(2,1)}, u32[]{:S(2)}, u32[]{:S(2)}) collective-permute-start(bf16[128,1024]{1,0:T(8,128)(2,1)} %state.3), channel_id=1, source_target_pairs={{0,2},{1,3},{2,0},{3,1},{4,6},{5,7},{6,4},{7,5},{8,10},{9,11},{10,... | collective-permute-start | bytes 786440 | tf_op jit(solution)/shard_map/ppermute | solution.py:48
  19.5 28.5 %collective-permute-start.3 = (bf16[272,768]{1,0:T(8,128)(2,1)}, bf16[272,768]{1,0:T(8,128)(2,1)}, u32[]{:S(2)}, u32[]{:S(2)}) collective-permute-start(bf16[272,768]{1,0:T(8,128)(2,1)} %get-tuple-element.185), channel_id=1, source_target_pairs={{0,1},{1,0},{2,3},{3,2},{4,5},{5,4},{6,7},{7,6},{8,9},{9,8},{10,11... | collective-permute-start | bytes 1253384 | tf_op jit(solution)/shard_map/ppermute | solution.py:48
  19.5 28.8 %collective-permute-start.4 = (bf16[272,768]{1,0:T(8,128)(2,1)}, bf16[272,768]{1,0:T(8,128)(2,1)}, u32[]{:S(2)}, u32[]{:S(2)}) collective-permute-start(bf16[272,768]{1,0:T(8,128)(2,1)} %get-tuple-element.186), channel_id=1, source_target_pairs={{0,2},{1,3},{2,0},{3,1},{4,6},{5,7},{6,4},{7,5},{8,10},{9,11},{10,... | collective-permute-start | bytes 1253384 | tf_op jit(solution)/shard_map/ppermute | solution.py:48
  28.9 28.0 %collective-permute-start.6 = (bf16[384,1024]{1,0:T(8,128)(2,1)S(1)}, bf16[384,1024]{1,0:T(8,128)(2,1)S(1)}, u32[]{:S(2)}, u32[]{:S(2)}) collective-permute-start(bf16[384,1024]{1,0:T(8,128)(2,1)S(1)} %get-tuple-element.193), channel_id=1, source_target_pairs={{0,2},{1,3},{2,0},{3,1},{4,6},{5,7},{6,4},{7,5},{8,10},{9,11},{10,... | collective-permute-start | bytes 2359304 | tf_op jit(solution)/shard_map/ppermute | solution.py:48
  29.1 15.4 %collective-permute-start.10 = (bf16[256,1024]{1,0:T(8,128)(2,1)S(1)}, bf16[256,1024]{1,0:T(8,128)(2,1)S(1)}, u32[]{:S(2)}, u32[]{:S(2)}) collective-permute-start(bf16[256,1024]{1,0:T(8,128)(2,1)S(1)} %get-tuple-element.199), channel_id=1, source_target_pairs={{0,19},{1,18},{2,17},{3,16},{4,23},{5,22},{6,21},{7,20},{8,27},{9,... | collective-permute-start | bytes 1572872 | tf_op jit(solution)/shard_map/ppermute | solution.py:48
  32.5 24.4 %collective-permute-start.9 = (bf16[256,1024]{1,0:T(8,128)(2,1)S(1)}, bf16[256,1024]{1,0:T(8,128)(2,1)S(1)}, u32[]{:S(2)}, u32[]{:S(2)}) collective-permute-start(bf16[256,1024]{1,0:T(8,128)(2,1)S(1)} %get-tuple-element.197), channel_id=1, source_target_pairs={{0,1},{1,0},{2,3},{3,2},{4,5},{5,4},{6,7},{7,6},{8,9},{9,8},{10,11... | collective-permute-start | bytes 1572872 | tf_op jit(solution)/shard_map/ppermute | solution.py:48
  44.5 43.7 %collective-permute-start.19 = (bf16[512,1792]{1,0:T(8,128)(2,1)S(1)}, bf16[512,1792]{1,0:T(8,128)(2,1)S(1)}, u32[]{:S(2)}, u32[]{:S(2)}) collective-permute-start(bf16[512,1792]{1,0:T(8,128)(2,1)S(1)} %get-tuple-element.209), channel_id=1, source_target_pairs={{0,18},{1,19},{2,16},{3,17},{4,22},{5,23},{6,20},{7,21},{8,26},{9,... | collective-permute-start | bytes 5505032 | tf_op jit(solution)/shard_map/ppermute | solution.py:48
  62.5 9.2 %collective-permute-start.12 = (bf16[128,1024]{1,0:T(8,128)(2,1)S(1)}, bf16[128,1024]{1,0:T(8,128)(2,1)S(1)}, u32[]{:S(2)}, u32[]{:S(2)}) collective-permute-start(bf16[128,1024]{1,0:T(8,128)(2,1)S(1)} %add_convert_fusion.2), channel_id=1, source_target_pairs={{0,2},{1,3},{2,0},{3,1},{4,6},{5,7},{6,4},{7,5},{8,10},{9,11},{10,... | collective-permute-start | bytes 786440 | tf_op jit(solution)/shard_map/ppermute | solution.py:48
  63.3 13.3 %collective-permute-start.8 = (bf16[128,1024]{1,0:T(8,128)(2,1)S(1)}, bf16[128,1024]{1,0:T(8,128)(2,1)S(1)}, u32[]{:S(2)}, u32[]{:S(2)}) collective-permute-start(bf16[128,1024]{1,0:T(8,128)(2,1)S(1)} %add_convert_fusion.3), channel_id=1, source_target_pairs={{0,2},{1,3},{2,0},{3,1},{4,6},{5,7},{6,4},{7,5},{8,10},{9,11},{10,... | collective-permute-start | bytes 786440 | tf_op jit(solution)/shard_map/ppermute | solution.py:48
  77.7 7.6 %collective-permute-start.14 = (bf16[128,1024]{1,0:T(8,128)(2,1)S(1)}, bf16[128,1024]{1,0:T(8,128)(2,1)S(1)}, u32[]{:S(2)}, u32[]{:S(2)}) collective-permute-start(bf16[128,1024]{1,0:T(8,128)(2,1)S(1)} %get-tuple-element.203.n0), channel_id=1, source_target_pairs={{0,2},{1,3},{2,0},{3,1},{4,6},{5,7},{6,4},{7,5},{8,10},{9,11},{10,... | collective-permute-start | bytes 786440 | tf_op jit(solution)/shard_map/ppermute | solution.py:48
  78.1 13.8 %collective-permute-start.18 = (bf16[256,1792]{1,0:T(8,128)(2,1)S(1)}, bf16[256,1792]{1,0:T(8,128)(2,1)S(1)}, u32[]{:S(2)}, u32[]{:S(2)}) collective-permute-start(bf16[256,1792]{1,0:T(8,128)(2,1)S(1)} %get-tuple-element.208), channel_id=1, source_target_pairs={{0,1},{1,0},{2,3},{3,2},{4,5},{5,4},{6,7},{7,6},{8,9},{9,8},{10,11... | collective-permute-start | bytes 2752520 | tf_op jit(solution)/shard_map/ppermute | solution.py:48
  88.3 5.0 %collective-permute-start.20 = (bf16[256,1792]{1,0:T(8,128)(2,1)S(1)}, bf16[256,1792]{1,0:T(8,128)(2,1)S(1)}, u32[]{:S(2)}, u32[]{:S(2)}) collective-permute-start(bf16[256,1792]{1,0:T(8,128)(2,1)S(1)} %slice.47), channel_id=1, source_target_pairs={{0,1},{1,0},{2,3},{3,2},{4,5},{5,4},{6,7},{7,6},{8,9},{9,8},{10,11... | collective-permute-start | bytes 2752520 | tf_op jit(solution)/shard_map/ppermute | solution.py:48
  109.8 3.9 %collective-permute-start.21 = (bf16[256,1024]{1,0:T(8,128)(2,1)S(1)}, bf16[256,1024]{1,0:T(8,128)(2,1)S(1)}, u32[]{:S(2)}, u32[]{:S(2)}) collective-permute-start(bf16[256,1024]{1,0:T(8,128)(2,1)S(1)} %get-tuple-element.214), channel_id=1, source_target_pairs={{0,1},{1,0},{2,3},{3,2},{4,5},{5,4},{6,7},{7,6},{8,9},{9,8},{10,11... | collective-permute-start | bytes 1572872 | tf_op jit(solution)/shard_map/ppermute | solution.py:48
  113.7 8.7 %collective-permute-start.22 = (bf16[128,1024]{1,0:T(8,128)(2,1)S(1)}, bf16[128,1024]{1,0:T(8,128)(2,1)S(1)}, u32[]{:S(2)}, u32[]{:S(2)}) collective-permute-start(bf16[128,1024]{1,0:T(8,128)(2,1)S(1)} %add_convert_fusion.1), channel_id=1, source_target_pairs={{0,2},{1,3},{2,0},{3,1},{4,6},{5,7},{6,4},{7,5},{8,10},{9,11},{10,... | collective-permute-start | bytes 786440 | tf_op jit(solution)/shard_map/ppermute | solution.py:48
  123.5 7.9 %collective-permute-start.23 = (bf16[128,1024]{1,0:T(8,128)(2,1)S(1)}, bf16[128,1024]{1,0:T(8,128)(2,1)S(1)}, u32[]{:S(2)}, u32[]{:S(2)}) collective-permute-start(bf16[128,1024]{1,0:T(8,128)(2,1)S(1)} %get-tuple-element.227.u0.up), channel_id=1, source_target_pairs={{0,2},{1,3},{2,0},{3,1},{4,6},{5,7},{6,4},{7,5},{8,10},{9,11},{10,... | collective-permute-start | bytes 786440 | tf_op jit(solution)/shard_map/ppermute | solution.py:48
  123.9 27.2 %collective-permute-start.40 = (bf16[512,768]{1,0:T(8,128)(2,1)}, bf16[512,768]{1,0:T(8,128)(2,1)S(1)}, u32[]{:S(2)}, u32[]{:S(2)}) collective-permute-start(bf16[512,768]{1,0:T(8,128)(2,1)} %get-tuple-element.277), channel_id=1, source_target_pairs={{0,32},{1,33},{2,34},{3,35},{4,36},{5,37},{6,38},{7,39},{8,40},{9,... | collective-permute-start | bytes 2359304 | tf_op jit(solution)/shard_map/ppermute | solution.py:48
  125.4 27.9 %collective-permute-start.41 = (bf16[512,768]{1,0:T(8,128)(2,1)}, bf16[512,768]{1,0:T(8,128)(2,1)S(1)}, u32[]{:S(2)}, u32[]{:S(2)}) collective-permute-start(bf16[512,768]{1,0:T(8,128)(2,1)} %get-tuple-element.279), channel_id=1, source_target_pairs={{0,96},{1,97},{2,98},{3,99},{4,100},{5,101},{6,102},{7,103},{8,104... | collective-permute-start | bytes 2359304 | tf_op jit(solution)/shard_map/ppermute | solution.py:48
  127.5 26.9 %collective-permute-start.31 = (bf16[512,768]{1,0:T(8,128)(2,1)}, bf16[512,768]{1,0:T(8,128)(2,1)S(1)}, u32[]{:S(2)}, u32[]{:S(2)}) collective-permute-start(bf16[512,768]{1,0:T(8,128)(2,1)} %get-tuple-element.249), channel_id=1, source_target_pairs={{0,4},{1,5},{2,6},{3,7},{4,0},{5,1},{6,2},{7,3},{8,12},{9,13},{10,... | collective-permute-start | bytes 2359304 | tf_op jit(solution)/shard_map/ppermute | solution.py:48
  131.4 4.5 %collective-permute-start.25 = (bf16[128,1024]{1,0:T(8,128)(2,1)S(1)}, bf16[128,1024]{1,0:T(8,128)(2,1)S(1)}, u32[]{:S(2)}, u32[]{:S(2)}) collective-permute-start(bf16[128,1024]{1,0:T(8,128)(2,1)S(1)} %collective-permute-done.23.u2), channel_id=1, source_target_pairs={{0,1},{1,0},{2,3},{3,2},{4,5},{5,4},{6,7},{7,6},{8,9},{9,8},{10,11... | collective-permute-start | bytes 786440 | tf_op jit(solution)/shard_map/ppermute | solution.py:48
  132.9 22.9 %collective-permute-start.32 = (bf16[512,768]{1,0:T(8,128)(2,1)}, bf16[512,768]{1,0:T(8,128)(2,1)S(1)}, u32[]{:S(2)}, u32[]{:S(2)}) collective-permute-start(bf16[512,768]{1,0:T(8,128)(2,1)} %get-tuple-element.251), channel_id=1, source_target_pairs={{0,12},{1,13},{2,14},{3,15},{4,8},{5,9},{6,10},{7,11},{8,4},{9,5},... | collective-permute-start | bytes 2359304 | tf_op jit(solution)/shard_map/ppermute | solution.py:48
  149.6 20.5 %collective-permute-start.28 = (bf16[512,768]{1,0:T(8,128)(2,1)S(1)}, bf16[512,768]{1,0:T(8,128)(2,1)S(1)}, u32[]{:S(2)}, u32[]{:S(2)}) collective-permute-start(bf16[512,768]{1,0:T(8,128)(2,1)S(1)} %get-tuple-element.241), channel_id=1, source_target_pairs={{0,32},{1,33},{2,34},{3,35},{4,36},{5,37},{6,38},{7,39},{8,40},{9,... | collective-permute-start | bytes 2359304 | tf_op jit(solution)/shard_map/ppermute | solution.py:48
  151.1 21.7 %collective-permute-start.29 = (bf16[512,768]{1,0:T(8,128)(2,1)S(1)}, bf16[512,768]{1,0:T(8,128)(2,1)S(1)}, u32[]{:S(2)}, u32[]{:S(2)}) collective-permute-start(bf16[512,768]{1,0:T(8,128)(2,1)S(1)} %get-tuple-element.243), channel_id=1, source_target_pairs={{0,96},{1,97},{2,98},{3,99},{4,100},{5,101},{6,102},{7,103},{8,104... | collective-permute-start | bytes 2359304 | tf_op jit(solution)/shard_map/ppermute | solution.py:48
  154.1 10.4 %collective-permute-start.42 = (bf16[256,768]{1,0:T(8,128)(2,1)S(1)}, bf16[256,768]{1,0:T(8,128)(2,1)S(1)}, u32[]{:S(2)}, u32[]{:S(2)}) collective-permute-start(bf16[256,768]{1,0:T(8,128)(2,1)S(1)} %get-tuple-element.281), channel_id=1, source_target_pairs={{0,4},{1,5},{2,6},{3,7},{4,0},{5,1},{6,2},{7,3},{8,12},{9,13},{10,... | collective-permute-start | bytes 1179656 | tf_op jit(solution)/shard_map/ppermute | solution.py:48
  154.4 11.9 %collective-permute-start.44 = (bf16[256,768]{1,0:T(8,128)(2,1)S(1)}, bf16[256,768]{1,0:T(8,128)(2,1)S(1)}, u32[]{:S(2)}, u32[]{:S(2)}) collective-permute-start(bf16[256,768]{1,0:T(8,128)(2,1)S(1)} %get-tuple-element.284), channel_id=1, source_target_pairs={{0,12},{1,13},{2,14},{3,15},{4,8},{5,9},{6,10},{7,11},{8,4},{9,5},... | collective-permute-start | bytes 1179656 | tf_op jit(solution)/shard_map/ppermute | solution.py:48
  156.7 20.6 %collective-permute-start.43 = (bf16[256,768]{1,0:T(8,128)(2,1)S(1)}, bf16[256,768]{1,0:T(8,128)(2,1)S(1)}, u32[]{:S(2)}, u32[]{:S(2)}) collective-permute-start(bf16[256,768]{1,0:T(8,128)(2,1)S(1)} %get-tuple-element.252), channel_id=1, source_target_pairs={{0,32},{1,33},{2,34},{3,35},{4,36},{5,37},{6,38},{7,39},{8,40},{9,... | collective-permute-start | bytes 1179656 | tf_op jit(solution)/shard_map/ppermute | solution.py:48
  164.5 19.6 %collective-permute-start.33 = (bf16[512,768]{1,0:T(8,128)(2,1)S(1)}, bf16[512,768]{1,0:T(8,128)(2,1)S(1)}, u32[]{:S(2)}, u32[]{:S(2)}) collective-permute-start(bf16[512,768]{1,0:T(8,128)(2,1)S(1)} %get-tuple-element.256), channel_id=1, source_target_pairs={{0,4},{1,5},{2,6},{3,7},{4,0},{5,1},{6,2},{7,3},{8,12},{9,13},{10,... | collective-permute-start | bytes 2359304 | tf_op jit(solution)/shard_map/ppermute | solution.py:48
  166.3 19.7 %collective-permute-start.34 = (bf16[512,768]{1,0:T(8,128)(2,1)S(1)}, bf16[512,768]{1,0:T(8,128)(2,1)S(1)}, u32[]{:S(2)}, u32[]{:S(2)}) collective-permute-start(bf16[512,768]{1,0:T(8,128)(2,1)S(1)} %get-tuple-element.258), channel_id=1, source_target_pairs={{0,12},{1,13},{2,14},{3,15},{4,8},{5,9},{6,10},{7,11},{8,4},{9,5},... | collective-permute-start | bytes 2359304 | tf_op jit(solution)/shard_map/ppermute | solution.py:48
  170.1 10.1 %collective-permute-start.45 = (bf16[256,768]{1,0:T(8,128)(2,1)S(1)}, bf16[256,768]{1,0:T(8,128)(2,1)S(1)}, u32[]{:S(2)}, u32[]{:S(2)}) collective-permute-start(bf16[256,768]{1,0:T(8,128)(2,1)S(1)} %get-tuple-element.286), channel_id=1, source_target_pairs={{0,96},{1,97},{2,98},{3,99},{4,100},{5,101},{6,102},{7,103},{8,104... | collective-permute-start | bytes 1179656 | tf_op jit(solution)/shard_map/ppermute | solution.py:48
  172.8 15.1 %collective-permute-start.26 = (bf16[256,1024]{1,0:T(8,128)(2,1)S(1)}, bf16[256,1024]{1,0:T(8,128)(2,1)S(1)}, u32[]{:S(2)}, u32[]{:S(2)}) collective-permute-start(bf16[256,1024]{1,0:T(8,128)(2,1)S(1)} %get-tuple-element.231), channel_id=1, source_target_pairs={{0,1},{1,0},{2,3},{3,2},{4,5},{5,4},{6,7},{7,6},{8,9},{9,8},{10,11... | collective-permute-start | bytes 1572872 | tf_op jit(solution)/shard_map/ppermute | solution.py:48
  181.1 9.4 %collective-permute-start.46 = (bf16[128,1536]{1,0:T(8,128)(2,1)S(1)}, bf16[128,1536]{1,0:T(8,128)(2,1)S(1)}, u32[]{:S(2)}, u32[]{:S(2)}) collective-permute-start(bf16[128,1536]{1,0:T(8,128)(2,1)S(1)} %get-tuple-element.288), channel_id=1, source_target_pairs={{0,96},{1,97},{2,98},{3,99},{4,100},{5,101},{6,102},{7,103},{8,104... | collective-permute-start | bytes 1179656 | tf_op jit(solution)/shard_map/ppermute | solution.py:48
  183.9 11.9 %collective-permute-start.47 = (bf16[128,1536]{1,0:T(8,128)(2,1)S(1)}, bf16[128,1536]{1,0:T(8,128)(2,1)S(1)}, u32[]{:S(2)}, u32[]{:S(2)}) collective-permute-start(bf16[128,1536]{1,0:T(8,128)(2,1)S(1)} %get-tuple-element.290), channel_id=1, source_target_pairs={{0,4},{1,5},{2,6},{3,7},{4,0},{5,1},{6,2},{7,3},{8,12},{9,13},{10,... | collective-permute-start | bytes 1179656 | tf_op jit(solution)/shard_map/ppermute | solution.py:48
  184.1 19.2 %collective-permute-start.30 = (bf16[256,768]{1,0:T(8,128)(2,1)S(1)}, bf16[256,768]{1,0:T(8,128)(2,1)S(1)}, u32[]{:S(2)}, u32[]{:S(2)}) collective-permute-start(bf16[256,768]{1,0:T(8,128)(2,1)S(1)} %get-tuple-element.245), channel_id=1, source_target_pairs={{0,4},{1,5},{2,6},{3,7},{4,0},{5,1},{6,2},{7,3},{8,12},{9,13},{10,... | collective-permute-start | bytes 1179656 | tf_op jit(solution)/shard_map/ppermute | solution.py:48
  186.0 19.9 %collective-permute-start.36 = (bf16[256,768]{1,0:T(8,128)(2,1)S(1)}, bf16[256,768]{1,0:T(8,128)(2,1)S(1)}, u32[]{:S(2)}, u32[]{:S(2)}) collective-permute-start(bf16[256,768]{1,0:T(8,128)(2,1)S(1)} %get-tuple-element.262), channel_id=1, source_target_pairs={{0,12},{1,13},{2,14},{3,15},{4,8},{5,9},{6,10},{7,11},{8,4},{9,5},... | collective-permute-start | bytes 1179656 | tf_op jit(solution)/shard_map/ppermute | solution.py:48
  187.9 18.0 %collective-permute-start.35 = (bf16[256,768]{1,0:T(8,128)(2,1)S(1)}, bf16[256,768]{1,0:T(8,128)(2,1)S(1)}, u32[]{:S(2)}, u32[]{:S(2)}) collective-permute-start(bf16[256,768]{1,0:T(8,128)(2,1)S(1)} %get-tuple-element.260), channel_id=1, source_target_pairs={{0,32},{1,33},{2,34},{3,35},{4,36},{5,37},{6,38},{7,39},{8,40},{9,... | collective-permute-start | bytes 1179656 | tf_op jit(solution)/shard_map/ppermute | solution.py:48
  190.5 15.5 %collective-permute-start.37 = (bf16[256,768]{1,0:T(8,128)(2,1)S(1)}, bf16[256,768]{1,0:T(8,128)(2,1)S(1)}, u32[]{:S(2)}, u32[]{:S(2)}) collective-permute-start(bf16[256,768]{1,0:T(8,128)(2,1)S(1)} %get-tuple-element.264), channel_id=1, source_target_pairs={{0,96},{1,97},{2,98},{3,99},{4,100},{5,101},{6,102},{7,103},{8,104... | collective-permute-start | bytes 1179656 | tf_op jit(solution)/shard_map/ppermute | solution.py:48
  195.8 6.4 %collective-permute-start.27 = (bf16[128,1024]{1,0:T(8,128)(2,1)S(1)}, bf16[128,1024]{1,0:T(8,128)(2,1)S(1)}, u32[]{:S(2)}, u32[]{:S(2)}) collective-permute-start(bf16[128,1024]{1,0:T(8,128)(2,1)S(1)} %add_convert_fusion), channel_id=1, source_target_pairs={{0,2},{1,3},{2,0},{3,1},{4,6},{5,7},{6,4},{7,5},{8,10},{9,11},{10,... | collective-permute-start | bytes 786440 | tf_op jit(solution)/shard_map/ppermute | solution.py:48
  202.2 6.9 %collective-permute-start.48 = (bf16[64,1536]{1,0:T(8,128)(2,1)S(1)}, bf16[64,1536]{1,0:T(8,128)(2,1)S(1)}, u32[]{:S(2)}, u32[]{:S(2)}) collective-permute-start(bf16[64,1536]{1,0:T(8,128)(2,1)S(1)} %get-tuple-element.292), channel_id=1, source_target_pairs={{0,12},{1,13},{2,14},{3,15},{4,8},{5,9},{6,10},{7,11},{8,4},{9,5},... | collective-permute-start | bytes 589832 | tf_op jit(solution)/shard_map/ppermute | solution.py:48
  203.4 5.7 %collective-permute-start.49 = (bf16[64,1536]{1,0:T(8,128)(2,1)S(1)}, bf16[64,1536]{1,0:T(8,128)(2,1)S(1)}, u32[]{:S(2)}, u32[]{:S(2)}) collective-permute-start(bf16[64,1536]{1,0:T(8,128)(2,1)S(1)} %get-tuple-element.294), channel_id=1, source_target_pairs={{0,32},{1,33},{2,34},{3,35},{4,36},{5,37},{6,38},{7,39},{8,40},{9,... | collective-permute-start | bytes 589832 | tf_op jit(solution)/shard_map/ppermute | solution.py:48
  206.9 9.1 %collective-permute-start.38 = (bf16[128,1536]{1,0:T(8,128)(2,1)S(1)}, bf16[128,1536]{1,0:T(8,128)(2,1)S(1)}, u32[]{:S(2)}, u32[]{:S(2)}) collective-permute-start(bf16[128,1536]{1,0:T(8,128)(2,1)S(1)} %get-tuple-element.266), channel_id=1, source_target_pairs={{0,96},{1,97},{2,98},{3,99},{4,100},{5,101},{6,102},{7,103},{8,104... | collective-permute-start | bytes 1179656 | tf_op jit(solution)/shard_map/ppermute | solution.py:48
  207.4 8.5 %collective-permute-start.39 = (bf16[128,1536]{1,0:T(8,128)(2,1)S(1)}, bf16[128,1536]{1,0:T(8,128)(2,1)S(1)}, u32[]{:S(2)}, u32[]{:S(2)}) collective-permute-start(bf16[128,1536]{1,0:T(8,128)(2,1)S(1)} %get-tuple-element.268), channel_id=1, source_target_pairs={{0,4},{1,5},{2,6},{3,7},{4,0},{5,1},{6,2},{7,3},{8,12},{9,13},{10,... | collective-permute-start | bytes 1179656 | tf_op jit(solution)/shard_map/ppermute | solution.py:48
  209.8 10.0 %collective-permute-start.52 = (bf16[32,4352]{1,0:T(8,128)(2,1)S(1)}, bf16[32,4352]{1,0:T(8,128)(2,1)S(1)}, u32[]{:S(2)}, u32[]{:S(2)}) collective-permute-start(bf16[32,4352]{1,0:T(8,128)(2,1)S(1)} %get-tuple-element.298), channel_id=1, source_target_pairs={{0,16},{1,17},{2,18},{3,19},{4,20},{5,21},{6,22},{7,23},{8,24},{9,... | collective-permute-start | bytes 835592 | tf_op jit(solution)/shard_map/ppermute | solution.py:48
  212.8 6.7 %collective-permute-start.50 = (bf16[32,1792]{1,0:T(8,128)(2,1)S(1)}, bf16[32,1792]{1,0:T(8,128)(2,1)S(1)}, u32[]{:S(2)}, u32[]{:S(2)}) collective-permute-start(bf16[32,1792]{1,0:T(8,128)(2,1)S(1)} %get-tuple-element.297), channel_id=1, source_target_pairs={{0,2},{1,3},{2,0},{3,1},{4,6},{5,7},{6,4},{7,5},{8,10},{9,11},{10,... | collective-permute-start | bytes 344072 | tf_op jit(solution)/shard_map/ppermute | solution.py:48
  213.8 6.0 %collective-permute-start.51 = (bf16[32,1792]{1,0:T(8,128)(2,1)S(1)}, bf16[32,1792]{1,0:T(8,128)(2,1)S(1)}, u32[]{:S(2)}, u32[]{:S(2)}) collective-permute-start(bf16[32,1792]{1,0:T(8,128)(2,1)S(1)} %get-tuple-element.297), channel_id=1, source_target_pairs={{0,18},{1,19},{2,16},{3,17},{4,22},{5,23},{6,20},{7,21},{8,26},{9,... | collective-permute-start | bytes 344072 | tf_op jit(solution)/shard_map/ppermute | solution.py:48
  223.2 15.4 %collective-permute-start.53 = (bf16[512,1024]{1,0:T(8,128)(2,1)}, bf16[512,1024]{1,0:T(8,128)(2,1)S(1)}, u32[]{:S(2)}, u32[]{:S(2)}) collective-permute-start(bf16[512,1024]{1,0:T(8,128)(2,1)} %copy-done.38), channel_id=1, source_target_pairs={{0,1},{1,0},{2,3},{3,2},{4,5},{5,4},{6,7},{7,6},{8,9},{9,8},{10,11... | collective-permute-start | bytes 3145736 | tf_op jit(solution)/shard_map/ppermute | solution.py:48
  223.4 8.6 %collective-permute-start.57 = (bf16[64,1536]{1,0:T(8,128)(2,1)}, bf16[64,1536]{1,0:T(8,128)(2,1)S(1)}, u32[]{:S(2)}, u32[]{:S(2)}) collective-permute-start(bf16[64,1536]{1,0:T(8,128)(2,1)} %copy-done.40), channel_id=1, source_target_pairs={{0,12},{1,13},{2,14},{3,15},{4,8},{5,9},{6,10},{7,11},{8,4},{9,5},... | collective-permute-start | bytes 589832 | tf_op jit(solution)/shard_map/ppermute | solution.py:48
  225.5 7.1 %collective-permute-start.58 = (bf16[64,1536]{1,0:T(8,128)(2,1)}, bf16[64,1536]{1,0:T(8,128)(2,1)S(1)}, u32[]{:S(2)}, u32[]{:S(2)}) collective-permute-start(bf16[64,1536]{1,0:T(8,128)(2,1)} %copy-done.39), channel_id=1, source_target_pairs={{0,32},{1,33},{2,34},{3,35},{4,36},{5,37},{6,38},{7,39},{8,40},{9,... | collective-permute-start | bytes 589832 | tf_op jit(solution)/shard_map/ppermute | solution.py:48
  234.2 6.4 %collective-permute-start.59 = (bf16[32,2304]{1,0:T(8,128)(2,1)S(1)}, bf16[32,2304]{1,0:T(8,128)(2,1)S(1)}, u32[]{:S(2)}, u32[]{:S(2)}) collective-permute-start(bf16[32,2304]{1,0:T(8,128)(2,1)S(1)} %get-tuple-element.312), channel_id=1, source_target_pairs={{0,2},{1,3},{2,0},{3,1},{4,6},{5,7},{6,4},{7,5},{8,10},{9,11},{10,... | collective-permute-start | bytes 442376 | tf_op jit(solution)/shard_map/ppermute | solution.py:48
  235.3 11.9 %collective-permute-start.60 = (bf16[32,2304]{1,0:T(8,128)(2,1)S(1)}, bf16[32,2304]{1,0:T(8,128)(2,1)S(1)}, u32[]{:S(2)}, u32[]{:S(2)}) collective-permute-start(bf16[32,2304]{1,0:T(8,128)(2,1)S(1)} %get-tuple-element.312), channel_id=1, source_target_pairs={{0,18},{1,19},{2,16},{3,17},{4,22},{5,23},{6,20},{7,21},{8,26},{9,... | collective-permute-start | bytes 442376 | tf_op jit(solution)/shard_map/ppermute | solution.py:48
  237.4 12.1 %collective-permute-start.61 = (bf16[32,4864]{1,0:T(8,128)(2,1)S(1)}, bf16[32,4864]{1,0:T(8,128)(2,1)S(1)}, u32[]{:S(2)}, u32[]{:S(2)}) collective-permute-start(bf16[32,4864]{1,0:T(8,128)(2,1)S(1)} %get-tuple-element.313), channel_id=1, source_target_pairs={{0,16},{1,17},{2,18},{3,19},{4,20},{5,21},{6,22},{7,23},{8,24},{9,... | collective-permute-start | bytes 933896 | tf_op jit(solution)/shard_map/ppermute | solution.py:48
  239.5 18.1 %collective-permute-start.54 = (bf16[256,1024]{1,0:T(8,128)(2,1)}, bf16[256,1024]{1,0:T(8,128)(2,1)}, u32[]{:S(2)}, u32[]{:S(2)}) collective-permute-start(bf16[256,1024]{1,0:T(8,128)(2,1)} %bitcast.9), channel_id=1, source_target_pairs={{0,2},{1,3},{2,0},{3,1},{4,6},{5,7},{6,4},{7,5},{8,10},{9,11},{10,... | collective-permute-start | bytes 1572872 | tf_op jit(solution)/shard_map/ppermute | solution.py:48
  252.9 13.3 %collective-permute-start.63 = (bf16[80,1536]{1,0:T(8,128)(2,1)S(1)}, bf16[80,1536]{1,0:T(8,128)(2,1)}, u32[]{:S(2)}, u32[]{:S(2)}) collective-permute-start(bf16[80,1536]{1,0:T(8,128)(2,1)S(1)} %get-tuple-element.318.oa), channel_id=1, source_target_pairs={{0,12},{1,13},{2,14},{3,15},{4,8},{5,9},{6,10},{7,11},{8,4},{9,5},... | collective-permute-start | bytes 737288 | tf_op jit(solution)/shard_map/ppermute | solution.py:48
  254.3 11.3 %collective-permute-start.64 = (bf16[64,1536]{1,0:T(8,128)(2,1)}, bf16[64,1536]{1,0:T(8,128)(2,1)}, u32[]{:S(2)}, u32[]{:S(2)}) collective-permute-start(bf16[64,1536]{1,0:T(8,128)(2,1)} %get-tuple-element.319.ob), channel_id=1, source_target_pairs={{0,32},{1,33},{2,34},{3,35},{4,36},{5,37},{6,38},{7,39},{8,40},{9,... | collective-permute-start | bytes 589832 | tf_op jit(solution)/shard_map/ppermute | solution.py:48
  267.4 22.7 %collective-permute-start.65 = (bf16[144,1536]{1,0:T(8,128)(2,1)S(1)}, bf16[144,1536]{1,0:T(8,128)(2,1)S(1)}, u32[]{:S(2)}, u32[]{:S(2)}) collective-permute-start(bf16[144,1536]{1,0:T(8,128)(2,1)S(1)} %get-tuple-element.320.oa), channel_id=1, source_target_pairs={{0,96},{1,97},{2,98},{3,99},{4,100},{5,101},{6,102},{7,103},{8,104... | collective-permute-start | bytes 1327112 | tf_op jit(solution)/shard_map/ppermute | solution.py:48
  267.7 19.3 %collective-permute-start.66 = (bf16[128,1536]{1,0:T(8,128)(2,1)S(1)}, bf16[128,1536]{1,0:T(8,128)(2,1)S(1)}, u32[]{:S(2)}, u32[]{:S(2)}) collective-permute-start(bf16[128,1536]{1,0:T(8,128)(2,1)S(1)} %get-tuple-element.321.ob), channel_id=1, source_target_pairs={{0,4},{1,5},{2,6},{3,7},{4,0},{5,1},{6,2},{7,3},{8,12},{9,13},{10,... | collective-permute-start | bytes 1179656 | tf_op jit(solution)/shard_map/ppermute | solution.py:48
  290.8 12.0 %collective-permute-start.67 = (bf16[288,768]{1,0:T(8,128)(2,1)S(1)}, bf16[288,768]{1,0:T(8,128)(2,1)S(1)}, u32[]{:S(2)}, u32[]{:S(2)}) collective-permute-start(bf16[288,768]{1,0:T(8,128)(2,1)S(1)} %get-tuple-element.322.o0), channel_id=1, source_target_pairs={{0,4},{1,5},{2,6},{3,7},{4,0},{5,1},{6,2},{7,3},{8,12},{9,13},{10,... | collective-permute-start | bytes 1327112 | tf_op jit(solution)/shard_map/ppermute | solution.py:48
  290.9 8.2 %collective-permute-start.68 = (bf16[256,768]{1,0:T(8,128)(2,1)S(1)}, bf16[256,768]{1,0:T(8,128)(2,1)S(1)}, u32[]{:S(2)}, u32[]{:S(2)}) collective-permute-start(bf16[256,768]{1,0:T(8,128)(2,1)S(1)} %get-tuple-element.323.o1), channel_id=1, source_target_pairs={{0,32},{1,33},{2,34},{3,35},{4,36},{5,37},{6,38},{7,39},{8,40},{9,... | collective-permute-start | bytes 1179656 | tf_op jit(solution)/shard_map/ppermute | solution.py:48
  290.9 9.4 %collective-permute-start.69 = (bf16[256,768]{1,0:T(8,128)(2,1)S(1)}, bf16[256,768]{1,0:T(8,128)(2,1)S(1)}, u32[]{:S(2)}, u32[]{:S(2)}) collective-permute-start(bf16[256,768]{1,0:T(8,128)(2,1)S(1)} %get-tuple-element.324.o2), channel_id=1, source_target_pairs={{0,12},{1,13},{2,14},{3,15},{4,8},{5,9},{6,10},{7,11},{8,4},{9,5},... | collective-permute-start | bytes 1179656 | tf_op jit(solution)/shard_map/ppermute | solution.py:48
  293.7 9.0 %collective-permute-start.70 = (bf16[256,768]{1,0:T(8,128)(2,1)S(1)}, bf16[256,768]{1,0:T(8,128)(2,1)S(1)}, u32[]{:S(2)}, u32[]{:S(2)}) collective-permute-start(bf16[256,768]{1,0:T(8,128)(2,1)S(1)} %get-tuple-element.325.o3), channel_id=1, source_target_pairs={{0,96},{1,97},{2,98},{3,99},{4,100},{5,101},{6,102},{7,103},{8,104... | collective-permute-start | bytes 1179656 | tf_op jit(solution)/shard_map/ppermute | solution.py:48
  304.4 20.8 %collective-permute-start.71 = (bf16[544,768]{1,0:T(8,128)(2,1)S(1)}, bf16[544,768]{1,0:T(8,128)(2,1)S(1)}, u32[]{:S(2)}, u32[]{:S(2)}) collective-permute-start(bf16[544,768]{1,0:T(8,128)(2,1)S(1)} %get-tuple-element.326.p0.refs_0_), channel_id=1, source_target_pairs={{0,32},{1,33},{2,34},{3,35},{4,36},{5,37},{6,38},{7,39},{8,40},{9,... | collective-permute-start | bytes 2506760 | tf_op jit(solution)/shard_map/ppermute | solution.py:48
  305.2 17.4 %collective-permute-start.72 = (bf16[512,768]{1,0:T(8,128)(2,1)}, bf16[512,768]{1,0:T(8,128)(2,1)}, u32[]{:S(2)}, u32[]{:S(2)}) collective-permute-start(bf16[512,768]{1,0:T(8,128)(2,1)} %get-tuple-element.327.p1), channel_id=1, source_target_pairs={{0,4},{1,5},{2,6},{3,7},{4,0},{5,1},{6,2},{7,3},{8,12},{9,13},{10,... | collective-permute-start | bytes 2359304 | tf_op jit(solution)/shard_map/ppermute | solution.py:48
  306.5 17.3 %collective-permute-start.73 = (bf16[512,768]{1,0:T(8,128)(2,1)S(1)}, bf16[512,768]{1,0:T(8,128)(2,1)}, u32[]{:S(2)}, u32[]{:S(2)}) collective-permute-start(bf16[512,768]{1,0:T(8,128)(2,1)S(1)} %get-tuple-element.328.p2), channel_id=1, source_target_pairs={{0,96},{1,97},{2,98},{3,99},{4,100},{5,101},{6,102},{7,103},{8,104... | collective-permute-start | bytes 2359304 | tf_op jit(solution)/shard_map/ppermute | solution.py:48
  307.1 18.2 %collective-permute-start.74 = (bf16[512,768]{1,0:T(8,128)(2,1)S(1)}, bf16[512,768]{1,0:T(8,128)(2,1)}, u32[]{:S(2)}, u32[]{:S(2)}) collective-permute-start(bf16[512,768]{1,0:T(8,128)(2,1)S(1)} %get-tuple-element.329.p3), channel_id=1, source_target_pairs={{0,12},{1,13},{2,14},{3,15},{4,8},{5,9},{6,10},{7,11},{8,4},{9,5},... | collective-permute-start | bytes 2359304 | tf_op jit(solution)/shard_map/ppermute | solution.py:48
  (54 other events, 492.2 us)
Sparse Core Ops, SparseCore 0:
  223.3 70.7 all-gather.1

commit v2 on v1

--- a/solution.py
+++ b/solution.py
@@ -363,7 +363,7 @@
 
 def last_layer(
     place, n0, n1, n2, n3, u0, u1, u2, u3, vec, turn, triple, merger, expander, shrinker, w1, w2, w3,
-    normed, up, act, ss, mixed, bsend, bkeep, send, keep, bias,
+    normed, up, act, ss, mixed, send, keep, bias,
     wide, merge, shrink, qkv, slopes, out, sems,
 ):
     shard, length = place[2], place[3]
@@ -382,14 +382,18 @@
         value, slope = gelu_both(part)
         act[:, cols] = value.astype(BF)
         ss[:, cols] = (dot_t(up[...], shrink[cols, :]) * slope).astype(BF)
-    hand_out(act, shrink, bsend.at[pl.ds(256, 256)], bkeep.at[pl.ds(256, 256)])
     allowed = (col <= row) & (col < length)
     heads_out(normed, wide, vec[pl.ds(9, 1), pl.ds(0, 768)], turn, qkv)
     out[...] = dot_t(up[...], merge[...]).astype(BF)
     attend_back(qkv, allowed, mixed, out, slopes, True)
-    hand_out(mixed, merge, bsend.at[pl.ds(0, 256)], bkeep.at[pl.ds(0, 256)])
     triple_slopes(slopes, turn, ss)
     slopes_out(ss, bias, wide, send, keep)
+
+
+def last_branches(act, mixed, merger, shrinker, send, keep, merge, shrink, sems):
+    finish(copies([(merger.at[1], merge), (shrinker.at[1], shrink)], sems))
+    hand_out(mixed, merge, send.at[pl.ds(0, 256)], keep.at[pl.ds(0, 256)])
+    hand_out(act, shrink, send.at[pl.ds(256, 256)], keep.at[pl.ds(256, 256)])
 
 
 def first_back(
@@ -1028,11 +1032,11 @@
     ]
     w_pieces = [move(w_near, flip_core=1), w_far, move(w_far[256:], flip_core=1)]
 
-    normed1, up1, act1, ss1, mixed1, b_send, b_keep, send1, keep1, bias1 = call(
+    normed1, up1, act1, ss1, mixed1, send1, keep1, bias1 = call(
         last_layer,
         [place] + n_blocks + up_blocks + [vec, turn, triple, merger, expander, shrinker] + w_pieces,
         [SM] + [VM] * 10 + [HBM] * 4 + [ANY] * 3,
-        [full, full, full, shape(512, WIDE), shape(512, 256), full, shape(512, W, dtype=F32)]
+        [full, full, full, shape(512, WIDE), shape(512, 256)]
         + [send, keep, shape(8, WIDE, dtype=F32)],
         scratch=[
             wide, merge, shrink, pltpu.VMEM((512, 768), BF), pltpu.VMEM((512, 768), F32),
@@ -1047,9 +1051,14 @@
     far1 = move(low1, flip_z=1)
     s1, k1, s3, k3 = weight_two(after(place, low1), act1, up1, normed1, ss1, mixed1)
     g0, g2 = hops(after((s0, s2), low1), (0, 2), 0)
+    b_send, b_keep = call(
+        last_branches, [after(act1, s1), mixed1, merger, shrinker], [VM] * 2 + [HBM] * 2,
+        [full, shape(512, W, dtype=F32)],
+        scratch=[merge, shrink, pltpu.SemaphoreType.DMA((2,))], room=9,
+    )
     slope1, low1, rows1 = call(
         functools.partial(norm_back, layer=1),
-        [after(place, s1), state1, cotangent, cotangent, keep1, got1, far1, vec],
+        [after(place, b_keep), state1, cotangent, cotangent, keep1, got1, far1, vec],
         [SM] + [VM] * 7,
         [shape(128, W, dtype=F32), shape(128, W), shape(8, W, dtype=F32)],
     )

time: 343 us -> 339 us (0.988)
    pallas_call x35 -> x36, Pallas kernels: 90.3 us -> 89.3 us  [call(): pl.pallas_call(body, out_shape=outs, in_specs=specs, out_specs=out_specs...]
    unnamed x82 -> x64, local copies, waits for them, and re-layouts: 14.3 us -> 14.3 us
  transfers between devices with their start and end apart: 77 -> 77, of which waited for: 47 -> 48; matrix products, arithmetic and copies ran while one was open for 1% -> 1% of each run, Pallas kernels for 19% -> 20%
where the time goes in v2:
time: 339 us; the launch traced here: 334 us
  waiting for transfers between devices  141 us (42%)
  Pallas kernels  89.3 us (26%)
  starting transfers between devices  69.2 us (20%)
  between operations  15.9 us (5%)
  local copies, waits for them, and re-layouts  14.7 us (4%)
  other arithmetic  3.98 us (1%)
    ppermute x76, waiting for transfers between devices, move(): return lax.ppermute(value, AXES, pairs)  141 us
    pallas_call x36, Pallas kernels, call(): pl.pallas_call(body, out_shape=outs, in_specs=specs, out_specs=out_specs...  89.3 us
    ppermute x76, starting transfers between devices, move(): return lax.ppermute(value, AXES, pairs)  69.1 us
    unnamed x64, local copies, waits for them, and re-layouts  14.3 us
  transfers between devices with their start and end apart: 77, of which 48 were waited for; matrix products, arithmetic and copies ran while one was open for 1% of the time, Pallas kernels for 20%

profile of v2, /device:TPU:0, one launch (start us, length us, event | category | flops | bytes accessed | tf_op | source)
XLA Modules:
  0.0 334.1 jit_solution(5847992733445469462)
XLA Ops:
  8.0 1.9 copy-done
  13.3 1.9 shard_map.228
  15.1 3.6 %collective-permute-start.5 = (bf16[272,768]{1,0:T(8,128)(2,1)}, bf16[272,768]{1,0:T(8,128)(2,1)}, u32[]{:S(2)}, u32[]{:S(2)}) collective-permute-start(bf16[272,768]{1,0:T(8,128)(2,1)} %get-tuple-element.188), channel_id=1, source_target_pairs={{0,19},{1,18},{2,17},{3,16},{4,23},{5,22},{6,21},{7,20},{8,27},{9,... | collective-permute-start | bytes 1253384 | tf_op jit(solution)/shard_map/ppermute | solution.py:48
  19.5 2.0 collective-permute-start.4
  21.6 2.2 copy-done.2
  26.1 2.8 collective-permute-done.1.x2
  29.1 3.4 %collective-permute-start.10 = (bf16[256,1024]{1,0:T(8,128)(2,1)S(1)}, bf16[256,1024]{1,0:T(8,128)(2,1)S(1)}, u32[]{:S(2)}, u32[]{:S(2)}) collective-permute-start(bf16[256,1024]{1,0:T(8,128)(2,1)S(1)} %get-tuple-element.200), channel_id=1, source_target_pairs={{0,19},{1,18},{2,17},{3,16},{4,23},{5,22},{6,21},{7,20},{8,27},{9,... | collective-permute-start | bytes 1572872 | tf_op jit(solution)/shard_map/ppermute | solution.py:48
  32.9 2.0 fusion.4
  35.0 9.5 %collective-permute-done.10.e3 = bf16[256,1024]{1,0:T(8,128)(2,1)S(1)} collective-permute-done((bf16[256,1024]{1,0:T(8,128)(2,1)S(1)}, bf16[256,1024]{1,0:T(8,128)(2,1)S(1)}, u32[]{:S(2)}, u32[]{:S(2)}) %collective-permute-start.10) | collective-permute-done | bytes 524320 | tf_op jit(solution)/shard_map/ppermute | solution.py:48
  44.5 3.4 %collective-permute-start.19 = (bf16[512,1792]{1,0:T(8,128)(2,1)S(1)}, bf16[512,1792]{1,0:T(8,128)(2,1)S(1)}, u32[]{:S(2)}, u32[]{:S(2)}) collective-permute-start(bf16[512,1792]{1,0:T(8,128)(2,1)S(1)} %get-tuple-element.210), channel_id=1, source_target_pairs={{0,18},{1,19},{2,16},{3,17},{4,22},{5,23},{6,20},{7,21},{8,26},{9,... | collective-permute-start | bytes 5505032 | tf_op jit(solution)/shard_map/ppermute | solution.py:48
  49.9 6.9 %shard_map.229 = (bf16[512,1024]{1,0:T(8,128)(2,1)S(1)}, bf16[512,768]{1,0:T(8,128)(2,1)S(1)}, bf16[512,256]{1,0:T(8,128)(2,1)S(1)}, bf16[256,1024]{1,0:T(8,128)...) custom-call(s32[8]{0:T(128)S(1)} %stack.37.place, bf16[128,1024]{1,0:T(8,128)(2,1)S(1)} %copy-done.14, ...), custom_call_target="tpu_custom_call" | custom-call | flops 1 | bytes 1 | tf_op jit(solution)/shard_map/pallas_call | solution.py:77
  56.8 3.4 %shard_map.231 = (f32[512,1024]{1,0:T(8,128)S(1)}, bf16[256,1024]{1,0:T(8,128)(2,1)S(1)}, f32[256,1024]{1,0:T(8,128)S(1)}) custom-call(s32[8]{0:T(128)S(1)} %stack.37.place, bf16[512,1024]{1,0:T(8,128)(2,1)S(1)} %get-tuple-element.196.normed, f32[16,1024]{1,0:T(8,128)S(1)} %get-tuple-element.197.vec.refs_6_.refs_3_, bf16[2,256,4096]{2,1,0:T(8,128)(2,1)S(1)} %copy-done.3, ...), custom_call_target="tpu_custom_call" | custom-call | flops 1 | bytes 1 | tf_op jit(solution)/shard_map/pallas_call | solution.py:77
  64.6 7.0 %collective-permute-done.12.refs_5_ = bf16[128,1024]{1,0:T(8,128)(2,1)S(1)} collective-permute-done((bf16[128,1024]{1,0:T(8,128)(2,1)S(1)}, bf16[128,1024]{1,0:T(8,128)(2,1)S(1)}, u32[]{:S(2)}, u32[]{:S(2)}) %collective-permute-start.12) | collective-permute-done | bytes 262176 | tf_op jit(solution)/shard_map/ppermute | solution.py:48
  71.6 4.8 %collective-permute-done.8.refs_2_ = bf16[128,1024]{1,0:T(8,128)(2,1)S(1)} collective-permute-done((bf16[128,1024]{1,0:T(8,128)(2,1)S(1)}, bf16[128,1024]{1,0:T(8,128)(2,1)S(1)}, u32[]{:S(2)}, u32[]{:S(2)}) %collective-permute-start.8) | collective-permute-done | bytes 262176 | tf_op jit(solution)/shard_map/ppermute | solution.py:48
  77.9 7.2 %collective-permute-done.14.n2 = bf16[128,1024]{1,0:T(8,128)(2,1)S(1)} collective-permute-done((bf16[128,1024]{1,0:T(8,128)(2,1)S(1)}, bf16[128,1024]{1,0:T(8,128)(2,1)S(1)}, u32[]{:S(2)}, u32[]{:S(2)}) %collective-permute-start.14) | collective-permute-done | bytes 262176 | tf_op jit(solution)/shard_map/ppermute | solution.py:48
  85.1 3.1 collective-permute-done.19.w2
  93.0 12.6 %shard_map.233 = (bf16[512,1024]{1,0:T(8,128)(2,1)S(1)}, bf16[512,1024]{1,0:T(8,128)(2,1)S(1)}, bf16[512,1024]{1,0:T(8,128)(2,1)S(1)}, bf16[512,1792]{1,0:T(8,12...) custom-call(s32[8]{0:T(128)S(1)} %stack.37.place, ...), custom_call_target="tpu_custom_call" | custom-call | flops 1 | bytes 1 | tf_op jit(solution)/shard_map/pallas_call | solution.py:77
  106.3 3.7 %shard_map.234 = (bf16[512,768]{1,0:T(8,128)(2,1)}, bf16[512,768]{1,0:T(8,128)(2,1)S(1)}, bf16[512,768]{1,0:T(8,128)(2,1)}, bf16[512,768]{1,0:T(8,128)(2,1)S(1)}) custom-call(s32[8]{0:T(128)S(1)} %stack.37.place, bf16[512,1024]{1,0:T(8,128)(2,1)S(1)} %get-tuple-element.223.act, bf16[512,1024]{1,0:T(8,128)(2,1)S(1)} %get-tuple-element.215.up, ...), custom_call_target="tpu_custom_call" | custom-call | flops 1 | bytes 1 | tf_op jit(solution)/shard_map/pallas_call | solution.py:77
  110.1 3.9 %shard_map.235 = (bf16[512,768]{1,0:T(8,128)(2,1)}, bf16[512,768]{1,0:T(8,128)(2,1)S(1)}, bf16[512,768]{1,0:T(8,128)(2,1)}, bf16[512,768]{1,0:T(8,128)(2,1)S(1)}) custom-call(s32[8]{0:T(128)S(1)} %stack.37.place, bf16[512,1024]{1,0:T(8,128)(2,1)S(1)} %get-tuple-element.223.act, bf16[512,1024]{1,0:T(8,128)(2,1)S(1)} %get-tuple-element.215.up, ...), custom_call_target="tpu_custom_call" | custom-call | flops 1 | bytes 1 | tf_op jit(solution)/shard_map/pallas_call | solution.py:77
  113.9 1.7 shard_map.236
  116.7 2.0 collective-permute-done.22.sz
  121.6 2.1 collective-permute-start.41
  125.3 2.3 collective-permute-done.23.u2
  129.2 3.1 collective-permute-start.32
  132.3 11.0 %shard_map.238 = (bf16[512,1024]{1,0:T(8,128)(2,1)S(1)}, bf16[512,1024]{1,0:T(8,128)(2,1)S(1)}, bf16[512,1792]{1,0:T(8,128)(2,1)S(1)}, bf16[256,1024]{1,0:T(8,12...) custom-call(s32[8]{0:T(128)S(1)} %stack.37.place, bf16[128,1024]{1,0:T(8,128)(2,1)S(1)} %get-tuple-element.229.u0.up, ...), custom_call_target="tpu_custom_call" | custom-call | flops 1 | bytes 1 | tf_op jit(solution)/shard_map/pallas_call | solution.py:77
  143.3 2.6 shard_map.241
  147.6 2.1 collective-permute-start.29
  153.6 2.8 shard_map.244
  156.4 4.5 %collective-permute-done.42.g0 = bf16[256,768]{1,0:T(8,128)(2,1)S(1)} collective-permute-done((bf16[256,768]{1,0:T(8,128)(2,1)S(1)}, bf16[256,768]{1,0:T(8,128)(2,1)S(1)}, u32[]{:S(2)}, u32[]{:S(2)}) %collective-permute-start.42) | collective-permute-done | bytes 393248 | tf_op jit(solution)/shard_map/ppermute | solution.py:48
  163.3 3.1 collective-permute-done.28.ga
  166.5 2.8 collective-permute-start.45
  170.2 3.6 %collective-permute-done.43.g1 = bf16[256,768]{1,0:T(8,128)(2,1)S(1)} collective-permute-done((bf16[256,768]{1,0:T(8,128)(2,1)S(1)}, bf16[256,768]{1,0:T(8,128)(2,1)S(1)}, u32[]{:S(2)}, u32[]{:S(2)}) %collective-permute-start.43) | collective-permute-done | bytes 393248 | tf_op jit(solution)/shard_map/ppermute | solution.py:48
  173.8 2.8 collective-permute-done.45.g3
  177.5 2.8 collective-permute-start.46
  180.5 1.9 collective-permute-start.30
  184.2 2.7 collective-permute-done.46.ga
  186.9 2.8 collective-permute-start.37
  189.7 2.5 collective-permute-done.47.gb
  193.5 5.1 %collective-permute-done.27.sz = bf16[128,1024]{1,0:T(8,128)(2,1)S(1)} collective-permute-done((bf16[128,1024]{1,0:T(8,128)(2,1)S(1)}, bf16[128,1024]{1,0:T(8,128)(2,1)S(1)}, u32[]{:S(2)}, u32[]{:S(2)}) %collective-permute-start.27) | collective-permute-done | bytes 262176 | tf_op jit(solution)/shard_map/ppermute | solution.py:48
  199.6 2.0 shard_map.239
  203.6 1.9 collective-permute-done.48.refs_1_
  206.2 3.0 collective-permute-start.52
  210.4 1.8 collective-permute-done.38.ga
  212.9 3.0 collective-permute-done.50.refs_2_
  219.8 2.0 collective-permute-start.57
  221.9 6.5 %collective-permute-done.57.refs_1_ = bf16[64,1536]{1,0:T(8,128)(2,1)S(1)} collective-permute-done((bf16[64,1536]{1,0:T(8,128)(2,1)}, bf16[64,1536]{1,0:T(8,128)(2,1)S(1)}, u32[]{:S(2)}, u32[]{:S(2)}) %collective-permute-start.57) | collective-permute-done | bytes 196640 | tf_op jit(solution)/shard_map/ppermute | solution.py:48
  231.8 2.0 collective-permute-start.60
  237.0 6.7 %collective-permute-done.60.refs_3_ = bf16[32,2304]{1,0:T(8,128)(2,1)S(1)} collective-permute-done((bf16[32,2304]{1,0:T(8,128)(2,1)S(1)}, bf16[32,2304]{1,0:T(8,128)(2,1)S(1)}, u32[]{:S(2)}, u32[]{:S(2)}) %collective-permute-start.60) | collective-permute-done | bytes 147488 | tf_op jit(solution)/shard_map/ppermute | solution.py:48
  243.7 2.2 collective-permute-done.61.refs_4_
  251.0 3.1 collective-permute-done.54.refs_2_
  255.1 2.1 shard_map.253
  257.2 4.8 %collective-permute-done.64.gb = bf16[64,1536]{1,0:T(8,128)(2,1)} collective-permute-done((bf16[64,1536]{1,0:T(8,128)(2,1)}, bf16[64,1536]{1,0:T(8,128)(2,1)}, u32[]{:S(2)}, u32[]{:S(2)}) %collective-permute-start.64) | collective-permute-done | bytes 196640 | tf_op jit(solution)/shard_map/ppermute | solution.py:48
  265.7 3.5 %collective-permute-done.56 = f32[1,6]{1,0:T(1,128)S(1)} collective-permute-done((f32[1,6]{1,0:T(1,128)S(1)}, f32[1,6]{1,0:T(1,128)S(1)}, u32[]{:S(2)}, u32[]{:S(2)}) %collective-permute-start.56) | collective-permute-done | bytes 56 | tf_op jit(solution)/shard_map/ppermute | solution.py:48
  269.7 13.9 %collective-permute-done.66.gb = bf16[128,1536]{1,0:T(8,128)(2,1)S(1)} collective-permute-done((bf16[128,1536]{1,0:T(8,128)(2,1)S(1)}, bf16[128,1536]{1,0:T(8,128)(2,1)S(1)}, u32[]{:S(2)}, u32[]{:S(2)}) %collective-permute-start.66) | collective-permute-done | bytes 393248 | tf_op jit(solution)/shard_map/ppermute | solution.py:48
  283.6 3.2 collective-permute-done.65.ga
  287.6 2.7 collective-permute-start.69
  290.4 5.5 %collective-permute-done.68.g1 = bf16[256,768]{1,0:T(8,128)(2,1)S(1)} collective-permute-done((bf16[256,768]{1,0:T(8,128)(2,1)S(1)}, bf16[256,768]{1,0:T(8,128)(2,1)S(1)}, u32[]{:S(2)}, u32[]{:S(2)}) %collective-permute-start.68) | collective-permute-done | bytes 393248 | tf_op jit(solution)/shard_map/ppermute | solution.py:48
  297.2 2.4 collective-permute-done.70.g3
  299.6 1.7 shard_map.259
  303.7 2.0 collective-permute-start.74
  305.7 2.8 copy-done.9
  308.5 5.6 %shard_map.261 = (f32[2,256,3072]{2,1,0:T(8,128)}, f32[2,256,1024]{2,1,0:T(8,128)}, f32[2,256,4096]{2,1,0:T(8,128)}, f32[2,1024,1024]{2,1,0:T(8,128)}) custom-call(bf16[2048,1536]{1,0:T(8,128)(2,1)S(1)} %copy-done.9), custom_call_target="tpu_custom_call" | custom-call | flops 1 | bytes 1 | tf_op jit(solution)/shard_map/pallas_call | solution.py:77
  314.1 4.1 %shard_map.262 = (f32[2,256,3072]{2,1,0:T(8,128)}, f32[2,256,1024]{2,1,0:T(8,128)}, f32[2,256,4096]{2,1,0:T(8,128)}, f32[2,1024,1024]{2,1,0:T(8,128)}) custom-call(s32[8]{0:T(128)S(1)} %stack.37.place, bf16[544,768]{1,0:T(8,128)(2,1)S(1)} %get-tuple-element.328.p0.refs_0_, ...), custom_call_target="tpu_custom_call", output_to_operand_aliasing={{0}: (5, {}), {1}: (6, {}), {2}: (7, {}), {3}: (8, {})} | custom-call | flops 1 | bytes 1 | tf_op jit(solution)/shard_map/pallas_call | solution.py:77
  321.6 5.2 %shard_map.263 = (f32[2,256,3072]{2,1,0:T(8,128)}, f32[2,256,1024]{2,1,0:T(8,128)}, f32[2,256,4096]{2,1,0:T(8,128)}, f32[2,1024,1024]{2,1,0:T(8,128)}, f32[2,256...) custom-call(s32[8]{0:T(128)S(1)} %stack.37.place, ...), custom_call_target="tpu_custom_call", output_to_operand_aliasing={{0}: (6, {}), {1}: (7, {}), {2}: (8, {}), {3}: (9, {})} | custom-call | flops 1 | bytes 1 | tf_op jit(solution)/shard_map/pallas_call | solution.py:77
  (215 shorter events, 74.8 us)
Async XLA Ops:
  7.2 298.5 %all-gather.2.cloned.1.call-start = ((), (), s32[]{:S(2)}) async-start(), calls=%async_computation | async-start | bytes 6684672 | tf_op jit(solution)/shard_map/all_gather | solution.py:884
  15.1 14.0 %collective-permute-start.5 = (bf16[272,768]{1,0:T(8,128)(2,1)}, bf16[272,768]{1,0:T(8,128)(2,1)}, u32[]{:S(2)}, u32[]{:S(2)}) collective-permute-start(bf16[272,768]{1,0:T(8,128)(2,1)} %get-tuple-element.188), channel_id=1, source_target_pairs={{0,19},{1,18},{2,17},{3,16},{4,23},{5,22},{6,21},{7,20},{8,27},{9,... | collective-permute-start | bytes 1253384 | tf_op jit(solution)/shard_map/ppermute | solution.py:48
  19.5 9.5 %collective-permute-start.1 = (bf16[128,1024]{1,0:T(8,128)(2,1)}, bf16[128,1024]{1,0:T(8,128)(2,1)}, u32[]{:S(2)}, u32[]{:S(2)}) collective-permute-start(bf16[128,1024]{1,0:T(8,128)(2,1)} %state.3), channel_id=1, source_target_pairs={{0,2},{1,3},{2,0},{3,1},{4,6},{5,7},{6,4},{7,5},{8,10},{9,11},{10,... | collective-permute-start | bytes 786440 | tf_op jit(solution)/shard_map/ppermute | solution.py:48
  19.5 28.5 %collective-permute-start.3 = (bf16[272,768]{1,0:T(8,128)(2,1)}, bf16[272,768]{1,0:T(8,128)(2,1)}, u32[]{:S(2)}, u32[]{:S(2)}) collective-permute-start(bf16[272,768]{1,0:T(8,128)(2,1)} %get-tuple-element.186), channel_id=1, source_target_pairs={{0,1},{1,0},{2,3},{3,2},{4,5},{5,4},{6,7},{7,6},{8,9},{9,8},{10,11... | collective-permute-start | bytes 1253384 | tf_op jit(solution)/shard_map/ppermute | solution.py:48
  19.5 28.7 %collective-permute-start.4 = (bf16[272,768]{1,0:T(8,128)(2,1)}, bf16[272,768]{1,0:T(8,128)(2,1)}, u32[]{:S(2)}, u32[]{:S(2)}) collective-permute-start(bf16[272,768]{1,0:T(8,128)(2,1)} %get-tuple-element.187), channel_id=1, source_target_pairs={{0,2},{1,3},{2,0},{3,1},{4,6},{5,7},{6,4},{7,5},{8,10},{9,11},{10,... | collective-permute-start | bytes 1253384 | tf_op jit(solution)/shard_map/ppermute | solution.py:48
  28.9 27.8 %collective-permute-start.6 = (bf16[384,1024]{1,0:T(8,128)(2,1)S(1)}, bf16[384,1024]{1,0:T(8,128)(2,1)S(1)}, u32[]{:S(2)}, u32[]{:S(2)}) collective-permute-start(bf16[384,1024]{1,0:T(8,128)(2,1)S(1)} %get-tuple-element.194), channel_id=1, source_target_pairs={{0,2},{1,3},{2,0},{3,1},{4,6},{5,7},{6,4},{7,5},{8,10},{9,11},{10,... | collective-permute-start | bytes 2359304 | tf_op jit(solution)/shard_map/ppermute | solution.py:48
  29.1 15.4 %collective-permute-start.10 = (bf16[256,1024]{1,0:T(8,128)(2,1)S(1)}, bf16[256,1024]{1,0:T(8,128)(2,1)S(1)}, u32[]{:S(2)}, u32[]{:S(2)}) collective-permute-start(bf16[256,1024]{1,0:T(8,128)(2,1)S(1)} %get-tuple-element.200), channel_id=1, source_target_pairs={{0,19},{1,18},{2,17},{3,16},{4,23},{5,22},{6,21},{7,20},{8,27},{9,... | collective-permute-start | bytes 1572872 | tf_op jit(solution)/shard_map/ppermute | solution.py:48
  32.5 24.3 %collective-permute-start.9 = (bf16[256,1024]{1,0:T(8,128)(2,1)S(1)}, bf16[256,1024]{1,0:T(8,128)(2,1)S(1)}, u32[]{:S(2)}, u32[]{:S(2)}) collective-permute-start(bf16[256,1024]{1,0:T(8,128)(2,1)S(1)} %get-tuple-element.198), channel_id=1, source_target_pairs={{0,1},{1,0},{2,3},{3,2},{4,5},{5,4},{6,7},{7,6},{8,9},{9,8},{10,11... | collective-permute-start | bytes 1572872 | tf_op jit(solution)/shard_map/ppermute | solution.py:48
  44.5 43.7 %collective-permute-start.19 = (bf16[512,1792]{1,0:T(8,128)(2,1)S(1)}, bf16[512,1792]{1,0:T(8,128)(2,1)S(1)}, u32[]{:S(2)}, u32[]{:S(2)}) collective-permute-start(bf16[512,1792]{1,0:T(8,128)(2,1)S(1)} %get-tuple-element.210), channel_id=1, source_target_pairs={{0,18},{1,19},{2,16},{3,17},{4,22},{5,23},{6,20},{7,21},{8,26},{9,... | collective-permute-start | bytes 5505032 | tf_op jit(solution)/shard_map/ppermute | solution.py:48
  62.4 9.2 %collective-permute-start.12 = (bf16[128,1024]{1,0:T(8,128)(2,1)S(1)}, bf16[128,1024]{1,0:T(8,128)(2,1)S(1)}, u32[]{:S(2)}, u32[]{:S(2)}) collective-permute-start(bf16[128,1024]{1,0:T(8,128)(2,1)S(1)} %add_convert_fusion.2), channel_id=1, source_target_pairs={{0,2},{1,3},{2,0},{3,1},{4,6},{5,7},{6,4},{7,5},{8,10},{9,11},{10,... | collective-permute-start | bytes 786440 | tf_op jit(solution)/shard_map/ppermute | solution.py:48
  63.1 13.3 %collective-permute-start.8 = (bf16[128,1024]{1,0:T(8,128)(2,1)S(1)}, bf16[128,1024]{1,0:T(8,128)(2,1)S(1)}, u32[]{:S(2)}, u32[]{:S(2)}) collective-permute-start(bf16[128,1024]{1,0:T(8,128)(2,1)S(1)} %add_convert_fusion.3), channel_id=1, source_target_pairs={{0,2},{1,3},{2,0},{3,1},{4,6},{5,7},{6,4},{7,5},{8,10},{9,11},{10,... | collective-permute-start | bytes 786440 | tf_op jit(solution)/shard_map/ppermute | solution.py:48
  77.5 7.6 %collective-permute-start.14 = (bf16[128,1024]{1,0:T(8,128)(2,1)S(1)}, bf16[128,1024]{1,0:T(8,128)(2,1)S(1)}, u32[]{:S(2)}, u32[]{:S(2)}) collective-permute-start(bf16[128,1024]{1,0:T(8,128)(2,1)S(1)} %get-tuple-element.204.n0), channel_id=1, source_target_pairs={{0,2},{1,3},{2,0},{3,1},{4,6},{5,7},{6,4},{7,5},{8,10},{9,11},{10,... | collective-permute-start | bytes 786440 | tf_op jit(solution)/shard_map/ppermute | solution.py:48
  77.9 13.7 %collective-permute-start.18 = (bf16[256,1792]{1,0:T(8,128)(2,1)S(1)}, bf16[256,1792]{1,0:T(8,128)(2,1)S(1)}, u32[]{:S(2)}, u32[]{:S(2)}) collective-permute-start(bf16[256,1792]{1,0:T(8,128)(2,1)S(1)} %get-tuple-element.209), channel_id=1, source_target_pairs={{0,1},{1,0},{2,3},{3,2},{4,5},{5,4},{6,7},{7,6},{8,9},{9,8},{10,11... | collective-permute-start | bytes 2752520 | tf_op jit(solution)/shard_map/ppermute | solution.py:48
  88.3 4.7 %collective-permute-start.20 = (bf16[256,1792]{1,0:T(8,128)(2,1)S(1)}, bf16[256,1792]{1,0:T(8,128)(2,1)S(1)}, u32[]{:S(2)}, u32[]{:S(2)}) collective-permute-start(bf16[256,1792]{1,0:T(8,128)(2,1)S(1)} %slice.47), channel_id=1, source_target_pairs={{0,1},{1,0},{2,3},{3,2},{4,5},{5,4},{6,7},{7,6},{8,9},{9,8},{10,11... | collective-permute-start | bytes 2752520 | tf_op jit(solution)/shard_map/ppermute | solution.py:48
  105.6 4.3 %collective-permute-start.21 = (bf16[256,1024]{1,0:T(8,128)(2,1)S(1)}, bf16[256,1024]{1,0:T(8,128)(2,1)S(1)}, u32[]{:S(2)}, u32[]{:S(2)}) collective-permute-start(bf16[256,1024]{1,0:T(8,128)(2,1)S(1)} %get-tuple-element.214), channel_id=1, source_target_pairs={{0,1},{1,0},{2,3},{3,2},{4,5},{5,4},{6,7},{7,6},{8,9},{9,8},{10,11... | collective-permute-start | bytes 1572872 | tf_op jit(solution)/shard_map/ppermute | solution.py:48
  110.0 8.7 %collective-permute-start.22 = (bf16[128,1024]{1,0:T(8,128)(2,1)S(1)}, bf16[128,1024]{1,0:T(8,128)(2,1)S(1)}, u32[]{:S(2)}, u32[]{:S(2)}) collective-permute-start(bf16[128,1024]{1,0:T(8,128)(2,1)S(1)} %add_convert_fusion.1), channel_id=1, source_target_pairs={{0,2},{1,3},{2,0},{3,1},{4,6},{5,7},{6,4},{7,5},{8,10},{9,11},{10,... | collective-permute-start | bytes 786440 | tf_op jit(solution)/shard_map/ppermute | solution.py:48
  119.8 7.9 %collective-permute-start.23 = (bf16[128,1024]{1,0:T(8,128)(2,1)S(1)}, bf16[128,1024]{1,0:T(8,128)(2,1)S(1)}, u32[]{:S(2)}, u32[]{:S(2)}) collective-permute-start(bf16[128,1024]{1,0:T(8,128)(2,1)S(1)} %get-tuple-element.229.u0.up), channel_id=1, source_target_pairs={{0,2},{1,3},{2,0},{3,1},{4,6},{5,7},{6,4},{7,5},{8,10},{9,11},{10,... | collective-permute-start | bytes 786440 | tf_op jit(solution)/shard_map/ppermute | solution.py:48
  120.1 27.4 %collective-permute-start.40 = (bf16[512,768]{1,0:T(8,128)(2,1)}, bf16[512,768]{1,0:T(8,128)(2,1)S(1)}, u32[]{:S(2)}, u32[]{:S(2)}) collective-permute-start(bf16[512,768]{1,0:T(8,128)(2,1)} %get-tuple-element.279), channel_id=1, source_target_pairs={{0,32},{1,33},{2,34},{3,35},{4,36},{5,37},{6,38},{7,39},{8,40},{9,... | collective-permute-start | bytes 2359304 | tf_op jit(solution)/shard_map/ppermute | solution.py:48
  121.6 28.0 %collective-permute-start.41 = (bf16[512,768]{1,0:T(8,128)(2,1)}, bf16[512,768]{1,0:T(8,128)(2,1)S(1)}, u32[]{:S(2)}, u32[]{:S(2)}) collective-permute-start(bf16[512,768]{1,0:T(8,128)(2,1)} %get-tuple-element.281), channel_id=1, source_target_pairs={{0,96},{1,97},{2,98},{3,99},{4,100},{5,101},{6,102},{7,103},{8,104... | collective-permute-start | bytes 2359304 | tf_op jit(solution)/shard_map/ppermute | solution.py:48
  123.7 27.1 %collective-permute-start.31 = (bf16[512,768]{1,0:T(8,128)(2,1)}, bf16[512,768]{1,0:T(8,128)(2,1)S(1)}, u32[]{:S(2)}, u32[]{:S(2)}) collective-permute-start(bf16[512,768]{1,0:T(8,128)(2,1)} %get-tuple-element.251), channel_id=1, source_target_pairs={{0,4},{1,5},{2,6},{3,7},{4,0},{5,1},{6,2},{7,3},{8,12},{9,13},{10,... | collective-permute-start | bytes 2359304 | tf_op jit(solution)/shard_map/ppermute | solution.py:48
  127.6 4.7 %collective-permute-start.25 = (bf16[128,1024]{1,0:T(8,128)(2,1)S(1)}, bf16[128,1024]{1,0:T(8,128)(2,1)S(1)}, u32[]{:S(2)}, u32[]{:S(2)}) collective-permute-start(bf16[128,1024]{1,0:T(8,128)(2,1)S(1)} %collective-permute-done.23.u2), channel_id=1, source_target_pairs={{0,1},{1,0},{2,3},{3,2},{4,5},{5,4},{6,7},{7,6},{8,9},{9,8},{10,11... | collective-permute-start | bytes 786440 | tf_op jit(solution)/shard_map/ppermute | solution.py:48
  129.2 22.9 %collective-permute-start.32 = (bf16[512,768]{1,0:T(8,128)(2,1)}, bf16[512,768]{1,0:T(8,128)(2,1)S(1)}, u32[]{:S(2)}, u32[]{:S(2)}) collective-permute-start(bf16[512,768]{1,0:T(8,128)(2,1)} %get-tuple-element.253), channel_id=1, source_target_pairs={{0,12},{1,13},{2,14},{3,15},{4,8},{5,9},{6,10},{7,11},{8,4},{9,5},... | collective-permute-start | bytes 2359304 | tf_op jit(solution)/shard_map/ppermute | solution.py:48
  146.0 20.5 %collective-permute-start.28 = (bf16[512,768]{1,0:T(8,128)(2,1)S(1)}, bf16[512,768]{1,0:T(8,128)(2,1)S(1)}, u32[]{:S(2)}, u32[]{:S(2)}) collective-permute-start(bf16[512,768]{1,0:T(8,128)(2,1)S(1)} %get-tuple-element.243), channel_id=1, source_target_pairs={{0,32},{1,33},{2,34},{3,35},{4,36},{5,37},{6,38},{7,39},{8,40},{9,... | collective-permute-start | bytes 2359304 | tf_op jit(solution)/shard_map/ppermute | solution.py:48
  147.6 21.7 %collective-permute-start.29 = (bf16[512,768]{1,0:T(8,128)(2,1)S(1)}, bf16[512,768]{1,0:T(8,128)(2,1)S(1)}, u32[]{:S(2)}, u32[]{:S(2)}) collective-permute-start(bf16[512,768]{1,0:T(8,128)(2,1)S(1)} %get-tuple-element.245), channel_id=1, source_target_pairs={{0,96},{1,97},{2,98},{3,99},{4,100},{5,101},{6,102},{7,103},{8,104... | collective-permute-start | bytes 2359304 | tf_op jit(solution)/shard_map/ppermute | solution.py:48
  150.6 10.4 %collective-permute-start.42 = (bf16[256,768]{1,0:T(8,128)(2,1)S(1)}, bf16[256,768]{1,0:T(8,128)(2,1)S(1)}, u32[]{:S(2)}, u32[]{:S(2)}) collective-permute-start(bf16[256,768]{1,0:T(8,128)(2,1)S(1)} %get-tuple-element.283), channel_id=1, source_target_pairs={{0,4},{1,5},{2,6},{3,7},{4,0},{5,1},{6,2},{7,3},{8,12},{9,13},{10,... | collective-permute-start | bytes 1179656 | tf_op jit(solution)/shard_map/ppermute | solution.py:48
  150.8 11.7 %collective-permute-start.44 = (bf16[256,768]{1,0:T(8,128)(2,1)S(1)}, bf16[256,768]{1,0:T(8,128)(2,1)S(1)}, u32[]{:S(2)}, u32[]{:S(2)}) collective-permute-start(bf16[256,768]{1,0:T(8,128)(2,1)S(1)} %get-tuple-element.286), channel_id=1, source_target_pairs={{0,12},{1,13},{2,14},{3,15},{4,8},{5,9},{6,10},{7,11},{8,4},{9,5},... | collective-permute-start | bytes 1179656 | tf_op jit(solution)/shard_map/ppermute | solution.py:48
  153.0 20.8 %collective-permute-start.43 = (bf16[256,768]{1,0:T(8,128)(2,1)S(1)}, bf16[256,768]{1,0:T(8,128)(2,1)S(1)}, u32[]{:S(2)}, u32[]{:S(2)}) collective-permute-start(bf16[256,768]{1,0:T(8,128)(2,1)S(1)} %get-tuple-element.254), channel_id=1, source_target_pairs={{0,32},{1,33},{2,34},{3,35},{4,36},{5,37},{6,38},{7,39},{8,40},{9,... | collective-permute-start | bytes 1179656 | tf_op jit(solution)/shard_map/ppermute | solution.py:48
  161.0 19.5 %collective-permute-start.33 = (bf16[512,768]{1,0:T(8,128)(2,1)S(1)}, bf16[512,768]{1,0:T(8,128)(2,1)S(1)}, u32[]{:S(2)}, u32[]{:S(2)}) collective-permute-start(bf16[512,768]{1,0:T(8,128)(2,1)S(1)} %get-tuple-element.258), channel_id=1, source_target_pairs={{0,4},{1,5},{2,6},{3,7},{4,0},{5,1},{6,2},{7,3},{8,12},{9,13},{10,... | collective-permute-start | bytes 2359304 | tf_op jit(solution)/shard_map/ppermute | solution.py:48
  162.5 19.9 %collective-permute-start.34 = (bf16[512,768]{1,0:T(8,128)(2,1)S(1)}, bf16[512,768]{1,0:T(8,128)(2,1)S(1)}, u32[]{:S(2)}, u32[]{:S(2)}) collective-permute-start(bf16[512,768]{1,0:T(8,128)(2,1)S(1)} %get-tuple-element.260), channel_id=1, source_target_pairs={{0,12},{1,13},{2,14},{3,15},{4,8},{5,9},{6,10},{7,11},{8,4},{9,5},... | collective-permute-start | bytes 2359304 | tf_op jit(solution)/shard_map/ppermute | solution.py:48
  166.5 10.1 %collective-permute-start.45 = (bf16[256,768]{1,0:T(8,128)(2,1)S(1)}, bf16[256,768]{1,0:T(8,128)(2,1)S(1)}, u32[]{:S(2)}, u32[]{:S(2)}) collective-permute-start(bf16[256,768]{1,0:T(8,128)(2,1)S(1)} %get-tuple-element.288), channel_id=1, source_target_pairs={{0,96},{1,97},{2,98},{3,99},{4,100},{5,101},{6,102},{7,103},{8,104... | collective-permute-start | bytes 1179656 | tf_op jit(solution)/shard_map/ppermute | solution.py:48
  169.3 14.8 %collective-permute-start.26 = (bf16[256,1024]{1,0:T(8,128)(2,1)S(1)}, bf16[256,1024]{1,0:T(8,128)(2,1)S(1)}, u32[]{:S(2)}, u32[]{:S(2)}) collective-permute-start(bf16[256,1024]{1,0:T(8,128)(2,1)S(1)} %get-tuple-element.233), channel_id=1, source_target_pairs={{0,1},{1,0},{2,3},{3,2},{4,5},{5,4},{6,7},{7,6},{8,9},{9,8},{10,11... | collective-permute-start | bytes 1572872 | tf_op jit(solution)/shard_map/ppermute | solution.py:48
  177.5 9.4 %collective-permute-start.46 = (bf16[128,1536]{1,0:T(8,128)(2,1)S(1)}, bf16[128,1536]{1,0:T(8,128)(2,1)S(1)}, u32[]{:S(2)}, u32[]{:S(2)}) collective-permute-start(bf16[128,1536]{1,0:T(8,128)(2,1)S(1)} %get-tuple-element.290), channel_id=1, source_target_pairs={{0,96},{1,97},{2,98},{3,99},{4,100},{5,101},{6,102},{7,103},{8,104... | collective-permute-start | bytes 1179656 | tf_op jit(solution)/shard_map/ppermute | solution.py:48
  180.3 11.9 %collective-permute-start.47 = (bf16[128,1536]{1,0:T(8,128)(2,1)S(1)}, bf16[128,1536]{1,0:T(8,128)(2,1)S(1)}, u32[]{:S(2)}, u32[]{:S(2)}) collective-permute-start(bf16[128,1536]{1,0:T(8,128)(2,1)S(1)} %get-tuple-element.292), channel_id=1, source_target_pairs={{0,4},{1,5},{2,6},{3,7},{4,0},{5,1},{6,2},{7,3},{8,12},{9,13},{10,... | collective-permute-start | bytes 1179656 | tf_op jit(solution)/shard_map/ppermute | solution.py:48
  180.5 19.1 %collective-permute-start.30 = (bf16[256,768]{1,0:T(8,128)(2,1)S(1)}, bf16[256,768]{1,0:T(8,128)(2,1)S(1)}, u32[]{:S(2)}, u32[]{:S(2)}) collective-permute-start(bf16[256,768]{1,0:T(8,128)(2,1)S(1)} %get-tuple-element.247), channel_id=1, source_target_pairs={{0,4},{1,5},{2,6},{3,7},{4,0},{5,1},{6,2},{7,3},{8,12},{9,13},{10,... | collective-permute-start | bytes 1179656 | tf_op jit(solution)/shard_map/ppermute | solution.py:48
  182.4 19.8 %collective-permute-start.36 = (bf16[256,768]{1,0:T(8,128)(2,1)S(1)}, bf16[256,768]{1,0:T(8,128)(2,1)S(1)}, u32[]{:S(2)}, u32[]{:S(2)}) collective-permute-start(bf16[256,768]{1,0:T(8,128)(2,1)S(1)} %get-tuple-element.264), channel_id=1, source_target_pairs={{0,12},{1,13},{2,14},{3,15},{4,8},{5,9},{6,10},{7,11},{8,4},{9,5},... | collective-permute-start | bytes 1179656 | tf_op jit(solution)/shard_map/ppermute | solution.py:48
  184.1 18.1 %collective-permute-start.35 = (bf16[256,768]{1,0:T(8,128)(2,1)S(1)}, bf16[256,768]{1,0:T(8,128)(2,1)S(1)}, u32[]{:S(2)}, u32[]{:S(2)}) collective-permute-start(bf16[256,768]{1,0:T(8,128)(2,1)S(1)} %get-tuple-element.262), channel_id=1, source_target_pairs={{0,32},{1,33},{2,34},{3,35},{4,36},{5,37},{6,38},{7,39},{8,40},{9,... | collective-permute-start | bytes 1179656 | tf_op jit(solution)/shard_map/ppermute | solution.py:48
  186.9 15.3 %collective-permute-start.37 = (bf16[256,768]{1,0:T(8,128)(2,1)S(1)}, bf16[256,768]{1,0:T(8,128)(2,1)S(1)}, u32[]{:S(2)}, u32[]{:S(2)}) collective-permute-start(bf16[256,768]{1,0:T(8,128)(2,1)S(1)} %get-tuple-element.266), channel_id=1, source_target_pairs={{0,96},{1,97},{2,98},{3,99},{4,100},{5,101},{6,102},{7,103},{8,104... | collective-permute-start | bytes 1179656 | tf_op jit(solution)/shard_map/ppermute | solution.py:48
  192.2 6.4 %collective-permute-start.27 = (bf16[128,1024]{1,0:T(8,128)(2,1)S(1)}, bf16[128,1024]{1,0:T(8,128)(2,1)S(1)}, u32[]{:S(2)}, u32[]{:S(2)}) collective-permute-start(bf16[128,1024]{1,0:T(8,128)(2,1)S(1)} %add_convert_fusion), channel_id=1, source_target_pairs={{0,2},{1,3},{2,0},{3,1},{4,6},{5,7},{6,4},{7,5},{8,10},{9,11},{10,... | collective-permute-start | bytes 786440 | tf_op jit(solution)/shard_map/ppermute | solution.py:48
  198.6 6.9 %collective-permute-start.48 = (bf16[64,1536]{1,0:T(8,128)(2,1)S(1)}, bf16[64,1536]{1,0:T(8,128)(2,1)S(1)}, u32[]{:S(2)}, u32[]{:S(2)}) collective-permute-start(bf16[64,1536]{1,0:T(8,128)(2,1)S(1)} %get-tuple-element.294), channel_id=1, source_target_pairs={{0,12},{1,13},{2,14},{3,15},{4,8},{5,9},{6,10},{7,11},{8,4},{9,5},... | collective-permute-start | bytes 589832 | tf_op jit(solution)/shard_map/ppermute | solution.py:48
  199.6 5.9 %collective-permute-start.49 = (bf16[64,1536]{1,0:T(8,128)(2,1)S(1)}, bf16[64,1536]{1,0:T(8,128)(2,1)S(1)}, u32[]{:S(2)}, u32[]{:S(2)}) collective-permute-start(bf16[64,1536]{1,0:T(8,128)(2,1)S(1)} %get-tuple-element.296), channel_id=1, source_target_pairs={{0,32},{1,33},{2,34},{3,35},{4,36},{5,37},{6,38},{7,39},{8,40},{9,... | collective-permute-start | bytes 589832 | tf_op jit(solution)/shard_map/ppermute | solution.py:48
  203.1 9.1 %collective-permute-start.38 = (bf16[128,1536]{1,0:T(8,128)(2,1)S(1)}, bf16[128,1536]{1,0:T(8,128)(2,1)S(1)}, u32[]{:S(2)}, u32[]{:S(2)}) collective-permute-start(bf16[128,1536]{1,0:T(8,128)(2,1)S(1)} %get-tuple-element.268), channel_id=1, source_target_pairs={{0,96},{1,97},{2,98},{3,99},{4,100},{5,101},{6,102},{7,103},{8,104... | collective-permute-start | bytes 1179656 | tf_op jit(solution)/shard_map/ppermute | solution.py:48
  203.6 8.5 %collective-permute-start.39 = (bf16[128,1536]{1,0:T(8,128)(2,1)S(1)}, bf16[128,1536]{1,0:T(8,128)(2,1)S(1)}, u32[]{:S(2)}, u32[]{:S(2)}) collective-permute-start(bf16[128,1536]{1,0:T(8,128)(2,1)S(1)} %get-tuple-element.270), channel_id=1, source_target_pairs={{0,4},{1,5},{2,6},{3,7},{4,0},{5,1},{6,2},{7,3},{8,12},{9,13},{10,... | collective-permute-start | bytes 1179656 | tf_op jit(solution)/shard_map/ppermute | solution.py:48
  206.2 9.9 %collective-permute-start.52 = (bf16[32,4352]{1,0:T(8,128)(2,1)S(1)}, bf16[32,4352]{1,0:T(8,128)(2,1)S(1)}, u32[]{:S(2)}, u32[]{:S(2)}) collective-permute-start(bf16[32,4352]{1,0:T(8,128)(2,1)S(1)} %get-tuple-element.300), channel_id=1, source_target_pairs={{0,16},{1,17},{2,18},{3,19},{4,20},{5,21},{6,22},{7,23},{8,24},{9,... | collective-permute-start | bytes 835592 | tf_op jit(solution)/shard_map/ppermute | solution.py:48
  209.2 6.7 %collective-permute-start.50 = (bf16[32,1792]{1,0:T(8,128)(2,1)S(1)}, bf16[32,1792]{1,0:T(8,128)(2,1)S(1)}, u32[]{:S(2)}, u32[]{:S(2)}) collective-permute-start(bf16[32,1792]{1,0:T(8,128)(2,1)S(1)} %get-tuple-element.299), channel_id=1, source_target_pairs={{0,2},{1,3},{2,0},{3,1},{4,6},{5,7},{6,4},{7,5},{8,10},{9,11},{10,... | collective-permute-start | bytes 344072 | tf_op jit(solution)/shard_map/ppermute | solution.py:48
  210.1 6.0 %collective-permute-start.51 = (bf16[32,1792]{1,0:T(8,128)(2,1)S(1)}, bf16[32,1792]{1,0:T(8,128)(2,1)S(1)}, u32[]{:S(2)}, u32[]{:S(2)}) collective-permute-start(bf16[32,1792]{1,0:T(8,128)(2,1)S(1)} %get-tuple-element.299), channel_id=1, source_target_pairs={{0,18},{1,19},{2,16},{3,17},{4,22},{5,23},{6,20},{7,21},{8,26},{9,... | collective-permute-start | bytes 344072 | tf_op jit(solution)/shard_map/ppermute | solution.py:48
  219.6 15.4 %collective-permute-start.53 = (bf16[512,1024]{1,0:T(8,128)(2,1)}, bf16[512,1024]{1,0:T(8,128)(2,1)S(1)}, u32[]{:S(2)}, u32[]{:S(2)}) collective-permute-start(bf16[512,1024]{1,0:T(8,128)(2,1)} %copy-done.29), channel_id=1, source_target_pairs={{0,1},{1,0},{2,3},{3,2},{4,5},{5,4},{6,7},{7,6},{8,9},{9,8},{10,11... | collective-permute-start | bytes 3145736 | tf_op jit(solution)/shard_map/ppermute | solution.py:48
  219.8 8.6 %collective-permute-start.57 = (bf16[64,1536]{1,0:T(8,128)(2,1)}, bf16[64,1536]{1,0:T(8,128)(2,1)S(1)}, u32[]{:S(2)}, u32[]{:S(2)}) collective-permute-start(bf16[64,1536]{1,0:T(8,128)(2,1)} %copy-done.31), channel_id=1, source_target_pairs={{0,12},{1,13},{2,14},{3,15},{4,8},{5,9},{6,10},{7,11},{8,4},{9,5},... | collective-permute-start | bytes 589832 | tf_op jit(solution)/shard_map/ppermute | solution.py:48
  221.8 7.1 %collective-permute-start.58 = (bf16[64,1536]{1,0:T(8,128)(2,1)}, bf16[64,1536]{1,0:T(8,128)(2,1)S(1)}, u32[]{:S(2)}, u32[]{:S(2)}) collective-permute-start(bf16[64,1536]{1,0:T(8,128)(2,1)} %copy-done.30), channel_id=1, source_target_pairs={{0,32},{1,33},{2,34},{3,35},{4,36},{5,37},{6,38},{7,39},{8,40},{9,... | collective-permute-start | bytes 589832 | tf_op jit(solution)/shard_map/ppermute | solution.py:48
  230.6 6.5 %collective-permute-start.59 = (bf16[32,2304]{1,0:T(8,128)(2,1)S(1)}, bf16[32,2304]{1,0:T(8,128)(2,1)S(1)}, u32[]{:S(2)}, u32[]{:S(2)}) collective-permute-start(bf16[32,2304]{1,0:T(8,128)(2,1)S(1)} %get-tuple-element.314), channel_id=1, source_target_pairs={{0,2},{1,3},{2,0},{3,1},{4,6},{5,7},{6,4},{7,5},{8,10},{9,11},{10,... | collective-permute-start | bytes 442376 | tf_op jit(solution)/shard_map/ppermute | solution.py:48
  231.8 11.9 %collective-permute-start.60 = (bf16[32,2304]{1,0:T(8,128)(2,1)S(1)}, bf16[32,2304]{1,0:T(8,128)(2,1)S(1)}, u32[]{:S(2)}, u32[]{:S(2)}) collective-permute-start(bf16[32,2304]{1,0:T(8,128)(2,1)S(1)} %get-tuple-element.314), channel_id=1, source_target_pairs={{0,18},{1,19},{2,16},{3,17},{4,22},{5,23},{6,20},{7,21},{8,26},{9,... | collective-permute-start | bytes 442376 | tf_op jit(solution)/shard_map/ppermute | solution.py:48
  233.8 12.1 %collective-permute-start.61 = (bf16[32,4864]{1,0:T(8,128)(2,1)S(1)}, bf16[32,4864]{1,0:T(8,128)(2,1)S(1)}, u32[]{:S(2)}, u32[]{:S(2)}) collective-permute-start(bf16[32,4864]{1,0:T(8,128)(2,1)S(1)} %get-tuple-element.315), channel_id=1, source_target_pairs={{0,16},{1,17},{2,18},{3,19},{4,20},{5,21},{6,22},{7,23},{8,24},{9,... | collective-permute-start | bytes 933896 | tf_op jit(solution)/shard_map/ppermute | solution.py:48
  236.0 18.1 %collective-permute-start.54 = (bf16[256,1024]{1,0:T(8,128)(2,1)}, bf16[256,1024]{1,0:T(8,128)(2,1)}, u32[]{:S(2)}, u32[]{:S(2)}) collective-permute-start(bf16[256,1024]{1,0:T(8,128)(2,1)} %bitcast.9), channel_id=1, source_target_pairs={{0,2},{1,3},{2,0},{3,1},{4,6},{5,7},{6,4},{7,5},{8,10},{9,11},{10,... | collective-permute-start | bytes 1572872 | tf_op jit(solution)/shard_map/ppermute | solution.py:48
  249.3 13.4 %collective-permute-start.63 = (bf16[80,1536]{1,0:T(8,128)(2,1)S(1)}, bf16[80,1536]{1,0:T(8,128)(2,1)}, u32[]{:S(2)}, u32[]{:S(2)}) collective-permute-start(bf16[80,1536]{1,0:T(8,128)(2,1)S(1)} %get-tuple-element.320.oa), channel_id=1, source_target_pairs={{0,12},{1,13},{2,14},{3,15},{4,8},{5,9},{6,10},{7,11},{8,4},{9,5},... | collective-permute-start | bytes 737288 | tf_op jit(solution)/shard_map/ppermute | solution.py:48
  250.8 11.3 %collective-permute-start.64 = (bf16[64,1536]{1,0:T(8,128)(2,1)}, bf16[64,1536]{1,0:T(8,128)(2,1)}, u32[]{:S(2)}, u32[]{:S(2)}) collective-permute-start(bf16[64,1536]{1,0:T(8,128)(2,1)} %get-tuple-element.321.ob), channel_id=1, source_target_pairs={{0,32},{1,33},{2,34},{3,35},{4,36},{5,37},{6,38},{7,39},{8,40},{9,... | collective-permute-start | bytes 589832 | tf_op jit(solution)/shard_map/ppermute | solution.py:48
  264.0 22.8 %collective-permute-start.65 = (bf16[144,1536]{1,0:T(8,128)(2,1)S(1)}, bf16[144,1536]{1,0:T(8,128)(2,1)S(1)}, u32[]{:S(2)}, u32[]{:S(2)}) collective-permute-start(bf16[144,1536]{1,0:T(8,128)(2,1)S(1)} %get-tuple-element.322.oa), channel_id=1, source_target_pairs={{0,96},{1,97},{2,98},{3,99},{4,100},{5,101},{6,102},{7,103},{8,104... | collective-permute-start | bytes 1327112 | tf_op jit(solution)/shard_map/ppermute | solution.py:48
  264.2 19.4 %collective-permute-start.66 = (bf16[128,1536]{1,0:T(8,128)(2,1)S(1)}, bf16[128,1536]{1,0:T(8,128)(2,1)S(1)}, u32[]{:S(2)}, u32[]{:S(2)}) collective-permute-start(bf16[128,1536]{1,0:T(8,128)(2,1)S(1)} %get-tuple-element.323.ob), channel_id=1, source_target_pairs={{0,4},{1,5},{2,6},{3,7},{4,0},{5,1},{6,2},{7,3},{8,12},{9,13},{10,... | collective-permute-start | bytes 1179656 | tf_op jit(solution)/shard_map/ppermute | solution.py:48
  287.4 12.2 %collective-permute-start.67 = (bf16[288,768]{1,0:T(8,128)(2,1)S(1)}, bf16[288,768]{1,0:T(8,128)(2,1)S(1)}, u32[]{:S(2)}, u32[]{:S(2)}) collective-permute-start(bf16[288,768]{1,0:T(8,128)(2,1)S(1)} %get-tuple-element.324.o0), channel_id=1, source_target_pairs={{0,4},{1,5},{2,6},{3,7},{4,0},{5,1},{6,2},{7,3},{8,12},{9,13},{10,... | collective-permute-start | bytes 1327112 | tf_op jit(solution)/shard_map/ppermute | solution.py:48
  287.5 8.4 %collective-permute-start.68 = (bf16[256,768]{1,0:T(8,128)(2,1)S(1)}, bf16[256,768]{1,0:T(8,128)(2,1)S(1)}, u32[]{:S(2)}, u32[]{:S(2)}) collective-permute-start(bf16[256,768]{1,0:T(8,128)(2,1)S(1)} %get-tuple-element.325.o1), channel_id=1, source_target_pairs={{0,32},{1,33},{2,34},{3,35},{4,36},{5,37},{6,38},{7,39},{8,40},{9,... | collective-permute-start | bytes 1179656 | tf_op jit(solution)/shard_map/ppermute | solution.py:48
  287.6 9.6 %collective-permute-start.69 = (bf16[256,768]{1,0:T(8,128)(2,1)S(1)}, bf16[256,768]{1,0:T(8,128)(2,1)S(1)}, u32[]{:S(2)}, u32[]{:S(2)}) collective-permute-start(bf16[256,768]{1,0:T(8,128)(2,1)S(1)} %get-tuple-element.326.o2), channel_id=1, source_target_pairs={{0,12},{1,13},{2,14},{3,15},{4,8},{5,9},{6,10},{7,11},{8,4},{9,5},... | collective-permute-start | bytes 1179656 | tf_op jit(solution)/shard_map/ppermute | solution.py:48
  290.3 9.3 %collective-permute-start.70 = (bf16[256,768]{1,0:T(8,128)(2,1)S(1)}, bf16[256,768]{1,0:T(8,128)(2,1)S(1)}, u32[]{:S(2)}, u32[]{:S(2)}) collective-permute-start(bf16[256,768]{1,0:T(8,128)(2,1)S(1)} %get-tuple-element.327.o3), channel_id=1, source_target_pairs={{0,96},{1,97},{2,98},{3,99},{4,100},{5,101},{6,102},{7,103},{8,104... | collective-permute-start | bytes 1179656 | tf_op jit(solution)/shard_map/ppermute | solution.py:48
  301.3 20.3 %collective-permute-start.71 = (bf16[544,768]{1,0:T(8,128)(2,1)S(1)}, bf16[544,768]{1,0:T(8,128)(2,1)S(1)}, u32[]{:S(2)}, u32[]{:S(2)}) collective-permute-start(bf16[544,768]{1,0:T(8,128)(2,1)S(1)} %get-tuple-element.328.p0.refs_0_), channel_id=1, source_target_pairs={{0,32},{1,33},{2,34},{3,35},{4,36},{5,37},{6,38},{7,39},{8,40},{9,... | collective-permute-start | bytes 2506760 | tf_op jit(solution)/shard_map/ppermute | solution.py:48
  301.8 17.2 %collective-permute-start.72 = (bf16[512,768]{1,0:T(8,128)(2,1)}, bf16[512,768]{1,0:T(8,128)(2,1)}, u32[]{:S(2)}, u32[]{:S(2)}) collective-permute-start(bf16[512,768]{1,0:T(8,128)(2,1)} %get-tuple-element.329.p1), channel_id=1, source_target_pairs={{0,4},{1,5},{2,6},{3,7},{4,0},{5,1},{6,2},{7,3},{8,12},{9,13},{10,... | collective-permute-start | bytes 2359304 | tf_op jit(solution)/shard_map/ppermute | solution.py:48
  303.1 17.2 %collective-permute-start.73 = (bf16[512,768]{1,0:T(8,128)(2,1)S(1)}, bf16[512,768]{1,0:T(8,128)(2,1)}, u32[]{:S(2)}, u32[]{:S(2)}) collective-permute-start(bf16[512,768]{1,0:T(8,128)(2,1)S(1)} %get-tuple-element.330.p2), channel_id=1, source_target_pairs={{0,96},{1,97},{2,98},{3,99},{4,100},{5,101},{6,102},{7,103},{8,104... | collective-permute-start | bytes 2359304 | tf_op jit(solution)/shard_map/ppermute | solution.py:48
  303.7 17.9 %collective-permute-start.74 = (bf16[512,768]{1,0:T(8,128)(2,1)S(1)}, bf16[512,768]{1,0:T(8,128)(2,1)}, u32[]{:S(2)}, u32[]{:S(2)}) collective-permute-start(bf16[512,768]{1,0:T(8,128)(2,1)S(1)} %get-tuple-element.331.p3), channel_id=1, source_target_pairs={{0,12},{1,13},{2,14},{3,15},{4,8},{5,9},{6,10},{7,11},{8,4},{9,5},... | collective-permute-start | bytes 2359304 | tf_op jit(solution)/shard_map/ppermute | solution.py:48
  (45 other events, 325.8 us)
Sparse Core Ops, SparseCore 0:
  219.7 70.6 all-gather.1
